TPU v7x, 512 devices: a whole 4x4x16 slice. The times are simulated.
512 devices in a mesh: section: 16 (over x, y_hi, core), tensor: 32 (over z, y_lo).
Axes of the slice: x: 4, y: 4 (y_hi: 2, y_lo: 2; y = y_hi * 2 + y_lo), z: 16, core: 2. Of those that a mesh axis runs over, the one named last changes fastest.
Arguments:
- hidden: bfloat16 [1024, 8192], P('section', 'tensor'), may hold values from -30 to 30
- audio: bfloat16 [512, 8192], P('section', 'tensor'), may hold values from -30 to 30
- audio_dest: int32 [512, 1], replicated, may hold values from 0 to 15; in each aligned block of 32 rows (0 to 31, 32 to 63, ...) at most 4 rows name the same one
- segment: int32 [32, 64], replicated, may hold values from 0 to 3, never falling along the last dimension, each value on 1 to 32 neighbouring positions
- norm_gain: bfloat16 [16, 8192], P('section', 'tensor'), may hold values from 0.25 to 1.75
- w_query: bfloat16 [16, 8192, 4096], P('section', None, 'tensor'), may hold values from -1 to 1
- w_keyval: bfloat16 [16, 8192, 1024], P('section', 'tensor'), may hold values from -1 to 1
- w_out: bfloat16 [16, 4096, 8192], P('section', None, 'tensor'), may hold values from -0.09375 to 0.09375
Outputs:
- lap_state: bfloat16 [2048, 8192], P('section', 'tensor')
Inputs may be any that keep to these rules, and one draw needn't show every extreme that they name: `audio_dest`: in each aligned block of 32 rows (the audio rows of one stop) no stop is named more than 4 times, a bound that some block reaches.
All inputs are finite; a program needn't handle non-finite values.
Results may differ from a plain program's by a relative error of at most 0.018.
Values may be sent and summed in bfloat16 or wider, within the bound.
No kernel may reach another device: no remote copies, remote signals or barrier semaphores. Data moves between devices by JAX's collectives and lax.ppermute only.
A program may use at most 64 MiB of HBM per device.

v0:
```python
import math

import jax
import jax.numpy as jnp
from jax import lax
from jax.sharding import PartitionSpec as P

D = 8192
HD = 128
KVH = 4
MB_DEV = 2
AUD_MB = 32
TXT_MB = 32
AUD_DEV = 32
STEPS = 4
MB_ROWS = 64


def from_behind(block, axis, distance):
    devices = range(lax.axis_size(axis))
    route = [((i - distance) % len(devices), i) for i in devices]
    return lax.ppermute(block, axis, route)


def rotate(values, cosine, sine):
    half = values.shape[-1] // 2
    first = values[..., :half]
    second = values[..., half:]
    return jnp.concatenate([first * cosine - second * sine, second * cosine + first * sine], -1)


def rope_tables(rows, width):
    position = jnp.arange(rows, dtype=jnp.float32)
    freq = 500000.0 ** (-(2.0 * jnp.arange(width // 2, dtype=jnp.float32)) / width)
    angle = position[:, None] * freq[None, :]
    return (jnp.cos(angle), jnp.sin(angle))


def local(hidden, audio, audio_dest, segment, norm_gain, w_query, w_keyval, w_out):
    stop_count = lax.axis_size("section")
    width_share = hidden.shape[1]
    section_index = lax.axis_index("section")
    part_index = lax.axis_index("tensor")
    capacity = MB_DEV * AUD_MB // stop_count
    heads = w_out.shape[1] // HD
    group_index = part_index // (heads // KVH)
    slot_count = MB_DEV * AUD_MB
    row_total = MB_DEV * MB_ROWS
    targets = audio_dest[:, 0].reshape(stop_count, AUD_DEV)
    order = jnp.arange(AUD_DEV, dtype=jnp.int32)
    earlier = order[None, :] < order[:, None]
    row_rank = jnp.sum(
        ((targets[:, :, None] == targets[:, None, :]) & earlier[None]).astype(jnp.int32), axis=2
    )
    sources = jnp.arange(stop_count, dtype=jnp.int32)[:, None]
    slot_index = sources * capacity + row_rank
    slot_ids = jnp.arange(slot_count, dtype=jnp.int32)
    every_row = lax.all_gather(audio, "section", axis=0, tiled=True)
    chosen = (slot_ids[:, None] == slot_index.reshape(-1)[None, :]) & (
        targets.reshape(-1) == section_index
    )[None, :]
    audio_slots = jnp.dot(
        chosen.astype(jnp.bfloat16), every_row, preferred_element_type=jnp.float32
    ).astype(jnp.bfloat16)
    state = jnp.concatenate(
        [
            audio_slots.reshape(MB_DEV, AUD_MB, width_share),
            hidden.reshape(MB_DEV, TXT_MB, width_share),
        ],
        1,
    )
    state = state.reshape(row_total, width_share)
    owner = slot_ids // capacity
    stop_ids = jnp.arange(stop_count, dtype=jnp.int32)
    gain_local = norm_gain[0].astype(jnp.float32)
    cosine, sine = rope_tables(MB_ROWS, HD)
    row_ids = jnp.arange(MB_ROWS, dtype=jnp.int32)
    causal = row_ids[None, :] <= row_ids[:, None]
    diagonal = row_ids[None, :] == row_ids[:, None]
    w_q = w_query[0]
    w_kv = w_keyval[0]
    w_o = w_out[0]
    scale = 1.0 / math.sqrt(HD)
    for lap_step in range(STEPS):
        root = (section_index - lap_step) % stop_count
        segment_now = lax.dynamic_slice_in_dim(segment, root * MB_DEV, MB_DEV, 0)
        counts = jnp.sum((targets == root).astype(jnp.int32), axis=1)
        per_slot = jnp.sum(
            jnp.where(owner[:, None] == stop_ids[None, :], counts[None, :], 0), axis=1
        )
        audio_live = (slot_ids % capacity < per_slot).reshape(MB_DEV, AUD_MB)
        allowed = (
            causal[None]
            & (segment_now[:, :, None] == segment_now[:, None, :])
            & (
                jnp.concatenate([audio_live, jnp.ones((MB_DEV, TXT_MB), jnp.bool_)], 1)[:, None, :]
                | diagonal[None]
            )
        )
        state_wide = state.astype(jnp.float32)
        squares = lax.psum(jnp.sum(state_wide * state_wide, axis=1), "tensor")
        inverse = lax.rsqrt(squares / D + 1e-05)[:, None]
        normed_local = (state_wide * inverse * gain_local[None, :]).astype(jnp.bfloat16)
        normed = lax.all_gather(normed_local, "tensor", axis=1, tiled=True)
        partial_kv = jnp.dot(normed_local, w_kv, preferred_element_type=jnp.float32)
        key_values = lax.psum(partial_kv, "tensor")
        own_block = lax.dynamic_slice_in_dim(key_values, group_index * 2 * HD, 2 * HD, 1)
        key_rows = rotate(own_block[:, :HD].reshape(MB_DEV, MB_ROWS, HD), cosine, sine).astype(
            jnp.bfloat16
        )
        value_rows = own_block[:, HD:].reshape(MB_DEV, MB_ROWS, HD).astype(jnp.bfloat16)
        queries = jnp.dot(normed, w_q, preferred_element_type=jnp.float32).reshape(
            MB_DEV, MB_ROWS, HD
        )
        queries = rotate(queries, cosine, sine).astype(jnp.bfloat16)
        scores = (
            jnp.einsum("mid,mjd->mij", queries, key_rows, preferred_element_type=jnp.float32)
            * scale
        )
        scores = jnp.where(allowed, scores, -jnp.inf)
        highest = jnp.max(scores, axis=-1, keepdims=True)
        weights = jnp.exp(scores - highest)
        probs = (weights / jnp.sum(weights, axis=-1, keepdims=True)).astype(jnp.bfloat16)
        attended = jnp.einsum("mij,mjd->mid", probs, value_rows, preferred_element_type=jnp.float32)
        attended = attended.astype(jnp.bfloat16).reshape(row_total, HD)
        projected = jnp.dot(
            lax.all_gather(attended, "tensor", axis=1, tiled=True),
            w_o,
            preferred_element_type=jnp.float32,
        )
        state = (state_wide + projected).astype(jnp.bfloat16)
        state = from_behind(state, "section", 1)
    return state


def solution(mesh):
    in_specs = (
        P("section", "tensor"),
        P("section", "tensor"),
        P(),
        P(),
        P("section", "tensor"),
        P("section", None, "tensor"),
        P("section", "tensor", None),
        P("section", None, "tensor"),
    )
    out_specs = P("section", "tensor")
    return jax.shard_map(local, mesh=mesh, in_specs=in_specs, out_specs=out_specs, check_vma=False)
```

profile of v0, /device:TPU:1, one launch (start us, length us, event | category | flops | bytes accessed | tf_op | source)
XLA Modules:
  0.0 2429.1 jit_solution(7635241776445869516)
XLA Ops:
  10.6 26.7 %all_gather.27 = bf16[512,256]{1,0:T(8,128)(2,1)S(1)} all-gather(bf16[32,256]{1,0:T(8,128)(2,1)} %param.9), channel_id=1, replica_groups=mesh['section'=16,'tensor'=32] {'section'}, dimensions={0}, use_global_device_ids=true | all-gather | bytes 278528 | tf_op jit(solution)/shard_map/all_gather | solution.py:58
  38.4 55.4 %psum.56 = f32[128]{0:T(128)S(1)} all-reduce(f32[128]{0:T(128)S(1)} %reduce_sum.168), channel_id=1, replica_groups=mesh['section'=16,'tensor'=32] {'tensor'}, use_global_device_ids=true, to_apply=%region_4.5 | all-reduce | flops 128 | bytes 1024 | tf_op jit(solution)/shard_map/psum | solution.py:101
  99.2 244.2 %all-reduce.9.cloned.1.call-done = f32[128,1024]{1,0:T(8,128)} async-done(((f32[128,1024]{1,0:T(8,128)}), f32[128,1024]{1,0:T(8,128)}) %all-reduce.9.cloned.1.call-update) | async-done | bytes 524304 | tf_op jit(solution)/shard_map/psum | solution.py:106
  345.2 133.5 %all-gather.9.cloned.1.call-done = bf16[128,8192]{1,0:T(8,128)(2,1)} async-done(((bf16[128,256]{1,0:T(8,128)(2,1)}), bf16[128,8192]{1,0:T(8,128)(2,1)}) %all-gather.9.cloned.1.call-update) | async-done | bytes 2097168 | tf_op jit(solution)/shard_map/all_gather | solution.py:104
  483.1 121.9 %all-gather.11.cloned.1.call-done = bf16[128,4096]{1,0:T(8,128)(2,1)} async-done(((bf16[128,128]{1,0:T(8,128)(2,1)}), bf16[128,4096]{1,0:T(8,128)(2,1)}) %all-gather.11.cloned.1.call-update) | async-done | bytes 1048592 | tf_op jit(solution)/shard_map/all_gather | solution.py:127
  606.7 29.1 %collective-permute-start = (bf16[128,256]{1,0:T(8,128)(2,1)S(1)}, bf16[128,256]{1,0:T(8,128)(2,1)S(1)}, u32[]{:S(2)}, u32[]{:S(2)}) collective-permute-start(bf16[128,256]{1,0:T(8,128)(2,1)S(1)} %fusion.41), channel_id=1, source_target_pairs={{480,0},{0,32},{32,64},{64,96},{96,128},{128,160},{160,192},{192,2... | collective-permute-start | bytes 196616 | tf_op jit(solution)/shard_map/ppermute | solution.py:22
  637.2 47.3 %psum.58 = f32[128]{0:T(128)S(1)} all-reduce(f32[128]{0:T(128)S(1)} %fusion.64), channel_id=1, replica_groups=mesh['section'=16,'tensor'=32] {'tensor'}, use_global_device_ids=true, to_apply=%region_11.12 | all-reduce | flops 128 | bytes 1024 | tf_op jit(solution)/shard_map/psum | solution.py:101
  686.4 252.1 %all-reduce.11.cloned.1.call-done = f32[128,1024]{1,0:T(8,128)} async-done(((f32[128,1024]{1,0:T(8,128)}), f32[128,1024]{1,0:T(8,128)}) %all-reduce.11.cloned.1.call-update) | async-done | bytes 524304 | tf_op jit(solution)/shard_map/psum | solution.py:106
  940.2 133.2 %all-gather.13.cloned.1.call-done = bf16[128,8192]{1,0:T(8,128)(2,1)} async-done(((bf16[128,256]{1,0:T(8,128)(2,1)}), bf16[128,8192]{1,0:T(8,128)(2,1)}) %all-gather.13.cloned.1.call-update) | async-done | bytes 2097168 | tf_op jit(solution)/shard_map/all_gather | solution.py:104
  1073.4 2.9 fusion.16
  1077.8 121.9 %all-gather.15.cloned.1.call-done = bf16[128,4096]{1,0:T(8,128)(2,1)} async-done(((bf16[128,128]{1,0:T(8,128)(2,1)}), bf16[128,4096]{1,0:T(8,128)(2,1)}) %all-gather.15.cloned.1.call-update) | async-done | bytes 1048592 | tf_op jit(solution)/shard_map/all_gather | solution.py:127
  1201.4 29.1 %collective-permute-start.1 = (bf16[128,256]{1,0:T(8,128)(2,1)S(1)}, bf16[128,256]{1,0:T(8,128)(2,1)S(1)}, u32[]{:S(2)}, u32[]{:S(2)}) collective-permute-start(bf16[128,256]{1,0:T(8,128)(2,1)S(1)} %fusion.38), channel_id=1, source_target_pairs={{480,0},{0,32},{32,64},{64,96},{96,128},{128,160},{160,192},{192,2... | collective-permute-start | bytes 196616 | tf_op jit(solution)/shard_map/ppermute | solution.py:22
  1231.9 47.3 %psum.60 = f32[128]{0:T(128)S(1)} all-reduce(f32[128]{0:T(128)S(1)} %fusion.67), channel_id=1, replica_groups=mesh['section'=16,'tensor'=32] {'tensor'}, use_global_device_ids=true, to_apply=%region_18.19 | all-reduce | flops 128 | bytes 1024 | tf_op jit(solution)/shard_map/psum | solution.py:101
  1281.4 251.7 %all-reduce.13.cloned.1.call-done = f32[128,1024]{1,0:T(8,128)} async-done(((f32[128,1024]{1,0:T(8,128)}), f32[128,1024]{1,0:T(8,128)}) %all-reduce.13.cloned.1.call-update) | async-done | bytes 524304 | tf_op jit(solution)/shard_map/psum | solution.py:106
  1534.8 133.5 %all-gather.17.cloned.1.call-done = bf16[128,8192]{1,0:T(8,128)(2,1)} async-done(((bf16[128,256]{1,0:T(8,128)(2,1)}), bf16[128,8192]{1,0:T(8,128)(2,1)}) %all-gather.17.cloned.1.call-update) | async-done | bytes 2097168 | tf_op jit(solution)/shard_map/all_gather | solution.py:104
  1668.3 2.9 fusion.14
  1672.8 121.9 %all-gather.19.cloned.1.call-done = bf16[128,4096]{1,0:T(8,128)(2,1)} async-done(((bf16[128,128]{1,0:T(8,128)(2,1)}), bf16[128,4096]{1,0:T(8,128)(2,1)}) %all-gather.19.cloned.1.call-update) | async-done | bytes 1048592 | tf_op jit(solution)/shard_map/all_gather | solution.py:127
  1796.3 29.1 %collective-permute-start.2 = (bf16[128,256]{1,0:T(8,128)(2,1)S(1)}, bf16[128,256]{1,0:T(8,128)(2,1)S(1)}, u32[]{:S(2)}, u32[]{:S(2)}) collective-permute-start(bf16[128,256]{1,0:T(8,128)(2,1)S(1)} %fusion.35), channel_id=1, source_target_pairs={{480,0},{0,32},{32,64},{64,96},{96,128},{128,160},{160,192},{192,2... | collective-permute-start | bytes 196616 | tf_op jit(solution)/shard_map/ppermute | solution.py:22
  1826.9 47.3 %psum.62 = f32[128]{0:T(128)S(1)} all-reduce(f32[128]{0:T(128)S(1)} %fusion.70), channel_id=1, replica_groups=mesh['section'=16,'tensor'=32] {'tensor'}, use_global_device_ids=true, to_apply=%region_25.26 | all-reduce | flops 128 | bytes 1024 | tf_op jit(solution)/shard_map/psum | solution.py:101
  1876.2 252.0 %all-reduce.15.cloned.1.call-done = f32[128,1024]{1,0:T(8,128)} async-done(((f32[128,1024]{1,0:T(8,128)}), f32[128,1024]{1,0:T(8,128)}) %all-reduce.15.cloned.1.call-update) | async-done | bytes 524304 | tf_op jit(solution)/shard_map/psum | solution.py:106
  2129.8 133.3 %all-gather.21.cloned.1.call-done = bf16[128,8192]{1,0:T(8,128)(2,1)} async-done(((bf16[128,256]{1,0:T(8,128)(2,1)}), bf16[128,8192]{1,0:T(8,128)(2,1)}) %all-gather.21.cloned.1.call-update) | async-done | bytes 2097168 | tf_op jit(solution)/shard_map/all_gather | solution.py:104
  2263.1 2.9 fusion.12
  2267.5 122.0 %all-gather.23.cloned.1.call-done = bf16[128,4096]{1,0:T(8,128)(2,1)} async-done(((bf16[128,128]{1,0:T(8,128)(2,1)}), bf16[128,4096]{1,0:T(8,128)(2,1)}) %all-gather.23.cloned.1.call-update) | async-done | bytes 1048592 | tf_op jit(solution)/shard_map/all_gather | solution.py:127
  2391.2 29.1 %collective-permute-start.3 = (bf16[128,256]{1,0:T(8,128)(2,1)S(1)}, bf16[128,256]{1,0:T(8,128)(2,1)S(1)}, u32[]{:S(2)}, u32[]{:S(2)}) collective-permute-start(bf16[128,256]{1,0:T(8,128)(2,1)S(1)} %fusion.32), channel_id=1, source_target_pairs={{480,0},{0,32},{32,64},{64,96},{96,128},{128,160},{160,192},{192,2... | collective-permute-start | bytes 196616 | tf_op jit(solution)/shard_map/ppermute | solution.py:22
  (118 shorter events, 44.7 us)
Async XLA Ops:
  6.5 598.5 %copy-start = (bf16[1,4096,256]{2,1,0:T(8,128)(2,1)S(1)}, bf16[1,4096,256]{2,1,0:T(8,128)(2,1)}, u32[]{:S(2)}) copy-start(bf16[1,4096,256]{2,1,0:T(8,128)(2,1)} %param.15) | copy-start | bytes 6291460
  6.5 90.4 %copy-start.5 = (bf16[64,256]{1,0:T(8,128)(2,1)S(1)}, bf16[64,256]{1,0:T(8,128)(2,1)}, u32[]{:S(2)}) copy-start(bf16[64,256]{1,0:T(8,128)(2,1)} %param.8) | copy-start | bytes 98308
  6.5 336.9 %all-reduce.9.cloned.1.call-start = ((), (), s32[]{:S(2)}) async-start(), calls=%async_computation.1 | async-start | bytes 1048576 | tf_op jit(solution)/shard_map/psum | solution.py:106
  96.9 381.8 %all-gather.9.cloned.1.call-start = ((), (), s32[]{:S(2)}) async-start(), calls=%async_computation | async-start | bytes 2162688 | tf_op jit(solution)/shard_map/all_gather | solution.py:104
  97.7 507.4 %all-gather.11.cloned.1.call-start = ((), (), s32[]{:S(2)}) async-start(), calls=%async_computation.2 | async-start | bytes 1081344 | tf_op jit(solution)/shard_map/all_gather | solution.py:127
  482.2 202.5 %copy-start.1 = (bf16[1,256,1024]{2,1,0:T(8,128)(2,1)S(1)}, bf16[1,256,1024]{2,1,0:T(8,128)(2,1)}, u32[]{:S(2)}) copy-start(bf16[1,256,1024]{2,1,0:T(8,128)(2,1)} %param.14) | copy-start | bytes 1572868
  483.1 455.4 %all-reduce.11.cloned.1.call-start = ((), (), s32[]{:S(2)}) async-start(), calls=%async_computation.4 | async-start | bytes 1048576 | tf_op jit(solution)/shard_map/psum | solution.py:106
  606.7 30.4 %collective-permute-start = (bf16[128,256]{1,0:T(8,128)(2,1)S(1)}, bf16[128,256]{1,0:T(8,128)(2,1)S(1)}, u32[]{:S(2)}, u32[]{:S(2)}) collective-permute-start(bf16[128,256]{1,0:T(8,128)(2,1)S(1)} %fusion.41), channel_id=1, source_target_pairs={{480,0},{0,32},{32,64},{64,96},{96,128},{128,160},{160,192},{192,2... | collective-permute-start | bytes 196616 | tf_op jit(solution)/shard_map/ppermute | solution.py:22
  684.6 1.1 copy-start.4
  685.7 387.6 %all-gather.13.cloned.1.call-start = ((), (), s32[]{:S(2)}) async-start(), calls=%async_computation.3 | async-start | bytes 2162688 | tf_op jit(solution)/shard_map/all_gather | solution.py:104
  686.3 513.4 %all-gather.15.cloned.1.call-start = ((), (), s32[]{:S(2)}) async-start(), calls=%async_computation.5 | async-start | bytes 1081344 | tf_op jit(solution)/shard_map/all_gather | solution.py:127
  1077.7 455.4 %all-reduce.13.cloned.1.call-start = ((), (), s32[]{:S(2)}) async-start(), calls=%async_computation.7 | async-start | bytes 1048576 | tf_op jit(solution)/shard_map/psum | solution.py:106
  1201.4 30.4 %collective-permute-start.1 = (bf16[128,256]{1,0:T(8,128)(2,1)S(1)}, bf16[128,256]{1,0:T(8,128)(2,1)S(1)}, u32[]{:S(2)}, u32[]{:S(2)}) collective-permute-start(bf16[128,256]{1,0:T(8,128)(2,1)S(1)} %fusion.38), channel_id=1, source_target_pairs={{480,0},{0,32},{32,64},{64,96},{96,128},{128,160},{160,192},{192,2... | collective-permute-start | bytes 196616 | tf_op jit(solution)/shard_map/ppermute | solution.py:22
  1279.3 1.1 copy-start.2
  1280.4 387.9 %all-gather.17.cloned.1.call-start = ((), (), s32[]{:S(2)}) async-start(), calls=%async_computation.6 | async-start | bytes 2162688 | tf_op jit(solution)/shard_map/all_gather | solution.py:104
  1281.1 513.5 %all-gather.19.cloned.1.call-start = ((), (), s32[]{:S(2)}) async-start(), calls=%async_computation.8 | async-start | bytes 1081344 | tf_op jit(solution)/shard_map/all_gather | solution.py:127
  1672.7 455.4 %all-reduce.15.cloned.1.call-start = ((), (), s32[]{:S(2)}) async-start(), calls=%async_computation.10 | async-start | bytes 1048576 | tf_op jit(solution)/shard_map/psum | solution.py:106
  1796.3 30.4 %collective-permute-start.2 = (bf16[128,256]{1,0:T(8,128)(2,1)S(1)}, bf16[128,256]{1,0:T(8,128)(2,1)S(1)}, u32[]{:S(2)}, u32[]{:S(2)}) collective-permute-start(bf16[128,256]{1,0:T(8,128)(2,1)S(1)} %fusion.35), channel_id=1, source_target_pairs={{480,0},{0,32},{32,64},{64,96},{96,128},{128,160},{160,192},{192,2... | collective-permute-start | bytes 196616 | tf_op jit(solution)/shard_map/ppermute | solution.py:22
  1874.3 1.1 copy-start.3
  1875.4 387.8 %all-gather.21.cloned.1.call-start = ((), (), s32[]{:S(2)}) async-start(), calls=%async_computation.9 | async-start | bytes 2162688 | tf_op jit(solution)/shard_map/all_gather | solution.py:104
  1876.1 513.4 %all-gather.23.cloned.1.call-start = ((), (), s32[]{:S(2)}) async-start(), calls=%async_computation.11 | async-start | bytes 1081344 | tf_op jit(solution)/shard_map/all_gather | solution.py:127
  2391.2 30.4 %collective-permute-start.3 = (bf16[128,256]{1,0:T(8,128)(2,1)S(1)}, bf16[128,256]{1,0:T(8,128)(2,1)S(1)}, u32[]{:S(2)}, u32[]{:S(2)}) collective-permute-start(bf16[128,256]{1,0:T(8,128)(2,1)S(1)} %fusion.32), channel_id=1, source_target_pairs={{480,0},{0,32},{32,64},{64,96},{96,128},{128,160},{160,192},{192,2... | collective-permute-start | bytes 196616 | tf_op jit(solution)/shard_map/ppermute | solution.py:22
Sparse Core Ops, SparseCore 0:
  97.0 246.4 all-reduce.8
  345.7 132.9 all-gather.8
  483.2 121.8 all-gather.10
  685.9 252.6 all-reduce.10
  940.4 132.9 all-gather.12
  1077.9 121.7 all-gather.14
  1280.5 252.5 all-reduce.12
  1535.3 132.9 all-gather.16
  1672.8 121.7 all-gather.18
  1875.5 252.6 all-reduce.14
  2130.1 132.9 all-gather.20
  2267.6 121.7 all-gather.22
where the time goes:
time: 2430 us
  waiting for transfers between devices  2030 us (84%)
  blocking collectives  224 us (9%)
  starting transfers between devices  117 us (5%)
  matrix products  29 us (1%)
    psum x4, waiting for transfers between devices, local(): key_values = lax.psum(partial_kv, 'tensor')  1000 us
    all_gather x4, waiting for transfers between devices, local(): normed = lax.all_gather(normed_local, 'tensor', axis=1, tiled=True)  534 us
    all_gather x4, waiting for transfers between devices, local(): lax.all_gather(attended, 'tensor', axis=1, tiled=True)  488 us
    psum x4, blocking collectives, local(): squares = lax.psum(jnp.sum(state_wide * state_wide, axis=1), 'tensor')  197 us
    ppermute x4, starting transfers between devices, from_behind(): return lax.ppermute(block, axis, route)  116 us
  transfers between devices with their start and end apart: 16, of which 16 were waited for; matrix products, arithmetic and copies ran while one was open for 0% of the time, Pallas kernels for 0%

commit v1 on v0

v1 whole, which is shorter than its diff:
```python
import math

import jax
import jax.numpy as jnp
from jax import lax
from jax.sharding import Mesh
from jax.sharding import PartitionSpec as P

D = 8192
HD = 128
KVH = 4
MB_DEV = 2
AUD_MB = 32
TXT_MB = 32
AUD_DEV = 32
STEPS = 4
MB_ROWS = 64
CAP = 4
COLS = 256
GROUP = 4
F32 = jnp.float32
BF16 = jnp.bfloat16


def shift(block, axis, distance):
    count = lax.axis_size(axis)
    return lax.ppermute(block, axis, [(i, (i + distance) % count) for i in range(count)])


def rotate(values, cosine, sine):
    half = values.shape[-1] // 2
    first = values[..., :half]
    second = values[..., half:]
    return jnp.concatenate([first * cosine - second * sine, second * cosine + first * sine], -1)


def rope_tables(rows, width):
    position = jnp.arange(rows, dtype=F32)
    freq = 500000.0 ** (-(2.0 * jnp.arange(width // 2, dtype=F32)) / width)
    angle = position[:, None] * freq[None, :]
    return (jnp.cos(angle), jnp.sin(angle))


def pick(stack, index, axis):
    return lax.dynamic_index_in_dim(stack, index, axis, keepdims=False)


def in_order(own, other, y, axis):
    first = jnp.where(y == 0, own, other)
    second = jnp.where(y == 0, other, own)
    return jnp.concatenate([first, second], axis)


def local(hidden, audio, audio_dest, segment, norm_gain, w_query, w_keyval, w_out):
    stops = lax.axis_size("section")
    s = lax.axis_index("section")
    a = lax.axis_index("za")
    b = lax.axis_index("zb")
    y = lax.axis_index("y")

    w_q = w_query[0].reshape(GROUP, GROUP, 2 * COLS, HD)
    query_parts = []
    for j in range(GROUP):
        piece = pick(w_q, (b - j) % GROUP, 1)
        if j:
            piece = shift(piece, "zb", -j)
        piece = piece.reshape(GROUP * 2 * COLS, HD)
        query_parts.append(jnp.concatenate([piece, shift(piece, "y", 1)], 1))

    w_kv = w_keyval[0].reshape(COLS, GROUP, 2 * HD)
    kv_pieces = []
    for k in range(GROUP):
        piece = pick(w_kv, (a + k) % GROUP, 1)
        if k:
            piece = shift(piece, "za", k)
        kv_pieces.append(piece)
    kv_stack = jnp.stack(kv_pieces)
    kv_own = jnp.stack([pick(kv_stack, (a - source) % GROUP, 0) for source in range(GROUP)])
    kv_other = shift(kv_own, "y", 1)
    w_kv_rows = in_order(kv_own, kv_other, y, 1).reshape(GROUP * 2 * COLS, 2 * HD)

    w_o = w_out[0]
    w_o_pair = jnp.concatenate([w_o, shift(w_o, "y", 1)], 1)

    targets = audio_dest[:, 0].reshape(stops, AUD_DEV)
    order = jnp.arange(AUD_DEV, dtype=jnp.int32)
    own_targets = pick(targets, s, 0)
    rank = jnp.sum(
        ((own_targets[:, None] == own_targets[None, :]) & (order[None, :] < order[:, None])).astype(jnp.int32),
        axis=1,
    )
    seats = jnp.arange(stops * CAP, dtype=jnp.int32)
    chosen = seats[:, None] == (own_targets * CAP + rank)[None, :]
    outgoing = jnp.dot(chosen.astype(BF16), audio, preferred_element_type=F32).astype(BF16)
    slots = lax.all_to_all(outgoing.reshape(stops, CAP, COLS), "section", 0, 0, tiled=True)
    slots = slots.reshape(MB_DEV, AUD_MB, COLS)
    text = hidden.reshape(MB_DEV, TXT_MB, COLS)
    gain_rows = jnp.broadcast_to(norm_gain, (16, COLS))

    def batch(index):
        return jnp.concatenate([pick(slots, index, 0), pick(text, index, 0), gain_rows], 0)

    both = in_order(batch(y), shift(batch(1 - y), "y", 1), y, 1)
    state = both[:MB_ROWS]
    gain = None

    seat_ids = jnp.arange(AUD_MB, dtype=jnp.int32)
    owner = y * (AUD_MB // CAP) + seat_ids // CAP
    row_ids = jnp.arange(MB_ROWS, dtype=jnp.int32)
    causal = row_ids[None, :] <= row_ids[:, None]
    diagonal = row_ids[None, :] == row_ids[:, None]
    allowed = []
    for lap_step in range(STEPS):
        root = (s - lap_step) % stops
        clip = pick(segment, root * MB_DEV + y, 0)
        counts = jnp.sum((targets == root).astype(jnp.int32), axis=1)
        held = jnp.sum(
            jnp.where(owner[:, None] == jnp.arange(stops, dtype=jnp.int32)[None, :], counts[None, :], 0), axis=1
        )
        live = jnp.concatenate([seat_ids % CAP < held, jnp.ones((TXT_MB,), jnp.bool_)], 0)
        allowed.append(causal & (clip[:, None] == clip[None, :]) & (live[None, :] | diagonal))
    cosine, sine = rope_tables(MB_ROWS, HD)
    scale = 1.0 / math.sqrt(HD)
    lane = jnp.arange(HD, dtype=jnp.int32)[None, :]

    for lap_step in range(STEPS):
        if lap_step == 0:
            wide = lax.all_gather(both, "za", axis=1, tiled=True)
            gain = wide[MB_ROWS : MB_ROWS + 1].astype(F32)
            wide = wide[:MB_ROWS]
        else:
            wide = lax.all_gather(state, "za", axis=1, tiled=True)
        wide = wide.astype(F32)
        squares = jnp.sum(wide * wide, axis=1, keepdims=True)
        scaled = (wide * gain).astype(BF16)
        queries = [jnp.dot(scaled, part, preferred_element_type=F32).astype(BF16) for part in query_parts]
        key_values = jnp.dot(scaled, w_kv_rows, preferred_element_type=F32).astype(BF16)
        coarse = squares.astype(BF16)
        middle = (squares - coarse.astype(F32)).astype(BF16)
        fine = (squares - coarse.astype(F32) - middle.astype(F32)).astype(BF16)
        square_lanes = jnp.where(
            lane == 0, coarse, jnp.where(lane == 1, middle, jnp.where(lane == 2, fine, jnp.zeros((), BF16)))
        )
        by_receiver = lax.dynamic_slice_in_dim(jnp.stack(queries + queries), (GROUP - b) % GROUP, GROUP, 0)
        shared = jnp.concatenate([key_values, square_lanes], 1)
        message = jnp.concatenate([by_receiver, jnp.broadcast_to(shared[None], (GROUP,) + shared.shape)], 2)
        arrived = lax.all_to_all(message, "zb", 0, 0, tiled=True)
        total = jnp.sum(arrived.astype(F32), axis=0)
        inverse = lax.rsqrt(jnp.sum(total[:, 4 * HD :], axis=1, keepdims=True) / D + 1e-05)
        total = total[:, : 4 * HD] * inverse
        key_rows = rotate(total[:, 2 * HD : 3 * HD], cosine, sine).astype(BF16)
        value_rows = total[:, 3 * HD :].astype(BF16)
        heads = []
        for head in range(2):
            query_rows = rotate(total[:, head * HD : (head + 1) * HD], cosine, sine).astype(BF16)
            scores = jnp.dot(query_rows, key_rows.T, preferred_element_type=F32) * scale
            scores = jnp.where(allowed[lap_step], scores, -jnp.inf)
            weights = jnp.exp(scores - jnp.max(scores, axis=-1, keepdims=True))
            probs = (weights / jnp.sum(weights, axis=-1, keepdims=True)).astype(BF16)
            heads.append(jnp.dot(probs, value_rows, preferred_element_type=F32).astype(BF16))
        attended = lax.all_gather(in_order(heads[0], heads[1], y, 1), ("za", "zb"), axis=1, tiled=True)
        projected = jnp.dot(attended, w_o_pair, preferred_element_type=F32)
        state_wide = state.astype(F32)
        if lap_step < STEPS - 1:
            update = in_order(projected[:, :COLS], projected[:, COLS:], y, 1)
            state = shift((state_wide + update).astype(BF16), "section", 1)
    low, high = state_wide[:, :COLS], state_wide[:, COLS:]
    own = (jnp.where(y == 0, low, high) + projected[:, :COLS]).astype(BF16)
    other = (jnp.where(y == 0, high, low) + projected[:, COLS:]).astype(BF16)
    crossing = [(2 * i + j, 2 * ((i + 1) % stops) + 1 - j) for i in range(stops) for j in range(2)]
    own = shift(own, "section", 1)
    other = lax.ppermute(other, ("section", "y"), crossing)
    return in_order(own, other, y, 0)


def solution(mesh):
    sections = mesh.shape["section"]
    parts = mesh.shape["tensor"]
    names = ("section", "za", "zb", "y")
    fine = Mesh(mesh.devices.reshape(sections, parts // (2 * GROUP), GROUP, 2), names)
    tensor = names[1:]
    in_specs = (
        P("section", tensor),
        P("section", tensor),
        P(),
        P(),
        P("section", tensor),
        P("section", None, tensor),
        P("section", tensor, None),
        P("section", None, tensor),
    )
    return jax.shard_map(local, mesh=fine, in_specs=in_specs, out_specs=P("section", tensor), check_vma=False)
```

time: 2430 us -> 451 us (0.19)
  waiting for transfers between devices: 2030 us -> 91.8 us
  blocking collectives: 224 us -> 176 us
    all_gather x8 -> x0, waiting for transfers between devices: 1020 us -> none  [the longest x4 534 us: local(): normed = lax.all_gather(normed_local, 'tensor', axis=1, tiled=True)]
    psum x4 -> x0, waiting for transfers between devices: 1000 us -> none  [local(): key_values = lax.psum(partial_kv, 'tensor')]
    psum x4 -> x0, blocking collectives: 197 us -> none  [local(): squares = lax.psum(jnp.sum(state_wide * state_wide, axis=1), 'tensor')]
    all_gather x1 -> x8, blocking collectives: 26.7 us -> 176 us  [the longest x4 95.8 us: local(): lax.all_gather(in_order(heads[0], heads[1], y, 1), ('za', 'zb'), axis=1,...]
    ppermute x4 -> x18, waiting for transfers between devices: 5.24 us -> 68.3 us  [the longest x17 64 us: shift(): lax.ppermute(block, axis, [(i, (i + distance) % count) for i in range(cou...]
    all_to_all x0 -> x5, starting transfers between devices: none -> 24.7 us  [the longest x4 16.7 us: local(): arrived = lax.all_to_all(message, 'zb', 0, 0, tiled=True)]
    ppermute x4 -> x18, starting transfers between devices: 116 us -> 113 us  [the longest x17 110 us: shift(): lax.ppermute(block, axis, [(i, (i + distance) % count) for i in range(cou...]
  transfers between devices with their start and end apart: 16 -> 23, of which waited for: 16 -> 13; matrix products, arithmetic and copies ran while one was open for 0% -> 2% of each run, Pallas kernels for 0% -> 0%
where the time goes in v1:
time: 451 us; the launch traced here: 449 us
  blocking collectives  176 us (39%)
  starting transfers between devices  138 us (31%)
  waiting for transfers between devices  91.8 us (20%)
  matrix products  28.6 us (6%)
  other arithmetic  8.35 us (2%)
  local copies, waits for them, and re-layouts  5.25 us (1%)
    ppermute x17, starting transfers between devices, shift(): lax.ppermute(block, axis, [(i, (i + distance) % count) for i in range(cou...  110 us
    all_gather x4, blocking collectives, local(): lax.all_gather(in_order(heads[0], heads[1], y, 1), ('za', 'zb'), axis=1,...  95.8 us
    ppermute x17, waiting for transfers between devices, shift(): lax.ppermute(block, axis, [(i, (i + distance) % count) for i in range(cou...  64 us
    all_gather x3, blocking collectives, local(): wide = lax.all_gather(state, 'za', axis=1, tiled=True)  49.2 us
    all_gather x1, blocking collectives, local(): wide = lax.all_gather(both, 'za', axis=1, tiled=True)  30.6 us
    all_to_all x4, waiting for transfers between devices, local(): arrived = lax.all_to_all(message, 'zb', 0, 0, tiled=True)  23.4 us
    all_to_all x4, starting transfers between devices, local(): arrived = lax.all_to_all(message, 'zb', 0, 0, tiled=True)  16.7 us
    dot_general x16, matrix products, local(): jnp.dot(scaled, part, preferred_element_type=F32).astype(BF16)  13.6 us
  transfers between devices with their start and end apart: 23, of which 13 were waited for; matrix products, arithmetic and copies ran while one was open for 2% of the time, Pallas kernels for 0%

profile of v1, /device:TPU:1, one launch (start us, length us, event | category | flops | bytes accessed | tf_op | source)
XLA Modules:
  0.0 449.0 jit_solution(1749392504779828959)
XLA Ops:
  8.1 8.0 %all-to-all-start = ((bf16[16,4,256]{2,1,0:T(4,128)(2,1)}), bf16[16,4,256]{2,1,0:T(4,128)(2,1)S(1)}, u32[]{:S(2)}, u32[]{:S(2)}) async-start(bf16[16,4,256]{2,1,0:T(4,128)(2,1)} %reshape.213), calls=%async_computation | async-start | bytes 65536 | tf_op jit(solution)/shard_map/all_to_all | solution.py:95
  16.1 5.8 %collective-permute-start.2 = (bf16[4,512,128]{2,1,0:T(8,128)(2,1)S(1)}, bf16[4,512,128]{2,1,0:T(8,128)(2,1)}, u32[]{:S(2)}, u32[]{:S(2)}) collective-permute-start(bf16[4,512,128]{2,1,0:T(8,128)(2,1)S(1)} %get-tuple-element.15), channel_id=1, source_target_pairs={{0,6},{2,0},{4,2},{6,4},{1,7},{3,1},{5,3},{7,5},{8,14},{10,8},{12,... | collective-permute-start | bytes 1572872 | tf_op jit(solution)/shard_map/ppermute | solution.py:27
  22.4 8.8 %collective-permute-start.8 = (bf16[256,256]{1,0:T(8,128)(2,1)S(1)}, bf16[256,256]{1,0:T(8,128)(2,1)S(1)}, u32[]{:S(2)}, u32[]{:S(2)}) collective-permute-start(bf16[256,256]{1,0:T(8,128)(2,1)S(1)} %bitcast.122), channel_id=1, source_target_pairs={{0,8},{8,16},{16,24},{24,0},{1,9},{9,17},{17,25},{25,1},{2,10},{10... | collective-permute-start | bytes 393224 | tf_op jit(solution)/shard_map/ppermute | solution.py:27
  31.3 7.9 %collective-permute-start.9 = (bf16[256,256]{1,0:T(8,128)(2,1)S(1)}, bf16[256,256]{1,0:T(8,128)(2,1)S(1)}, u32[]{:S(2)}, u32[]{:S(2)}) collective-permute-start(bf16[256,256]{1,0:T(8,128)(2,1)S(1)} %bitcast.121), channel_id=1, source_target_pairs={{0,16},{8,24},{16,0},{24,8},{1,17},{9,25},{17,1},{25,9},{2,18},{10... | collective-permute-start | bytes 393224 | tf_op jit(solution)/shard_map/ppermute | solution.py:27
  49.4 30.6 %all_gather.24 = bf16[80,2048]{1,0:T(8,128)(2,1)S(1)} all-gather(bf16[80,512]{1,0:T(8,128)(2,1)S(1)} %pad_maximum_fusion.12), channel_id=1, replica_groups=mesh['section'=16,'za'=4,'zb'=4,'y'=2] {'za'}, dimensions={1}, use_global_device_ids=true | all-gather | bytes 409600 | tf_op jit(solution)/shard_map/all_gather | solution.py:128
  90.0 26.7 %collective-permute-done.4 = bf16[4,512,128]{2,1,0:T(8,128)(2,1)S(1)} collective-permute-done((bf16[4,512,128]{2,1,0:T(8,128)(2,1)S(1)}, bf16[4,512,128]{2,1,0:T(8,128)(2,1)S(1)}, u32[]{:S(2)}, u32[]{:S(2)}) %collective-permute-start.4) | collective-permute-done | bytes 524320 | tf_op jit(solution)/shard_map/ppermute | solution.py:27
  125.4 6.1 %collective-permute-done.5 = bf16[2048,128]{1,0:T(8,128)(2,1)S(1)} collective-permute-done((bf16[2048,128]{1,0:T(8,128)(2,1)S(1)}, bf16[2048,128]{1,0:T(8,128)(2,1)S(1)}, u32[]{:S(2)}, u32[]{:S(2)}) %collective-permute-start.5) | collective-permute-done | bytes 524320 | tf_op jit(solution)/shard_map/ppermute | solution.py:27
  131.9 10.9 %collective-permute-done.7 = bf16[2048,128]{1,0:T(8,128)(2,1)S(1)} collective-permute-done((bf16[2048,128]{1,0:T(8,128)(2,1)S(1)}, bf16[2048,128]{1,0:T(8,128)(2,1)S(1)}, u32[]{:S(2)}, u32[]{:S(2)}) %collective-permute-start.7) | collective-permute-done | bytes 524320 | tf_op jit(solution)/shard_map/ppermute | solution.py:27
  157.8 24.2 %all_gather.25 = bf16[64,4096]{1,0:T(8,128)(2,1)S(1)} all-gather(bf16[64,256]{1,0:T(8,128)(2,1)S(1)} %pad_maximum_fusion.20), channel_id=1, replica_groups=mesh['section'=16,'za'=4,'zb'=4,'y'=2] {'za','zb'}, dimensions={1}, use_global_device_ids=true | all-gather | bytes 557056 | tf_op jit(solution)/shard_map/all_gather | solution.py:161
  182.0 13.8 %collective-permute-done.12 = bf16[4096,256]{1,0:T(8,128)(2,1)} collective-permute-done((bf16[4096,256]{1,0:T(8,128)(2,1)}, bf16[4096,256]{1,0:T(8,128)(2,1)}, u32[]{:S(2)}, u32[]{:S(2)}) %collective-permute-start.12) | collective-permute-done | bytes 2097184 | tf_op jit(solution)/shard_map/ppermute | solution.py:27
  198.3 6.6 %collective-permute-start.13 = (bf16[64,512]{1,0:T(8,128)(2,1)S(1)}, bf16[64,512]{1,0:T(8,128)(2,1)S(1)}, u32[]{:S(2)}, u32[]{:S(2)}) collective-permute-start(bf16[64,512]{1,0:T(8,128)(2,1)S(1)} %fusion.32), channel_id=1, source_target_pairs={{0,32},{32,64},{64,96},{96,128},{128,160},{160,192},{192,224},{224... | collective-permute-start | bytes 196616 | tf_op jit(solution)/shard_map/ppermute | solution.py:27
  206.2 17.0 %all_gather.26 = bf16[64,2048]{1,0:T(8,128)(2,1)S(1)} all-gather(bf16[64,512]{1,0:T(8,128)(2,1)S(1)} %collective-permute-done.13), channel_id=1, replica_groups=mesh['section'=16,'za'=4,'zb'=4,'y'=2] {'za'}, dimensions={1}, use_global_device_ids=true | all-gather | bytes 327680 | tf_op jit(solution)/shard_map/all_gather | solution.py:132
  228.2 6.3 %all-to-all-start.2 = ((bf16[4,64,640]{2,1,0:T(8,128)(2,1)}), bf16[4,64,640]{2,1,0:T(8,128)(2,1)S(1)}, u32[]{:S(2)}, u32[]{:S(2)}) async-start(bf16[4,64,640]{2,1,0:T(8,128)(2,1)} %pad_maximum_fusion.9), calls=%async_computation.2 | async-start | bytes 655360 | tf_op jit(solution)/shard_map/all_to_all | solution.py:147
  234.5 6.1 %all-to-all-done.2 = bf16[4,64,640]{2,1,0:T(8,128)(2,1)S(1)} async-done(((bf16[4,64,640]{2,1,0:T(8,128)(2,1)}), bf16[4,64,640]{2,1,0:T(8,128)(2,1)S(1)}, u32[]{:S(2)}, u32[]{:S(2)}) %all-to-all-start.2) | async-done | bytes 327712 | tf_op jit(solution)/shard_map/all_to_all | solution.py:147
  242.0 24.2 %all_gather.27 = bf16[64,4096]{1,0:T(8,128)(2,1)S(1)} all-gather(bf16[64,256]{1,0:T(8,128)(2,1)S(1)} %pad_maximum_fusion.21), channel_id=1, replica_groups=mesh['section'=16,'za'=4,'zb'=4,'y'=2] {'za','zb'}, dimensions={1}, use_global_device_ids=true | all-gather | bytes 557056 | tf_op jit(solution)/shard_map/all_gather | solution.py:161
  268.7 17.0 %collective-permute-start.14 = (bf16[64,512]{1,0:T(8,128)(2,1)S(1)}, bf16[64,512]{1,0:T(8,128)(2,1)S(1)}, u32[]{:S(2)}, u32[]{:S(2)}) collective-permute-start(bf16[64,512]{1,0:T(8,128)(2,1)S(1)} %fusion.33), channel_id=1, source_target_pairs={{0,32},{32,64},{64,96},{96,128},{128,160},{160,192},{192,224},{224... | collective-permute-start | bytes 196616 | tf_op jit(solution)/shard_map/ppermute | solution.py:27
  287.0 15.4 %all_gather.28 = bf16[64,2048]{1,0:T(8,128)(2,1)S(1)} all-gather(bf16[64,512]{1,0:T(8,128)(2,1)S(1)} %collective-permute-done.14), channel_id=1, replica_groups=mesh['section'=16,'za'=4,'zb'=4,'y'=2] {'za'}, dimensions={1}, use_global_device_ids=true | all-gather | bytes 327680 | tf_op jit(solution)/shard_map/all_gather | solution.py:132
  310.8 6.1 %all-to-all-done.3 = bf16[4,64,640]{2,1,0:T(8,128)(2,1)S(1)} async-done(((bf16[4,64,640]{2,1,0:T(8,128)(2,1)}), bf16[4,64,640]{2,1,0:T(8,128)(2,1)S(1)}, u32[]{:S(2)}, u32[]{:S(2)}) %all-to-all-start.3) | async-done | bytes 327712 | tf_op jit(solution)/shard_map/all_to_all | solution.py:147
  318.3 23.5 %all_gather.29 = bf16[64,4096]{1,0:T(8,128)(2,1)S(1)} all-gather(bf16[64,256]{1,0:T(8,128)(2,1)S(1)} %pad_maximum_fusion.22), channel_id=1, replica_groups=mesh['section'=16,'za'=4,'zb'=4,'y'=2] {'za','zb'}, dimensions={1}, use_global_device_ids=true | all-gather | bytes 557056 | tf_op jit(solution)/shard_map/all_gather | solution.py:161
  344.3 18.9 %collective-permute-start.15 = (bf16[64,512]{1,0:T(8,128)(2,1)S(1)}, bf16[64,512]{1,0:T(8,128)(2,1)S(1)}, u32[]{:S(2)}, u32[]{:S(2)}) collective-permute-start(bf16[64,512]{1,0:T(8,128)(2,1)S(1)} %fusion.34), channel_id=1, source_target_pairs={{0,32},{32,64},{64,96},{96,128},{128,160},{160,192},{192,224},{224... | collective-permute-start | bytes 196616 | tf_op jit(solution)/shard_map/ppermute | solution.py:27
  364.5 16.8 %all_gather.30 = bf16[64,2048]{1,0:T(8,128)(2,1)S(1)} all-gather(bf16[64,512]{1,0:T(8,128)(2,1)S(1)} %collective-permute-done.15), channel_id=1, replica_groups=mesh['section'=16,'za'=4,'zb'=4,'y'=2] {'za'}, dimensions={1}, use_global_device_ids=true | all-gather | bytes 327680 | tf_op jit(solution)/shard_map/all_gather | solution.py:132
  389.6 6.1 %all-to-all-done.4 = bf16[4,64,640]{2,1,0:T(8,128)(2,1)S(1)} async-done(((bf16[4,64,640]{2,1,0:T(8,128)(2,1)}), bf16[4,64,640]{2,1,0:T(8,128)(2,1)S(1)}, u32[]{:S(2)}, u32[]{:S(2)}) %all-to-all-start.4) | async-done | bytes 327712 | tf_op jit(solution)/shard_map/all_to_all | solution.py:147
  397.1 23.8 %all_gather.31 = bf16[64,4096]{1,0:T(8,128)(2,1)S(1)} all-gather(bf16[64,256]{1,0:T(8,128)(2,1)S(1)} %pad_maximum_fusion.23), channel_id=1, replica_groups=mesh['section'=16,'za'=4,'zb'=4,'y'=2] {'za','zb'}, dimensions={1}, use_global_device_ids=true | all-gather | bytes 557056 | tf_op jit(solution)/shard_map/all_gather | solution.py:161
  424.0 17.1 %collective-permute-start.16 = (bf16[64,256]{1,0:T(8,128)(2,1)S(1)}, bf16[64,256]{1,0:T(8,128)(2,1)S(1)}, u32[]{:S(2)}, u32[]{:S(2)}) collective-permute-start(bf16[64,256]{1,0:T(8,128)(2,1)S(1)} %get-tuple-element.27), channel_id=1, source_target_pairs={{0,32},{32,64},{64,96},{96,128},{128,160},{160,192},{192,224},{224... | collective-permute-start | bytes 98312 | tf_op jit(solution)/shard_map/ppermute | solution.py:27
  (254 shorter events, 99.4 us)
Async XLA Ops:
  1.8 120.2 %collective-permute-start.1 = (bf16[2048,128]{1,0:T(8,128)(2,1)S(1)}, bf16[2048,128]{1,0:T(8,128)(2,1)}, u32[]{:S(2)}, u32[]{:S(2)}) collective-permute-start(bf16[2048,128]{1,0:T(8,128)(2,1)S(1)} %bitcast.96), channel_id=1, source_target_pairs={{0,1},{1,0},{2,3},{3,2},{4,5},{5,4},{6,7},{7,6},{8,9},{9,8},{10,11... | collective-permute-start | bytes 1572872 | tf_op jit(solution)/shard_map/ppermute | solution.py:27
  8.1 31.3 %all-to-all-start = ((bf16[16,4,256]{2,1,0:T(4,128)(2,1)}), bf16[16,4,256]{2,1,0:T(4,128)(2,1)S(1)}, u32[]{:S(2)}, u32[]{:S(2)}) async-start(bf16[16,4,256]{2,1,0:T(4,128)(2,1)} %reshape.213), calls=%async_computation | async-start | bytes 65536 | tf_op jit(solution)/shard_map/all_to_all | solution.py:95
  16.1 71.9 %collective-permute-start.2 = (bf16[4,512,128]{2,1,0:T(8,128)(2,1)S(1)}, bf16[4,512,128]{2,1,0:T(8,128)(2,1)}, u32[]{:S(2)}, u32[]{:S(2)}) collective-permute-start(bf16[4,512,128]{2,1,0:T(8,128)(2,1)S(1)} %get-tuple-element.15), channel_id=1, source_target_pairs={{0,6},{2,0},{4,2},{6,4},{1,7},{3,1},{5,3},{7,5},{8,14},{10,8},{12,... | collective-permute-start | bytes 1572872 | tf_op jit(solution)/shard_map/ppermute | solution.py:27
  22.4 57.8 %collective-permute-start.8 = (bf16[256,256]{1,0:T(8,128)(2,1)S(1)}, bf16[256,256]{1,0:T(8,128)(2,1)S(1)}, u32[]{:S(2)}, u32[]{:S(2)}) collective-permute-start(bf16[256,256]{1,0:T(8,128)(2,1)S(1)} %bitcast.122), channel_id=1, source_target_pairs={{0,8},{8,16},{16,24},{24,0},{1,9},{9,17},{17,25},{25,1},{2,10},{10... | collective-permute-start | bytes 393224 | tf_op jit(solution)/shard_map/ppermute | solution.py:27
  31.3 51.1 %collective-permute-start.9 = (bf16[256,256]{1,0:T(8,128)(2,1)S(1)}, bf16[256,256]{1,0:T(8,128)(2,1)S(1)}, u32[]{:S(2)}, u32[]{:S(2)}) collective-permute-start(bf16[256,256]{1,0:T(8,128)(2,1)S(1)} %bitcast.121), channel_id=1, source_target_pairs={{0,16},{8,24},{16,0},{24,8},{1,17},{9,25},{17,1},{25,9},{2,18},{10... | collective-permute-start | bytes 393224 | tf_op jit(solution)/shard_map/ppermute | solution.py:27
  39.4 4.7 %collective-permute-start = (bf16[80,256]{1,0:T(8,128)(2,1)S(1)}, bf16[80,256]{1,0:T(8,128)(2,1)S(1)}, u32[]{:S(2)}, u32[]{:S(2)}) collective-permute-start(bf16[80,256]{1,0:T(8,128)(2,1)S(1)} %pad_maximum_fusion.14), channel_id=1, source_target_pairs={{0,1},{1,0},{2,3},{3,2},{4,5},{5,4},{6,7},{7,6},{8,9},{9,8},{10,11... | collective-permute-start | bytes 122888 | tf_op jit(solution)/shard_map/ppermute | solution.py:27
  44.2 40.2 %collective-permute-start.10 = (bf16[256,256]{1,0:T(8,128)(2,1)S(1)}, bf16[256,256]{1,0:T(8,128)(2,1)S(1)}, u32[]{:S(2)}, u32[]{:S(2)}) collective-permute-start(bf16[256,256]{1,0:T(8,128)(2,1)S(1)} %bitcast.123), channel_id=1, source_target_pairs={{0,24},{8,0},{16,8},{24,16},{1,25},{9,1},{17,9},{25,17},{2,26},{10... | collective-permute-start | bytes 393224 | tf_op jit(solution)/shard_map/ppermute | solution.py:27
  49.4 74.0 %copy-start.2 = (bf16[80,256]{1,0:T(8,128)(2,1)}, bf16[80,256]{1,0:T(8,128)(2,1)S(1)}, u32[]{:S(2)}) copy-start(bf16[80,256]{1,0:T(8,128)(2,1)S(1)} %get-tuple-element.60) | copy-start | bytes 122884
  80.2 36.5 %collective-permute-start.4 = (bf16[4,512,128]{2,1,0:T(8,128)(2,1)S(1)}, bf16[4,512,128]{2,1,0:T(8,128)(2,1)S(1)}, u32[]{:S(2)}, u32[]{:S(2)}) collective-permute-start(bf16[4,512,128]{2,1,0:T(8,128)(2,1)S(1)} %get-tuple-element.14), channel_id=1, source_target_pairs={{0,4},{2,6},{4,0},{6,2},{1,5},{3,7},{5,1},{7,3},{8,12},{10,14},{12... | collective-permute-start | bytes 1572872 | tf_op jit(solution)/shard_map/ppermute | solution.py:27
  82.4 36.2 %collective-permute-start.6 = (bf16[4,512,128]{2,1,0:T(8,128)(2,1)S(1)}, bf16[4,512,128]{2,1,0:T(8,128)(2,1)S(1)}, u32[]{:S(2)}, u32[]{:S(2)}) collective-permute-start(bf16[4,512,128]{2,1,0:T(8,128)(2,1)S(1)} %get-tuple-element.13), channel_id=1, source_target_pairs={{0,2},{2,4},{4,6},{6,0},{1,3},{3,5},{5,7},{7,1},{8,10},{10,12},{12... | collective-permute-start | bytes 1572872 | tf_op jit(solution)/shard_map/ppermute | solution.py:27
  84.6 38.8 %collective-permute-start.11 = (bf16[4,256,256]{2,1,0:T(8,128)(2,1)S(1)}, bf16[4,256,256]{2,1,0:T(8,128)(2,1)S(1)}, u32[]{:S(2)}, u32[]{:S(2)}) collective-permute-start(bf16[4,256,256]{2,1,0:T(8,128)(2,1)S(1)} %pad_maximum_fusion.7), channel_id=1, source_target_pairs={{0,1},{1,0},{2,3},{3,2},{4,5},{5,4},{6,7},{7,6},{8,9},{9,8},{10,11... | collective-permute-start | bytes 1572872 | tf_op jit(solution)/shard_map/ppermute | solution.py:27
  88.0 35.9 %collective-permute-start.3 = (bf16[2048,128]{1,0:T(8,128)(2,1)}, bf16[2048,128]{1,0:T(8,128)(2,1)S(1)}, u32[]{:S(2)}, u32[]{:S(2)}) collective-permute-start(bf16[2048,128]{1,0:T(8,128)(2,1)} %bitcast.14), channel_id=1, source_target_pairs={{0,1},{1,0},{2,3},{3,2},{4,5},{5,4},{6,7},{7,6},{8,9},{9,8},{10,11... | collective-permute-start | bytes 1572872 | tf_op jit(solution)/shard_map/ppermute | solution.py:27
  116.7 14.9 %collective-permute-start.5 = (bf16[2048,128]{1,0:T(8,128)(2,1)S(1)}, bf16[2048,128]{1,0:T(8,128)(2,1)S(1)}, u32[]{:S(2)}, u32[]{:S(2)}) collective-permute-start(bf16[2048,128]{1,0:T(8,128)(2,1)S(1)} %bitcast.133), channel_id=1, source_target_pairs={{0,1},{1,0},{2,3},{3,2},{4,5},{5,4},{6,7},{7,6},{8,9},{9,8},{10,11... | collective-permute-start | bytes 1572872 | tf_op jit(solution)/shard_map/ppermute | solution.py:27
  118.6 24.2 %collective-permute-start.7 = (bf16[2048,128]{1,0:T(8,128)(2,1)S(1)}, bf16[2048,128]{1,0:T(8,128)(2,1)S(1)}, u32[]{:S(2)}, u32[]{:S(2)}) collective-permute-start(bf16[2048,128]{1,0:T(8,128)(2,1)S(1)} %bitcast.138), channel_id=1, source_target_pairs={{0,1},{1,0},{2,3},{3,2},{4,5},{5,4},{6,7},{7,6},{8,9},{9,8},{10,11... | collective-permute-start | bytes 1572872 | tf_op jit(solution)/shard_map/ppermute | solution.py:27
  144.4 12.0 %all-to-all-start.1 = ((bf16[4,64,640]{2,1,0:T(8,128)(2,1)}), bf16[4,64,640]{2,1,0:T(8,128)(2,1)S(1)}, u32[]{:S(2)}, u32[]{:S(2)}) async-start(bf16[4,64,640]{2,1,0:T(8,128)(2,1)} %pad_maximum_fusion.8), calls=%async_computation.1 | async-start | bytes 655360 | tf_op jit(solution)/shard_map/all_to_all | solution.py:147
  147.8 48.0 %collective-permute-start.12 = (bf16[4096,256]{1,0:T(8,128)(2,1)}, bf16[4096,256]{1,0:T(8,128)(2,1)}, u32[]{:S(2)}, u32[]{:S(2)}) collective-permute-start(bf16[4096,256]{1,0:T(8,128)(2,1)} %bitcast.128), channel_id=1, source_target_pairs={{0,1},{1,0},{2,3},{3,2},{4,5},{5,4},{6,7},{7,6},{8,9},{9,8},{10,11... | collective-permute-start | bytes 6291464 | tf_op jit(solution)/shard_map/ppermute | solution.py:27
  198.3 7.9 %collective-permute-start.13 = (bf16[64,512]{1,0:T(8,128)(2,1)S(1)}, bf16[64,512]{1,0:T(8,128)(2,1)S(1)}, u32[]{:S(2)}, u32[]{:S(2)}) collective-permute-start(bf16[64,512]{1,0:T(8,128)(2,1)S(1)} %fusion.32), channel_id=1, source_target_pairs={{0,32},{32,64},{64,96},{96,128},{128,160},{160,192},{192,224},{224... | collective-permute-start | bytes 196616 | tf_op jit(solution)/shard_map/ppermute | solution.py:27
  228.2 12.5 %all-to-all-start.2 = ((bf16[4,64,640]{2,1,0:T(8,128)(2,1)}), bf16[4,64,640]{2,1,0:T(8,128)(2,1)S(1)}, u32[]{:S(2)}, u32[]{:S(2)}) async-start(bf16[4,64,640]{2,1,0:T(8,128)(2,1)} %pad_maximum_fusion.9), calls=%async_computation.2 | async-start | bytes 655360 | tf_op jit(solution)/shard_map/all_to_all | solution.py:147
  268.7 18.3 %collective-permute-start.14 = (bf16[64,512]{1,0:T(8,128)(2,1)S(1)}, bf16[64,512]{1,0:T(8,128)(2,1)S(1)}, u32[]{:S(2)}, u32[]{:S(2)}) collective-permute-start(bf16[64,512]{1,0:T(8,128)(2,1)S(1)} %fusion.33), channel_id=1, source_target_pairs={{0,32},{32,64},{64,96},{96,128},{128,160},{160,192},{192,224},{224... | collective-permute-start | bytes 196616 | tf_op jit(solution)/shard_map/ppermute | solution.py:27
  307.3 9.6 %all-to-all-start.3 = ((bf16[4,64,640]{2,1,0:T(8,128)(2,1)}), bf16[4,64,640]{2,1,0:T(8,128)(2,1)S(1)}, u32[]{:S(2)}, u32[]{:S(2)}) async-start(bf16[4,64,640]{2,1,0:T(8,128)(2,1)} %pad_maximum_fusion.10), calls=%async_computation.3 | async-start | bytes 655360 | tf_op jit(solution)/shard_map/all_to_all | solution.py:147
  344.3 20.2 %collective-permute-start.15 = (bf16[64,512]{1,0:T(8,128)(2,1)S(1)}, bf16[64,512]{1,0:T(8,128)(2,1)S(1)}, u32[]{:S(2)}, u32[]{:S(2)}) collective-permute-start(bf16[64,512]{1,0:T(8,128)(2,1)S(1)} %fusion.34), channel_id=1, source_target_pairs={{0,32},{32,64},{64,96},{96,128},{128,160},{160,192},{192,224},{224... | collective-permute-start | bytes 196616 | tf_op jit(solution)/shard_map/ppermute | solution.py:27
  386.1 9.6 %all-to-all-start.4 = ((bf16[4,64,640]{2,1,0:T(8,128)(2,1)}), bf16[4,64,640]{2,1,0:T(8,128)(2,1)S(1)}, u32[]{:S(2)}, u32[]{:S(2)}) async-start(bf16[4,64,640]{2,1,0:T(8,128)(2,1)} %pad_maximum_fusion.11), calls=%async_computation.4 | async-start | bytes 655360 | tf_op jit(solution)/shard_map/all_to_all | solution.py:147
  424.0 20.1 %collective-permute-start.16 = (bf16[64,256]{1,0:T(8,128)(2,1)S(1)}, bf16[64,256]{1,0:T(8,128)(2,1)S(1)}, u32[]{:S(2)}, u32[]{:S(2)}) collective-permute-start(bf16[64,256]{1,0:T(8,128)(2,1)S(1)} %get-tuple-element.27), channel_id=1, source_target_pairs={{0,32},{32,64},{64,96},{96,128},{128,160},{160,192},{192,224},{224... | collective-permute-start | bytes 98312 | tf_op jit(solution)/shard_map/ppermute | solution.py:27
  441.1 7.3 %collective-permute-start.17 = (bf16[64,256]{1,0:T(8,128)(2,1)S(1)}, bf16[64,256]{1,0:T(8,128)(2,1)S(1)}, u32[]{:S(2)}, u32[]{:S(2)}) collective-permute-start(bf16[64,256]{1,0:T(8,128)(2,1)S(1)} %get-tuple-element.28), channel_id=1, source_target_pairs={{0,33},{1,32},{32,65},{33,64},{64,97},{65,96},{96,129},{97,128},{1... | collective-permute-start | bytes 98312 | tf_op jit(solution)/shard_map/ppermute | solution.py:172
  (27 other events, 443.3 us)

commit v2 on v1

v2 whole, which is shorter than its diff:
```python
import math

import jax
import jax.numpy as jnp
from jax import lax
from jax.sharding import Mesh
from jax.sharding import PartitionSpec as P

D = 8192
HD = 128
KVH = 4
MB_DEV = 2
AUD_MB = 32
TXT_MB = 32
AUD_DEV = 32
STEPS = 4
MB_ROWS = 64
CAP = 4
COLS = 256
GROUP = 4
F32 = jnp.float32
BF16 = jnp.bfloat16


def shift(block, axis, distance):
    count = lax.axis_size(axis)
    return lax.ppermute(block, axis, [(i, (i + distance) % count) for i in range(count)])


def rotate(values, cosine, sine):
    half = values.shape[-1] // 2
    first = values[..., :half]
    second = values[..., half:]
    return jnp.concatenate([first * cosine - second * sine, second * cosine + first * sine], -1)


def rope_tables(rows, width):
    position = jnp.arange(rows, dtype=F32)
    freq = 500000.0 ** (-(2.0 * jnp.arange(width // 2, dtype=F32)) / width)
    angle = position[:, None] * freq[None, :]
    return (jnp.cos(angle), jnp.sin(angle))


def pick(stack, index, axis):
    return lax.dynamic_index_in_dim(stack, index, axis, keepdims=False)


def to_all(block, count):
    return jnp.broadcast_to(block[None], (count,) + block.shape)


def split_float(values):
    coarse = values.astype(BF16)
    rest = values - coarse.astype(F32)
    middle = rest.astype(BF16)
    lane = jnp.arange(HD, dtype=jnp.int32)[None, :]
    fine = (rest - middle.astype(F32)).astype(BF16)
    zero = jnp.zeros((), BF16)
    return jnp.where(lane == 0, coarse, jnp.where(lane == 1, middle, jnp.where(lane == 2, fine, zero)))


def in_order(own, other, y, axis):
    first = jnp.where(y == 0, own, other)
    second = jnp.where(y == 0, other, own)
    return jnp.concatenate([first, second], axis)


def local(hidden, audio, audio_dest, segment, norm_gain, w_query, w_keyval, w_out):
    stops = lax.axis_size("section")
    s = lax.axis_index("section")
    a = lax.axis_index("za")
    b = lax.axis_index("zb")
    y = lax.axis_index("y")

    targets = audio_dest[:, 0].reshape(stops, AUD_DEV)
    half_stops = stops // MB_DEV

    order = jnp.arange(AUD_DEV, dtype=jnp.int32)
    own_targets = pick(targets, s, 0)
    rank = jnp.sum(
        ((own_targets[:, None] == own_targets[None, :]) & (order[None, :] < order[:, None])).astype(jnp.int32),
        axis=1,
    )
    holder = 2 * own_targets + s // half_stops
    seats = jnp.arange(stops * MB_DEV * CAP, dtype=jnp.int32)
    chosen = seats[:, None] == (holder * CAP + rank)[None, :]
    outgoing = jnp.dot(chosen.astype(BF16), audio, preferred_element_type=F32).astype(BF16)
    outgoing, w_keys, w_queries = lax.optimization_barrier((outgoing, w_keyval[0], w_query[0]))
    slots = lax.all_to_all(outgoing.reshape(stops * MB_DEV, CAP, COLS), ("section", "y"), 0, 0, tiled=True)
    slots = pick(slots.reshape(MB_DEV, half_stops, 2, CAP, COLS), y, 0)
    slots = slots.transpose(0, 2, 1, 3).reshape(AUD_MB, 2 * COLS)

    text = hidden.reshape(MB_DEV, TXT_MB, COLS)
    gain_rows = jnp.broadcast_to(norm_gain, (16, COLS))

    def batch(index):
        return jnp.concatenate([pick(text, index, 0), gain_rows], 0)

    written = in_order(batch(y), shift(batch(1 - y), "y", 1), y, 1)
    features = GROUP * 2 * COLS
    w_kv = w_keys.reshape(COLS, GROUP, 2 * HD)
    kv_pieces = [pick(w_kv, (a + k) % GROUP, 1) for k in range(GROUP)]
    kv_stack = jnp.stack([shift(piece, "za", k) if k else piece for k, piece in enumerate(kv_pieces)])
    kv_own = jnp.stack([pick(kv_stack, (a - source) % GROUP, 0) for source in range(GROUP)])
    both, kv_own = lax.optimization_barrier((jnp.concatenate([slots, written], 0), kv_own))
    state = both[:MB_ROWS]
    w_kv_rows = in_order(kv_own, shift(kv_own, "y", 1), y, 1).reshape(features, 2 * HD)
    w_q = w_queries.reshape(GROUP, GROUP, 2 * COLS, HD)
    rows_own = jnp.stack([pick(w_q, (b - j) % GROUP, 1).reshape(features, HD) for j in range(GROUP)])
    rows_other = shift(rows_own, "y", 1)

    seat_ids = jnp.arange(AUD_MB, dtype=jnp.int32)
    owner = y * (AUD_MB // CAP) + seat_ids // CAP
    row_ids = jnp.arange(MB_ROWS, dtype=jnp.int32)
    causal = row_ids[None, :] <= row_ids[:, None]
    diagonal = row_ids[None, :] == row_ids[:, None]
    allowed = []
    for lap_step in range(STEPS):
        root = (s - lap_step) % stops
        clip = pick(segment, root * MB_DEV + y, 0)
        counts = jnp.sum((targets == root).astype(jnp.int32), axis=1)
        held = jnp.sum(
            jnp.where(owner[:, None] == jnp.arange(stops, dtype=jnp.int32)[None, :], counts[None, :], 0), axis=1
        )
        live = jnp.concatenate([seat_ids % CAP < held, jnp.ones((TXT_MB,), jnp.bool_)], 0)
        allowed.append(causal & (clip[:, None] == clip[None, :]) & (live[None, :] | diagonal))
    cosine, sine = rope_tables(MB_ROWS, HD)
    scale = 1.0 / math.sqrt(HD)

    for lap_step in range(STEPS):
        if lap_step == 0:
            wide = lax.all_gather(both, "za", axis=1, tiled=True)
            wide, w_o = lax.optimization_barrier((wide, w_out[0]))
            w_o_halves = (w_out[0], shift(w_o, "y", 1))
            w_pair = lax.optimization_barrier(jnp.concatenate([rows_own, rows_other], 2))
            gain_wide = wide[MB_ROWS : MB_ROWS + 1].astype(F32)
            wide = wide[:MB_ROWS].astype(F32)
        else:
            wide = lax.all_gather(state, "za", axis=1, tiled=True).astype(F32)
        scaled = (wide * gain_wide).astype(BF16)
        squares = jnp.sum(wide * wide, axis=1, keepdims=True)
        key_values = jnp.dot(scaled, w_kv_rows, preferred_element_type=F32).astype(BF16)
        payload = jnp.concatenate([scaled, key_values, split_float(squares)], 1)
        gathered = [payload] + [shift(payload, "zb", j) for j in range(1, GROUP)]
        total = sum(part[:, features:].astype(F32) for part in gathered)
        queries = sum(
            jnp.dot(part[:, :features], w_pair[j], preferred_element_type=F32) for j, part in enumerate(gathered)
        )
        total = jnp.concatenate([queries, total], 1)
        inverse = lax.rsqrt(jnp.sum(total[:, 4 * HD :], axis=1, keepdims=True) / D + 1e-05)
        total = total[:, : 4 * HD] * inverse
        key_rows = rotate(total[:, 2 * HD : 3 * HD], cosine, sine).astype(BF16)
        value_rows = total[:, 3 * HD :].astype(BF16)
        heads = []
        for head in range(2):
            query_rows = rotate(total[:, head * HD : (head + 1) * HD], cosine, sine).astype(BF16)
            scores = jnp.dot(query_rows, key_rows.T, preferred_element_type=F32) * scale
            scores = jnp.where(allowed[lap_step], scores, -jnp.inf)
            weights = jnp.exp(scores - jnp.max(scores, axis=-1, keepdims=True))
            probs = (weights / jnp.sum(weights, axis=-1, keepdims=True)).astype(BF16)
            heads.append(jnp.dot(probs, value_rows, preferred_element_type=F32).astype(BF16))
        attended = in_order(heads[0], heads[1], y, 1)
        attended = lax.all_gather(attended, ("za", "zb"), axis=1, tiled=True)
        projected = [jnp.dot(attended, half, preferred_element_type=F32) for half in w_o_halves]
        state_wide = state.astype(F32)
        if lap_step < STEPS - 1:
            update = in_order(projected[0], projected[1], y, 1)
            state = shift((state_wide + update).astype(BF16), "section", 1)
    low, high = state_wide[:, :COLS], state_wide[:, COLS:]
    own = (jnp.where(y == 0, low, high) + projected[0]).astype(BF16)
    other = (jnp.where(y == 0, high, low) + projected[1]).astype(BF16)
    crossing = [(2 * i + j, 2 * ((i + 1) % stops) + 1 - j) for i in range(stops) for j in range(2)]
    own = shift(own, "section", 1)
    other = lax.ppermute(other, ("section", "y"), crossing)
    return in_order(own, other, y, 0)


def solution(mesh):
    sections = mesh.shape["section"]
    parts = mesh.shape["tensor"]
    names = ("section", "za", "zb", "y")
    fine = Mesh(mesh.devices.reshape(sections, parts // (2 * GROUP), GROUP, 2), names)
    tensor = names[1:]
    in_specs = (
        P("section", tensor),
        P("section", tensor),
        P(),
        P(),
        P("section", tensor),
        P("section", None, tensor),
        P("section", tensor, None),
        P("section", None, tensor),
    )
    return jax.shard_map(local, mesh=fine, in_specs=in_specs, out_specs=P("section", tensor), check_vma=False)
```

time: 451 us -> 444 us (0.984)
  matrix products: 28.6 us -> 16.1 us
  blocking collectives: 176 us -> 171 us
    ppermute x17 -> x23, waiting for transfers between devices: 64 us -> 88 us  [shift(): lax.ppermute(block, axis, [(i, (i + distance) % count) for i in range(cou...]
    all_to_all x5 -> x1, starting transfers between devices: 24.7 us -> 8.59 us  [local(): lax.all_to_all(outgoing.reshape(stops * MB_DEV, CAP, COLS), ('section', '...]
    all_to_all x5 -> x1, waiting for transfers between devices: 23.4 us -> 7.75 us  [local(): lax.all_to_all(outgoing.reshape(stops * MB_DEV, CAP, COLS), ('section', '...]
    dot_general x20 -> x24, matrix products: 23.9 us -> 11.4 us  [the longest x16 7.71 us: local(): jnp.dot(part[:, :features], w_pair[j], preferred_element_type=F32)]
    ppermute x1, starting transfers between devices: 2.97 us -> 12.6 us  [local(): other = lax.ppermute(other, ('section', 'y'), crossing)]
    all_gather x1, blocking collectives: 30.6 us -> 25.5 us  [local(): wide = lax.all_gather(both, 'za', axis=1, tiled=True)]
    ppermute x17 -> x23, starting transfers between devices: 110 us -> 115 us  [shift(): lax.ppermute(block, axis, [(i, (i + distance) % count) for i in range(cou...]
  transfers between devices with their start and end apart: 23 -> 25, of which waited for: 13 -> 17; matrix products, arithmetic and copies ran while one was open for 2% -> 4% of each run, Pallas kernels for 0% -> 0%
where the time goes in v2:
time: 444 us; the launch traced here: 441 us
  blocking collectives  171 us (39%)
  starting transfers between devices  136 us (31%)
  waiting for transfers between devices  95.7 us (22%)
  matrix products  16.1 us (4%)
  other arithmetic  12.6 us (3%)
  local copies, waits for them, and re-layouts  7.7 us (2%)
    ppermute x23, starting transfers between devices, shift(): lax.ppermute(block, axis, [(i, (i + distance) % count) for i in range(cou...  115 us
    all_gather x4, blocking collectives, local(): attended = lax.all_gather(attended, ('za', 'zb'), axis=1, tiled=True)  97.4 us
    ppermute x23, waiting for transfers between devices, shift(): lax.ppermute(block, axis, [(i, (i + distance) % count) for i in range(cou...  88 us
    all_gather x3, blocking collectives, local(): wide = lax.all_gather(state, 'za', axis=1, tiled=True).astype(F32)  48.1 us
    all_gather x1, blocking collectives, local(): wide = lax.all_gather(both, 'za', axis=1, tiled=True)  25.5 us
    ppermute x1, starting transfers between devices, local(): other = lax.ppermute(other, ('section', 'y'), crossing)  12.6 us
  transfers between devices with their start and end apart: 25, of which 17 were waited for; matrix products, arithmetic and copies ran while one was open for 4% of the time, Pallas kernels for 0%

profile of v2, /device:TPU:1, one launch (start us, length us, event | category | flops | bytes accessed | tf_op | source)
XLA Modules:
  0.0 440.6 jit_solution(4547622893819378297)
XLA Ops:
  11.9 8.8 %collective-permute-start.1 = (bf16[256,256]{1,0:T(8,128)(2,1)S(1)}, bf16[256,256]{1,0:T(8,128)(2,1)S(1)}, u32[]{:S(2)}, u32[]{:S(2)}) collective-permute-start(bf16[256,256]{1,0:T(8,128)(2,1)S(1)} %bitcast.130), channel_id=1, source_target_pairs={{0,8},{8,16},{16,24},{24,0},{1,9},{9,17},{17,25},{25,1},{2,10},{10... | collective-permute-start | bytes 393224 | tf_op jit(solution)/shard_map/ppermute | solution.py:27
  20.8 10.6 %collective-permute-start.2 = (bf16[256,256]{1,0:T(8,128)(2,1)S(1)}, bf16[256,256]{1,0:T(8,128)(2,1)S(1)}, u32[]{:S(2)}, u32[]{:S(2)}) collective-permute-start(bf16[256,256]{1,0:T(8,128)(2,1)S(1)} %bitcast.131), channel_id=1, source_target_pairs={{0,16},{8,24},{16,0},{24,8},{1,17},{9,25},{17,1},{25,9},{2,18},{10... | collective-permute-start | bytes 393224 | tf_op jit(solution)/shard_map/ppermute | solution.py:27
  31.6 5.2 %collective-permute-start.3 = (bf16[256,256]{1,0:T(8,128)(2,1)S(1)}, bf16[256,256]{1,0:T(8,128)(2,1)S(1)}, u32[]{:S(2)}, u32[]{:S(2)}) collective-permute-start(bf16[256,256]{1,0:T(8,128)(2,1)S(1)} %bitcast.132), channel_id=1, source_target_pairs={{0,24},{8,0},{16,8},{24,16},{1,25},{9,1},{17,9},{25,17},{2,26},{10... | collective-permute-start | bytes 393224 | tf_op jit(solution)/shard_map/ppermute | solution.py:27
  37.4 8.6 %all-to-all-start = ((bf16[32,4,256]{2,1,0:T(4,128)(2,1)}), bf16[32,4,256]{2,1,0:T(4,128)(2,1)S(1)}, u32[]{:S(2)}, u32[]{:S(2)}) async-start(bf16[32,4,256]{2,1,0:T(4,128)(2,1)} %reshape.209), calls=%async_computation | async-start | bytes 131072 | tf_op jit(solution)/shard_map/all_to_all | solution.py:89
  53.6 7.8 %all-to-all-done = bf16[32,4,256]{2,1,0:T(4,128)(2,1)S(1)} async-done(((bf16[32,4,256]{2,1,0:T(4,128)(2,1)}), bf16[32,4,256]{2,1,0:T(4,128)(2,1)S(1)}, u32[]{:S(2)}, u32[]{:S(2)}) %all-to-all-start) | async-done | bytes 65568 | tf_op jit(solution)/shard_map/all_to_all | solution.py:89
  63.7 25.5 %all_gather.24 = bf16[80,2048]{1,0:T(8,128)(2,1)S(1)} all-gather(bf16[80,512]{1,0:T(8,128)(2,1)S(1)} %maximum_maximum_fusion), channel_id=1, replica_groups=mesh['section'=16,'za'=4,'zb'=4,'y'=2] {'za'}, dimensions={1}, use_global_device_ids=true | all-gather | bytes 409600 | tf_op jit(solution)/shard_map/all_gather | solution.py:132
  93.1 4.8 %collective-permute-start.8 = (bf16[64,2432]{1,0:T(8,128)(2,1)}, bf16[64,2432]{1,0:T(8,128)(2,1)}, u32[]{:S(2)}, u32[]{:S(2)}) collective-permute-start(bf16[64,2432]{1,0:T(8,128)(2,1)} %pad_maximum_fusion.5), channel_id=1, source_target_pairs={{0,6},{2,0},{4,2},{6,4},{1,7},{3,1},{5,3},{7,5},{8,14},{10,8},{12,... | collective-permute-start | bytes 933896 | tf_op jit(solution)/shard_map/ppermute | solution.py:27
  105.0 5.0 %collective-permute-done.8 = bf16[64,2432]{1,0:T(8,128)(2,1)} collective-permute-done((bf16[64,2432]{1,0:T(8,128)(2,1)}, bf16[64,2432]{1,0:T(8,128)(2,1)}, u32[]{:S(2)}, u32[]{:S(2)}) %collective-permute-start.8) | collective-permute-done | bytes 311328 | tf_op jit(solution)/shard_map/ppermute | solution.py:27
  109.9 13.2 %collective-permute-done.7 = bf16[64,2432]{1,0:T(8,128)(2,1)} collective-permute-done((bf16[64,2432]{1,0:T(8,128)(2,1)}, bf16[64,2432]{1,0:T(8,128)(2,1)}, u32[]{:S(2)}, u32[]{:S(2)}) %collective-permute-start.7) | collective-permute-done | bytes 311328 | tf_op jit(solution)/shard_map/ppermute | solution.py:27
  131.9 22.2 %all_gather.25 = bf16[64,4096]{1,0:T(8,128)(2,1)S(1)} all-gather(bf16[64,256]{1,0:T(8,128)(2,1)S(1)} %pad_maximum_fusion.16), channel_id=1, replica_groups=mesh['section'=16,'za'=4,'zb'=4,'y'=2] {'za','zb'}, dimensions={1}, use_global_device_ids=true | all-gather | bytes 557056 | tf_op jit(solution)/shard_map/all_gather | solution.py:163
  155.1 11.6 %collective-permute-start.10 = (bf16[64,512]{1,0:T(8,128)(2,1)S(1)}, bf16[64,512]{1,0:T(8,128)(2,1)S(1)}, u32[]{:S(2)}, u32[]{:S(2)}) collective-permute-start(bf16[64,512]{1,0:T(8,128)(2,1)S(1)} %fusion.46), channel_id=1, source_target_pairs={{0,32},{32,64},{64,96},{96,128},{128,160},{160,192},{192,224},{224... | collective-permute-start | bytes 196616 | tf_op jit(solution)/shard_map/ppermute | solution.py:27
  168.0 15.7 %all_gather.26 = bf16[64,2048]{1,0:T(8,128)(2,1)S(1)} all-gather(bf16[64,512]{1,0:T(8,128)(2,1)S(1)} %collective-permute-done.10), channel_id=1, replica_groups=mesh['section'=16,'za'=4,'zb'=4,'y'=2] {'za'}, dimensions={1}, use_global_device_ids=true | all-gather | bytes 327680 | tf_op jit(solution)/shard_map/all_gather | solution.py:139
  197.6 16.9 %collective-permute-done.12 = bf16[64,2432]{1,0:T(8,128)(2,1)S(1)} collective-permute-done((bf16[64,2432]{1,0:T(8,128)(2,1)S(1)}, bf16[64,2432]{1,0:T(8,128)(2,1)S(1)}, u32[]{:S(2)}, u32[]{:S(2)}) %collective-permute-start.12) | collective-permute-done | bytes 311328 | tf_op jit(solution)/shard_map/ppermute | solution.py:27
  216.5 27.1 %all_gather.27 = bf16[64,4096]{1,0:T(8,128)(2,1)S(1)} all-gather(bf16[64,256]{1,0:T(8,128)(2,1)S(1)} %pad_maximum_fusion.17), channel_id=1, replica_groups=mesh['section'=16,'za'=4,'zb'=4,'y'=2] {'za','zb'}, dimensions={1}, use_global_device_ids=true | all-gather | bytes 557056 | tf_op jit(solution)/shard_map/all_gather | solution.py:163
  244.5 12.0 %collective-permute-start.14 = (bf16[64,512]{1,0:T(8,128)(2,1)S(1)}, bf16[64,512]{1,0:T(8,128)(2,1)S(1)}, u32[]{:S(2)}, u32[]{:S(2)}) collective-permute-start(bf16[64,512]{1,0:T(8,128)(2,1)S(1)} %fusion.47), channel_id=1, source_target_pairs={{0,32},{32,64},{64,96},{96,128},{128,160},{160,192},{192,224},{224... | collective-permute-start | bytes 196616 | tf_op jit(solution)/shard_map/ppermute | solution.py:27
  257.8 16.3 %all_gather.28 = bf16[64,2048]{1,0:T(8,128)(2,1)S(1)} all-gather(bf16[64,512]{1,0:T(8,128)(2,1)S(1)} %collective-permute-done.14), channel_id=1, replica_groups=mesh['section'=16,'za'=4,'zb'=4,'y'=2] {'za'}, dimensions={1}, use_global_device_ids=true | all-gather | bytes 327680 | tf_op jit(solution)/shard_map/all_gather | solution.py:139
  287.8 16.5 %collective-permute-done.16 = bf16[64,2432]{1,0:T(8,128)(2,1)S(1)} collective-permute-done((bf16[64,2432]{1,0:T(8,128)(2,1)S(1)}, bf16[64,2432]{1,0:T(8,128)(2,1)S(1)}, u32[]{:S(2)}, u32[]{:S(2)}) %collective-permute-start.16) | collective-permute-done | bytes 311328 | tf_op jit(solution)/shard_map/ppermute | solution.py:27
  306.3 24.2 %all_gather.29 = bf16[64,4096]{1,0:T(8,128)(2,1)S(1)} all-gather(bf16[64,256]{1,0:T(8,128)(2,1)S(1)} %pad_maximum_fusion.18), channel_id=1, replica_groups=mesh['section'=16,'za'=4,'zb'=4,'y'=2] {'za','zb'}, dimensions={1}, use_global_device_ids=true | all-gather | bytes 557056 | tf_op jit(solution)/shard_map/all_gather | solution.py:163
  331.4 16.9 %collective-permute-start.18 = (bf16[64,512]{1,0:T(8,128)(2,1)S(1)}, bf16[64,512]{1,0:T(8,128)(2,1)S(1)}, u32[]{:S(2)}, u32[]{:S(2)}) collective-permute-start(bf16[64,512]{1,0:T(8,128)(2,1)S(1)} %fusion.48), channel_id=1, source_target_pairs={{0,32},{32,64},{64,96},{96,128},{128,160},{160,192},{192,224},{224... | collective-permute-start | bytes 196616 | tf_op jit(solution)/shard_map/ppermute | solution.py:27
  349.6 16.1 %all_gather.30 = bf16[64,2048]{1,0:T(8,128)(2,1)S(1)} all-gather(bf16[64,512]{1,0:T(8,128)(2,1)S(1)} %collective-permute-done.18), channel_id=1, replica_groups=mesh['section'=16,'za'=4,'zb'=4,'y'=2] {'za'}, dimensions={1}, use_global_device_ids=true | all-gather | bytes 327680 | tf_op jit(solution)/shard_map/all_gather | solution.py:139
  376.6 7.0 %collective-permute-done.21 = bf16[64,2432]{1,0:T(8,128)(2,1)S(1)} collective-permute-done((bf16[64,2432]{1,0:T(8,128)(2,1)S(1)}, bf16[64,2432]{1,0:T(8,128)(2,1)S(1)}, u32[]{:S(2)}, u32[]{:S(2)}) %collective-permute-start.21) | collective-permute-done | bytes 311328 | tf_op jit(solution)/shard_map/ppermute | solution.py:27
  383.6 13.8 %collective-permute-done.20 = bf16[64,2432]{1,0:T(8,128)(2,1)S(1)} collective-permute-done((bf16[64,2432]{1,0:T(8,128)(2,1)S(1)}, bf16[64,2432]{1,0:T(8,128)(2,1)S(1)}, u32[]{:S(2)}, u32[]{:S(2)}) %collective-permute-start.20) | collective-permute-done | bytes 311328 | tf_op jit(solution)/shard_map/ppermute | solution.py:27
  399.4 23.9 %all_gather.31 = bf16[64,4096]{1,0:T(8,128)(2,1)S(1)} all-gather(bf16[64,256]{1,0:T(8,128)(2,1)S(1)} %pad_maximum_fusion.19), channel_id=1, replica_groups=mesh['section'=16,'za'=4,'zb'=4,'y'=2] {'za','zb'}, dimensions={1}, use_global_device_ids=true | all-gather | bytes 557056 | tf_op jit(solution)/shard_map/all_gather | solution.py:163
  424.3 12.6 %collective-permute-start.23 = (bf16[64,256]{1,0:T(8,128)(2,1)S(1)}, bf16[64,256]{1,0:T(8,128)(2,1)S(1)}, u32[]{:S(2)}, u32[]{:S(2)}) collective-permute-start(bf16[64,256]{1,0:T(8,128)(2,1)S(1)} %add_convert_fusion), channel_id=1, source_target_pairs={{0,33},{1,32},{32,65},{33,64},{64,97},{65,96},{96,129},{97,128},{1... | collective-permute-start | bytes 98312 | tf_op jit(solution)/shard_map/ppermute | solution.py:174
  (211 shorter events, 97.1 us)
Async XLA Ops:
  7.7 116.5 %collective-permute-start.4 = (bf16[4,2048,128]{2,1,0:T(8,128)(2,1)}, bf16[4,2048,128]{2,1,0:T(8,128)(2,1)}, u32[]{:S(2)}, u32[]{:S(2)}) collective-permute-start(bf16[4,2048,128]{2,1,0:T(8,128)(2,1)} %pad_maximum_fusion.1), channel_id=1, source_target_pairs={{0,1},{1,0},{2,3},{3,2},{4,5},{5,4},{6,7},{7,6},{8,9},{9,8},{10,11... | collective-permute-start | bytes 6291464 | tf_op jit(solution)/shard_map/ppermute | solution.py:27
  11.9 49.5 %collective-permute-start.1 = (bf16[256,256]{1,0:T(8,128)(2,1)S(1)}, bf16[256,256]{1,0:T(8,128)(2,1)S(1)}, u32[]{:S(2)}, u32[]{:S(2)}) collective-permute-start(bf16[256,256]{1,0:T(8,128)(2,1)S(1)} %bitcast.130), channel_id=1, source_target_pairs={{0,8},{8,16},{16,24},{24,0},{1,9},{9,17},{17,25},{25,1},{2,10},{10... | collective-permute-start | bytes 393224 | tf_op jit(solution)/shard_map/ppermute | solution.py:27
  20.8 40.6 %collective-permute-start.2 = (bf16[256,256]{1,0:T(8,128)(2,1)S(1)}, bf16[256,256]{1,0:T(8,128)(2,1)S(1)}, u32[]{:S(2)}, u32[]{:S(2)}) collective-permute-start(bf16[256,256]{1,0:T(8,128)(2,1)S(1)} %bitcast.131), channel_id=1, source_target_pairs={{0,16},{8,24},{16,0},{24,8},{1,17},{9,25},{17,1},{25,9},{2,18},{10... | collective-permute-start | bytes 393224 | tf_op jit(solution)/shard_map/ppermute | solution.py:27
  31.6 29.8 %collective-permute-start.3 = (bf16[256,256]{1,0:T(8,128)(2,1)S(1)}, bf16[256,256]{1,0:T(8,128)(2,1)S(1)}, u32[]{:S(2)}, u32[]{:S(2)}) collective-permute-start(bf16[256,256]{1,0:T(8,128)(2,1)S(1)} %bitcast.132), channel_id=1, source_target_pairs={{0,24},{8,0},{16,8},{24,16},{1,25},{9,1},{17,9},{25,17},{2,26},{10... | collective-permute-start | bytes 393224 | tf_op jit(solution)/shard_map/ppermute | solution.py:27
  37.4 23.9 %all-to-all-start = ((bf16[32,4,256]{2,1,0:T(4,128)(2,1)}), bf16[32,4,256]{2,1,0:T(4,128)(2,1)S(1)}, u32[]{:S(2)}, u32[]{:S(2)}) async-start(bf16[32,4,256]{2,1,0:T(4,128)(2,1)} %reshape.209), calls=%async_computation | async-start | bytes 131072 | tf_op jit(solution)/shard_map/all_to_all | solution.py:89
  46.1 7.4 %collective-permute-start = (bf16[48,256]{1,0:T(8,128)(2,1)S(1)}, bf16[48,256]{1,0:T(8,128)(2,1)S(1)}, u32[]{:S(2)}, u32[]{:S(2)}) collective-permute-start(bf16[48,256]{1,0:T(8,128)(2,1)S(1)} %pad_maximum_fusion.14), channel_id=1, source_target_pairs={{0,1},{1,0},{2,3},{3,2},{4,5},{5,4},{6,7},{7,6},{8,9},{9,8},{10,11... | collective-permute-start | bytes 73736 | tf_op jit(solution)/shard_map/ppermute | solution.py:27
  61.7 27.8 %collective-permute-start.5 = (bf16[4,256,256]{2,1,0:T(8,128)(2,1)S(1)}, bf16[4,256,256]{2,1,0:T(8,128)(2,1)S(1)}, u32[]{:S(2)}, u32[]{:S(2)}) collective-permute-start(bf16[4,256,256]{2,1,0:T(8,128)(2,1)S(1)} %pad_maximum_fusion.4), channel_id=1, source_target_pairs={{0,1},{1,0},{2,3},{3,2},{4,5},{5,4},{6,7},{7,6},{8,9},{9,8},{10,11... | collective-permute-start | bytes 1572872 | tf_op jit(solution)/shard_map/ppermute | solution.py:27
  90.9 14.1 %collective-permute-start.6 = (bf16[64,2432]{1,0:T(8,128)(2,1)}, bf16[64,2432]{1,0:T(8,128)(2,1)}, u32[]{:S(2)}, u32[]{:S(2)}) collective-permute-start(bf16[64,2432]{1,0:T(8,128)(2,1)} %pad_maximum_fusion.5), channel_id=1, source_target_pairs={{0,2},{2,4},{4,6},{6,0},{1,3},{3,5},{5,7},{7,1},{8,10},{10,12},{12... | collective-permute-start | bytes 933896 | tf_op jit(solution)/shard_map/ppermute | solution.py:27
  93.1 16.8 %collective-permute-start.8 = (bf16[64,2432]{1,0:T(8,128)(2,1)}, bf16[64,2432]{1,0:T(8,128)(2,1)}, u32[]{:S(2)}, u32[]{:S(2)}) collective-permute-start(bf16[64,2432]{1,0:T(8,128)(2,1)} %pad_maximum_fusion.5), channel_id=1, source_target_pairs={{0,6},{2,0},{4,2},{6,4},{1,7},{3,1},{5,3},{7,5},{8,14},{10,8},{12,... | collective-permute-start | bytes 933896 | tf_op jit(solution)/shard_map/ppermute | solution.py:27
  98.0 25.2 %collective-permute-start.7 = (bf16[64,2432]{1,0:T(8,128)(2,1)}, bf16[64,2432]{1,0:T(8,128)(2,1)}, u32[]{:S(2)}, u32[]{:S(2)}) collective-permute-start(bf16[64,2432]{1,0:T(8,128)(2,1)} %pad_maximum_fusion.5), channel_id=1, source_target_pairs={{0,4},{2,6},{4,0},{6,2},{1,5},{3,7},{5,1},{7,3},{8,12},{10,14},{12... | collective-permute-start | bytes 933896 | tf_op jit(solution)/shard_map/ppermute | solution.py:27
  102.5 52.0 %collective-permute-start.9 = (bf16[4096,256]{1,0:T(8,128)(2,1)S(1)}, bf16[4096,256]{1,0:T(8,128)(2,1)S(1)}, u32[]{:S(2)}, u32[]{:S(2)}) collective-permute-start(bf16[4096,256]{1,0:T(8,128)(2,1)S(1)} %bitcast.108), channel_id=1, source_target_pairs={{0,1},{1,0},{2,3},{3,2},{4,5},{5,4},{6,7},{7,6},{8,9},{9,8},{10,11... | collective-permute-start | bytes 6291464 | tf_op jit(solution)/shard_map/ppermute | solution.py:27
  155.1 13.0 %collective-permute-start.10 = (bf16[64,512]{1,0:T(8,128)(2,1)S(1)}, bf16[64,512]{1,0:T(8,128)(2,1)S(1)}, u32[]{:S(2)}, u32[]{:S(2)}) collective-permute-start(bf16[64,512]{1,0:T(8,128)(2,1)S(1)} %fusion.46), channel_id=1, source_target_pairs={{0,32},{32,64},{64,96},{96,128},{128,160},{160,192},{192,224},{224... | collective-permute-start | bytes 196616 | tf_op jit(solution)/shard_map/ppermute | solution.py:27
  184.3 10.5 %collective-permute-start.11 = (bf16[64,2432]{1,0:T(8,128)(2,1)S(1)}, bf16[64,2432]{1,0:T(8,128)(2,1)S(1)}, u32[]{:S(2)}, u32[]{:S(2)}) collective-permute-start(bf16[64,2432]{1,0:T(8,128)(2,1)S(1)} %pad_maximum_fusion.6), channel_id=1, source_target_pairs={{0,2},{2,4},{4,6},{6,0},{1,3},{3,5},{5,7},{7,1},{8,10},{10,12},{12... | collective-permute-start | bytes 933896 | tf_op jit(solution)/shard_map/ppermute | solution.py:27
  186.7 10.9 %collective-permute-start.13 = (bf16[64,2432]{1,0:T(8,128)(2,1)S(1)}, bf16[64,2432]{1,0:T(8,128)(2,1)S(1)}, u32[]{:S(2)}, u32[]{:S(2)}) collective-permute-start(bf16[64,2432]{1,0:T(8,128)(2,1)S(1)} %pad_maximum_fusion.6), channel_id=1, source_target_pairs={{0,6},{2,0},{4,2},{6,4},{1,7},{3,1},{5,3},{7,5},{8,14},{10,8},{12,... | collective-permute-start | bytes 933896 | tf_op jit(solution)/shard_map/ppermute | solution.py:27
  191.4 23.0 %collective-permute-start.12 = (bf16[64,2432]{1,0:T(8,128)(2,1)S(1)}, bf16[64,2432]{1,0:T(8,128)(2,1)S(1)}, u32[]{:S(2)}, u32[]{:S(2)}) collective-permute-start(bf16[64,2432]{1,0:T(8,128)(2,1)S(1)} %pad_maximum_fusion.6), channel_id=1, source_target_pairs={{0,4},{2,6},{4,0},{6,2},{1,5},{3,7},{5,1},{7,3},{8,12},{10,14},{12... | collective-permute-start | bytes 933896 | tf_op jit(solution)/shard_map/ppermute | solution.py:27
  244.5 13.3 %collective-permute-start.14 = (bf16[64,512]{1,0:T(8,128)(2,1)S(1)}, bf16[64,512]{1,0:T(8,128)(2,1)S(1)}, u32[]{:S(2)}, u32[]{:S(2)}) collective-permute-start(bf16[64,512]{1,0:T(8,128)(2,1)S(1)} %fusion.47), channel_id=1, source_target_pairs={{0,32},{32,64},{64,96},{96,128},{128,160},{160,192},{192,224},{224... | collective-permute-start | bytes 196616 | tf_op jit(solution)/shard_map/ppermute | solution.py:27
  274.7 9.9 %collective-permute-start.15 = (bf16[64,2432]{1,0:T(8,128)(2,1)S(1)}, bf16[64,2432]{1,0:T(8,128)(2,1)S(1)}, u32[]{:S(2)}, u32[]{:S(2)}) collective-permute-start(bf16[64,2432]{1,0:T(8,128)(2,1)S(1)} %pad_maximum_fusion.7), channel_id=1, source_target_pairs={{0,2},{2,4},{4,6},{6,0},{1,3},{3,5},{5,7},{7,1},{8,10},{10,12},{12... | collective-permute-start | bytes 933896 | tf_op jit(solution)/shard_map/ppermute | solution.py:27
  279.0 8.8 %collective-permute-start.17 = (bf16[64,2432]{1,0:T(8,128)(2,1)S(1)}, bf16[64,2432]{1,0:T(8,128)(2,1)S(1)}, u32[]{:S(2)}, u32[]{:S(2)}) collective-permute-start(bf16[64,2432]{1,0:T(8,128)(2,1)S(1)} %pad_maximum_fusion.7), channel_id=1, source_target_pairs={{0,6},{2,0},{4,2},{6,4},{1,7},{3,1},{5,3},{7,5},{8,14},{10,8},{12,... | collective-permute-start | bytes 933896 | tf_op jit(solution)/shard_map/ppermute | solution.py:27
  281.8 22.5 %collective-permute-start.16 = (bf16[64,2432]{1,0:T(8,128)(2,1)S(1)}, bf16[64,2432]{1,0:T(8,128)(2,1)S(1)}, u32[]{:S(2)}, u32[]{:S(2)}) collective-permute-start(bf16[64,2432]{1,0:T(8,128)(2,1)S(1)} %pad_maximum_fusion.7), channel_id=1, source_target_pairs={{0,4},{2,6},{4,0},{6,2},{1,5},{3,7},{5,1},{7,3},{8,12},{10,14},{12... | collective-permute-start | bytes 933896 | tf_op jit(solution)/shard_map/ppermute | solution.py:27
  331.4 18.2 %collective-permute-start.18 = (bf16[64,512]{1,0:T(8,128)(2,1)S(1)}, bf16[64,512]{1,0:T(8,128)(2,1)S(1)}, u32[]{:S(2)}, u32[]{:S(2)}) collective-permute-start(bf16[64,512]{1,0:T(8,128)(2,1)S(1)} %fusion.48), channel_id=1, source_target_pairs={{0,32},{32,64},{64,96},{96,128},{128,160},{160,192},{192,224},{224... | collective-permute-start | bytes 196616 | tf_op jit(solution)/shard_map/ppermute | solution.py:27
  366.4 9.6 %collective-permute-start.19 = (bf16[64,2432]{1,0:T(8,128)(2,1)S(1)}, bf16[64,2432]{1,0:T(8,128)(2,1)S(1)}, u32[]{:S(2)}, u32[]{:S(2)}) collective-permute-start(bf16[64,2432]{1,0:T(8,128)(2,1)S(1)} %pad_maximum_fusion.8), channel_id=1, source_target_pairs={{0,2},{2,4},{4,6},{6,0},{1,3},{3,5},{5,7},{7,1},{8,10},{10,12},{12... | collective-permute-start | bytes 933896 | tf_op jit(solution)/shard_map/ppermute | solution.py:27
  369.4 14.2 %collective-permute-start.21 = (bf16[64,2432]{1,0:T(8,128)(2,1)S(1)}, bf16[64,2432]{1,0:T(8,128)(2,1)S(1)}, u32[]{:S(2)}, u32[]{:S(2)}) collective-permute-start(bf16[64,2432]{1,0:T(8,128)(2,1)S(1)} %pad_maximum_fusion.8), channel_id=1, source_target_pairs={{0,6},{2,0},{4,2},{6,4},{1,7},{3,1},{5,3},{7,5},{8,14},{10,8},{12,... | collective-permute-start | bytes 933896 | tf_op jit(solution)/shard_map/ppermute | solution.py:27
  373.5 24.0 %collective-permute-start.20 = (bf16[64,2432]{1,0:T(8,128)(2,1)S(1)}, bf16[64,2432]{1,0:T(8,128)(2,1)S(1)}, u32[]{:S(2)}, u32[]{:S(2)}) collective-permute-start(bf16[64,2432]{1,0:T(8,128)(2,1)S(1)} %pad_maximum_fusion.8), channel_id=1, source_target_pairs={{0,4},{2,6},{4,0},{6,2},{1,5},{3,7},{5,1},{7,3},{8,12},{10,14},{12... | collective-permute-start | bytes 933896 | tf_op jit(solution)/shard_map/ppermute | solution.py:27
  424.3 14.5 %collective-permute-start.23 = (bf16[64,256]{1,0:T(8,128)(2,1)S(1)}, bf16[64,256]{1,0:T(8,128)(2,1)S(1)}, u32[]{:S(2)}, u32[]{:S(2)}) collective-permute-start(bf16[64,256]{1,0:T(8,128)(2,1)S(1)} %add_convert_fusion), channel_id=1, source_target_pairs={{0,33},{1,32},{32,65},{33,64},{64,97},{65,96},{96,129},{97,128},{1... | collective-permute-start | bytes 98312 | tf_op jit(solution)/shard_map/ppermute | solution.py:174
  (18 other events, 413.4 us)

commit v3 on v2

--- a/solution.py
+++ b/solution.py
@@ -72,6 +72,18 @@
     b = lax.axis_index("zb")
     y = lax.axis_index("y")
 
+    features = GROUP * 2 * COLS
+    w_q = w_query[0].reshape(GROUP, GROUP, 2 * COLS, HD)
+    parts = [pick(w_q, (b - j) % GROUP, 1).reshape(features, HD) for j in range(GROUP)]
+    group_own = [shift(part, "zb", -j) if j else part for j, part in enumerate(parts)]
+
+    text = hidden.reshape(MB_DEV, TXT_MB, COLS)
+    gain_rows = jnp.broadcast_to(norm_gain, (16, COLS))
+
+    def batch(index):
+        return jnp.concatenate([pick(text, index, 0), gain_rows], 0)
+
+    written = in_order(batch(y), shift(batch(1 - y), "y", 1), y, 1)
     targets = audio_dest[:, 0].reshape(stops, AUD_DEV)
     half_stops = stops // MB_DEV
 
@@ -85,29 +97,22 @@
     seats = jnp.arange(stops * MB_DEV * CAP, dtype=jnp.int32)
     chosen = seats[:, None] == (holder * CAP + rank)[None, :]
     outgoing = jnp.dot(chosen.astype(BF16), audio, preferred_element_type=F32).astype(BF16)
-    outgoing, w_keys, w_queries = lax.optimization_barrier((outgoing, w_keyval[0], w_query[0]))
     slots = lax.all_to_all(outgoing.reshape(stops * MB_DEV, CAP, COLS), ("section", "y"), 0, 0, tiled=True)
     slots = pick(slots.reshape(MB_DEV, half_stops, 2, CAP, COLS), y, 0)
     slots = slots.transpose(0, 2, 1, 3).reshape(AUD_MB, 2 * COLS)
 
-    text = hidden.reshape(MB_DEV, TXT_MB, COLS)
-    gain_rows = jnp.broadcast_to(norm_gain, (16, COLS))
-
-    def batch(index):
-        return jnp.concatenate([pick(text, index, 0), gain_rows], 0)
-
-    written = in_order(batch(y), shift(batch(1 - y), "y", 1), y, 1)
-    features = GROUP * 2 * COLS
-    w_kv = w_keys.reshape(COLS, GROUP, 2 * HD)
-    kv_pieces = [pick(w_kv, (a + k) % GROUP, 1) for k in range(GROUP)]
-    kv_stack = jnp.stack([shift(piece, "za", k) if k else piece for k, piece in enumerate(kv_pieces)])
-    kv_own = jnp.stack([pick(kv_stack, (a - source) % GROUP, 0) for source in range(GROUP)])
-    both, kv_own = lax.optimization_barrier((jnp.concatenate([slots, written], 0), kv_own))
+    both = jnp.concatenate([slots, written], 0)
+    first_other = shift(parts[0], "y", 1)
+    both, group_own, first_other, w_kv = lax.optimization_barrier((both, group_own, first_other, w_keyval[0]))
     state = both[:MB_ROWS]
+    group_other = shift(jnp.stack(group_own[1:]), "y", 1)
+    w_kv = w_kv.reshape(COLS, GROUP, 2 * HD).transpose(1, 0, 2)
+    kv_own = lax.all_to_all(w_kv, "za", 0, 0, tiled=True)
+    both, kv_own = lax.optimization_barrier((both, kv_own))
     w_kv_rows = in_order(kv_own, shift(kv_own, "y", 1), y, 1).reshape(features, 2 * HD)
-    w_q = w_queries.reshape(GROUP, GROUP, 2 * COLS, HD)
-    rows_own = jnp.stack([pick(w_q, (b - j) % GROUP, 1).reshape(features, HD) for j in range(GROUP)])
-    rows_other = shift(rows_own, "y", 1)
+    group_other = [first_other] + [group_other[j] for j in range(GROUP - 1)]
+    w_group = [jnp.concatenate([mine, others], 1) for mine, others in zip(group_own, group_other)]
+    w_group = lax.optimization_barrier(w_group)
 
     seat_ids = jnp.arange(AUD_MB, dtype=jnp.int32)
     owner = y * (AUD_MB // CAP) + seat_ids // CAP
@@ -131,22 +136,20 @@
         if lap_step == 0:
             wide = lax.all_gather(both, "za", axis=1, tiled=True)
             wide, w_o = lax.optimization_barrier((wide, w_out[0]))
-            w_o_halves = (w_out[0], shift(w_o, "y", 1))
-            w_pair = lax.optimization_barrier(jnp.concatenate([rows_own, rows_other], 2))
+            w_o_pair = lax.optimization_barrier(jnp.concatenate([w_out[0], shift(w_o, "y", 1)], 1))
             gain_wide = wide[MB_ROWS : MB_ROWS + 1].astype(F32)
             wide = wide[:MB_ROWS].astype(F32)
         else:
             wide = lax.all_gather(state, "za", axis=1, tiled=True).astype(F32)
         scaled = (wide * gain_wide).astype(BF16)
         squares = jnp.sum(wide * wide, axis=1, keepdims=True)
+        queries = [jnp.dot(scaled, part, preferred_element_type=F32).astype(BF16) for part in w_group]
         key_values = jnp.dot(scaled, w_kv_rows, preferred_element_type=F32).astype(BF16)
-        payload = jnp.concatenate([scaled, key_values, split_float(squares)], 1)
-        gathered = [payload] + [shift(payload, "zb", j) for j in range(1, GROUP)]
-        total = sum(part[:, features:].astype(F32) for part in gathered)
-        queries = sum(
-            jnp.dot(part[:, :features], w_pair[j], preferred_element_type=F32) for j, part in enumerate(gathered)
-        )
-        total = jnp.concatenate([queries, total], 1)
+        shared = jnp.concatenate([key_values, split_float(squares)], 1)
+        message = jnp.stack([jnp.concatenate([part, shared], 1) for part in queries])
+        message = jnp.roll(message, b, axis=0)
+        arrived = lax.all_to_all(message, "zb", 0, 0, tiled=True)
+        total = jnp.sum(arrived.astype(F32), axis=0)
         inverse = lax.rsqrt(jnp.sum(total[:, 4 * HD :], axis=1, keepdims=True) / D + 1e-05)
         total = total[:, : 4 * HD] * inverse
         key_rows = rotate(total[:, 2 * HD : 3 * HD], cosine, sine).astype(BF16)
@@ -160,15 +163,19 @@
             probs = (weights / jnp.sum(weights, axis=-1, keepdims=True)).astype(BF16)
             heads.append(jnp.dot(probs, value_rows, preferred_element_type=F32).astype(BF16))
         attended = in_order(heads[0], heads[1], y, 1)
-        attended = lax.all_gather(attended, ("za", "zb"), axis=1, tiled=True)
-        projected = [jnp.dot(attended, half, preferred_element_type=F32) for half in w_o_halves]
+        if lap_step in (1, 2):
+            attended = lax.all_to_all(to_all(attended, GROUP * GROUP), ("za", "zb"), 0, 0, tiled=True)
+            attended = attended.transpose(1, 0, 2).reshape(MB_ROWS, GROUP * GROUP * 2 * HD)
+        else:
+            attended = lax.all_gather(attended, ("za", "zb"), axis=1, tiled=True)
+        projected = jnp.dot(attended, w_o_pair, preferred_element_type=F32)
         state_wide = state.astype(F32)
         if lap_step < STEPS - 1:
-            update = in_order(projected[0], projected[1], y, 1)
+            update = in_order(projected[:, :COLS], projected[:, COLS:], y, 1)
             state = shift((state_wide + update).astype(BF16), "section", 1)
     low, high = state_wide[:, :COLS], state_wide[:, COLS:]
-    own = (jnp.where(y == 0, low, high) + projected[0]).astype(BF16)
-    other = (jnp.where(y == 0, high, low) + projected[1]).astype(BF16)
+    own = (jnp.where(y == 0, low, high) + projected[:, :COLS]).astype(BF16)
+    other = (jnp.where(y == 0, high, low) + projected[:, COLS:]).astype(BF16)
     crossing = [(2 * i + j, 2 * ((i + 1) % stops) + 1 - j) for i in range(stops) for j in range(2)]
     own = shift(own, "section", 1)
     other = lax.ppermute(other, ("section", "y"), crossing)

time: 444 us -> 434 us (0.977)
  waiting for transfers between devices: 95.7 us -> 71.9 us
  blocking collectives: 171 us -> 182 us
  starting transfers between devices: 136 us -> 128 us
  other arithmetic: 12.6 us -> 18.8 us
  local copies, waits for them, and re-layouts: 7.7 us -> 13.1 us
    ppermute x23 -> x12, waiting for transfers between devices: 88 us -> 29.7 us  [shift(): lax.ppermute(block, axis, [(i, (i + distance) % count) for i in range(cou...]
    all_to_all x0 -> x2, blocking collectives: none -> 52.8 us  [local(): lax.all_to_all(to_all(attended, GROUP * GROUP), ('za', 'zb'), 0, 0, tiled...]
    all_gather x4 -> x2, blocking collectives: 97.4 us -> 55.1 us  [local(): attended = lax.all_gather(attended, ('za', 'zb'), axis=1, tiled=True)]
    all_to_all x0 -> x5, starting transfers between devices: none -> 35 us  [the longest x4 21.9 us: local(): arrived = lax.all_to_all(message, 'zb', 0, 0, tiled=True)]
    ppermute x23 -> x12, starting transfers between devices: 115 us -> 82 us  [shift(): lax.ppermute(block, axis, [(i, (i + distance) % count) for i in range(cou...]
    all_to_all x0 -> x5, waiting for transfers between devices: none -> 32.5 us  [the longest x4 21.4 us: local(): arrived = lax.all_to_all(message, 'zb', 0, 0, tiled=True)]
    ppermute x1, starting transfers between devices: 12.6 us -> 1.92 us  [local(): other = lax.ppermute(other, ('section', 'y'), crossing)]
    concatenate x6 -> x9, other arithmetic: 3.23 us -> 8.65 us  [the longest x4 4.64 us: local(): message = jnp.roll(message, b, axis=0)]
  transfers between devices with their start and end apart: 25 -> 19, of which waited for: 17 -> 14; matrix products, arithmetic and copies ran while one was open for 4% -> 4% of each run, Pallas kernels for 0% -> 0%
where the time goes in v3:
time: 434 us; the launch traced here: 432 us
  blocking collectives  182 us (42%)
  starting transfers between devices  128 us (29%)
  waiting for transfers between devices  71.9 us (17%)
  other arithmetic  18.8 us (4%)
  matrix products  16.7 us (4%)
  local copies, waits for them, and re-layouts  13.1 us (3%)
    ppermute x12, starting transfers between devices, shift(): lax.ppermute(block, axis, [(i, (i + distance) % count) for i in range(cou...  82 us
    all_gather x2, blocking collectives, local(): attended = lax.all_gather(attended, ('za', 'zb'), axis=1, tiled=True)  55.1 us
    all_to_all x2, blocking collectives, local(): lax.all_to_all(to_all(attended, GROUP * GROUP), ('za', 'zb'), 0, 0, tiled...  52.8 us
    all_gather x3, blocking collectives, local(): wide = lax.all_gather(state, 'za', axis=1, tiled=True).astype(F32)  49.1 us
    ppermute x12, waiting for transfers between devices, shift(): lax.ppermute(block, axis, [(i, (i + distance) % count) for i in range(cou...  29.7 us
    all_gather x1, blocking collectives, local(): wide = lax.all_gather(both, 'za', axis=1, tiled=True)  25.5 us
    all_to_all x4, starting transfers between devices, local(): arrived = lax.all_to_all(message, 'zb', 0, 0, tiled=True)  21.9 us
    all_to_all x4, waiting for transfers between devices, local(): arrived = lax.all_to_all(message, 'zb', 0, 0, tiled=True)  21.4 us
  transfers between devices with their start and end apart: 19, of which 14 were waited for; matrix products, arithmetic and copies ran while one was open for 4% of the time, Pallas kernels for 0%

profile of v3, /device:TPU:1, one launch (start us, length us, event | category | flops | bytes accessed | tf_op | source)
XLA Modules:
  0.0 432.1 jit_solution(5407715787492953446)
XLA Ops:
  24.8 9.2 %all-to-all-start = ((bf16[32,4,256]{2,1,0:T(4,128)(2,1)}), bf16[32,4,256]{2,1,0:T(4,128)(2,1)S(1)}, u32[]{:S(2)}, u32[]{:S(2)}) async-start(bf16[32,4,256]{2,1,0:T(4,128)(2,1)} %reshape.225), calls=%async_computation | async-start | bytes 131072 | tf_op jit(solution)/shard_map/all_to_all | solution.py:100
  35.0 6.2 %all-to-all-done = bf16[32,4,256]{2,1,0:T(4,128)(2,1)S(1)} async-done(((bf16[32,4,256]{2,1,0:T(4,128)(2,1)}), bf16[32,4,256]{2,1,0:T(4,128)(2,1)S(1)}, u32[]{:S(2)}, u32[]{:S(2)}) %all-to-all-start) | async-done | bytes 65568 | tf_op jit(solution)/shard_map/all_to_all | solution.py:100
  41.8 5.1 %collective-permute-done.2 = bf16[2048,128]{1,0:T(8,128)(2,1)S(1)} collective-permute-done((bf16[2048,128]{1,0:T(8,128)(2,1)}, bf16[2048,128]{1,0:T(8,128)(2,1)S(1)}, u32[]{:S(2)}, u32[]{:S(2)}) %collective-permute-start.2) | collective-permute-done | bytes 524320 | tf_op jit(solution)/shard_map/ppermute | solution.py:27
  52.7 13.1 %all-to-all-start.1 = ((bf16[4,256,256]{1,2,0:T(8,128)(2,1)}), bf16[4,256,256]{1,2,0:T(8,128)(2,1)S(1)}, u32[]{:S(2)}, u32[]{:S(2)}) async-start(bf16[4,256,256]{1,2,0:T(8,128)(2,1)} %bitcast.17), calls=%async_computation.1 | async-start | bytes 1048576 | tf_op jit(solution)/shard_map/all_to_all | solution.py:110
  71.5 11.1 %all-to-all-done.1 = bf16[4,256,256]{1,2,0:T(8,128)(2,1)S(1)} async-done(((bf16[4,256,256]{1,2,0:T(8,128)(2,1)}), bf16[4,256,256]{1,2,0:T(8,128)(2,1)S(1)}, u32[]{:S(2)}, u32[]{:S(2)}) %all-to-all-start.1) | async-done | bytes 524320 | tf_op jit(solution)/shard_map/all_to_all | solution.py:110
  82.5 25.5 %all_gather.18 = bf16[80,2048]{1,0:T(8,128)(2,1)S(1)} all-gather(bf16[80,512]{1,0:T(8,128)(2,1)} %maximum_maximum_fusion), channel_id=1, replica_groups=mesh['section'=16,'za'=4,'zb'=4,'y'=2] {'za'}, dimensions={1}, use_global_device_ids=true | all-gather | bytes 409600 | tf_op jit(solution)/shard_map/all_gather | solution.py:137
  115.5 6.6 %collective-permute-done.6 = bf16[4,256,256]{1,2,0:T(8,128)(2,1)S(1)} collective-permute-done((bf16[4,256,256]{1,2,0:T(8,128)(2,1)S(1)}, bf16[4,256,256]{1,2,0:T(8,128)(2,1)S(1)}, u32[]{:S(2)}, u32[]{:S(2)}) %collective-permute-start.6) | collective-permute-done | bytes 524320 | tf_op jit(solution)/shard_map/ppermute | solution.py:27
  127.1 7.4 %all-to-all-start.2 = ((bf16[4,64,640]{2,1,0:T(8,128)(2,1)}), bf16[4,64,640]{2,1,0:T(8,128)(2,1)S(1)}, u32[]{:S(2)}, u32[]{:S(2)}) async-start(bf16[4,64,640]{2,1,0:T(8,128)(2,1)} %fusion.40), calls=%async_computation.2 | async-start | bytes 655360 | tf_op jit(solution)/shard_map/all_to_all | solution.py:151
  142.0 29.2 %all_gather.19 = bf16[64,4096]{1,0:T(8,128)(2,1)S(1)} all-gather(bf16[64,256]{1,0:T(8,128)(2,1)S(1)} %pad_maximum_fusion.42), channel_id=1, replica_groups=mesh['section'=16,'za'=4,'zb'=4,'y'=2] {'za','zb'}, dimensions={1}, use_global_device_ids=true | all-gather | bytes 557056 | tf_op jit(solution)/shard_map/all_gather | solution.py:170
  171.2 9.2 %collective-permute-done.7 = bf16[4096,256]{1,0:T(8,128)(2,1)} collective-permute-done((bf16[4096,256]{1,0:T(8,128)(2,1)}, bf16[4096,256]{1,0:T(8,128)(2,1)}, u32[]{:S(2)}, u32[]{:S(2)}) %collective-permute-start.7) | collective-permute-done | bytes 2097184 | tf_op jit(solution)/shard_map/ppermute | solution.py:27
  184.3 10.1 %collective-permute-start.8 = (bf16[64,512]{1,0:T(8,128)(2,1)S(1)}, bf16[64,512]{1,0:T(8,128)(2,1)S(1)}, u32[]{:S(2)}, u32[]{:S(2)}) collective-permute-start(bf16[64,512]{1,0:T(8,128)(2,1)S(1)} %fusion.44), channel_id=1, source_target_pairs={{0,32},{32,64},{64,96},{96,128},{128,160},{160,192},{192,224},{224... | collective-permute-start | bytes 196616 | tf_op jit(solution)/shard_map/ppermute | solution.py:27
  196.3 17.3 %all_gather.20 = bf16[64,2048]{1,0:T(8,128)(2,1)S(1)} all-gather(bf16[64,512]{1,0:T(8,128)(2,1)S(1)} %collective-permute-done.8), channel_id=1, replica_groups=mesh['section'=16,'za'=4,'zb'=4,'y'=2] {'za'}, dimensions={1}, use_global_device_ids=true | all-gather | bytes 327680 | tf_op jit(solution)/shard_map/all_gather | solution.py:143
  216.6 5.5 %all-to-all-start.3 = ((bf16[4,64,640]{2,1,0:T(8,128)(2,1)}), bf16[4,64,640]{2,1,0:T(8,128)(2,1)S(1)}, u32[]{:S(2)}, u32[]{:S(2)}) async-start(bf16[4,64,640]{2,1,0:T(8,128)(2,1)} %fusion.33), calls=%async_computation.3 | async-start | bytes 655360 | tf_op jit(solution)/shard_map/all_to_all | solution.py:151
  222.1 6.1 %all-to-all-done.3 = bf16[4,64,640]{2,1,0:T(8,128)(2,1)S(1)} async-done(((bf16[4,64,640]{2,1,0:T(8,128)(2,1)}), bf16[4,64,640]{2,1,0:T(8,128)(2,1)S(1)}, u32[]{:S(2)}, u32[]{:S(2)}) %all-to-all-start.3) | async-done | bytes 327712 | tf_op jit(solution)/shard_map/all_to_all | solution.py:151
  229.7 27.8 %all_to_all.40 = bf16[16,64,256]{2,1,0:T(8,128)(2,1)S(1)} all-to-all(bf16[16,64,256]{2,1,0:T(8,128)(2,1)S(1)} %broadcast_in_dim.279), channel_id=1, replica_groups=mesh['section'=16,'za'=4,'zb'=4,'y'=2] {'za','zb'}, dimensions={0} | all-to-all | bytes 1048576 | tf_op jit(solution)/shard_map/all_to_all | solution.py:167
  258.5 13.7 %collective-permute-start.9 = (bf16[64,512]{1,0:T(8,128)(2,1)S(1)}, bf16[64,512]{1,0:T(8,128)(2,1)S(1)}, u32[]{:S(2)}, u32[]{:S(2)}) collective-permute-start(bf16[64,512]{1,0:T(8,128)(2,1)S(1)} %fusion.45), channel_id=1, source_target_pairs={{0,32},{32,64},{64,96},{96,128},{128,160},{160,192},{192,224},{224... | collective-permute-start | bytes 196616 | tf_op jit(solution)/shard_map/ppermute | solution.py:27
  274.1 15.9 %all_gather.21 = bf16[64,2048]{1,0:T(8,128)(2,1)S(1)} all-gather(bf16[64,512]{1,0:T(8,128)(2,1)S(1)} %collective-permute-done.9), channel_id=1, replica_groups=mesh['section'=16,'za'=4,'zb'=4,'y'=2] {'za'}, dimensions={1}, use_global_device_ids=true | all-gather | bytes 327680 | tf_op jit(solution)/shard_map/all_gather | solution.py:143
  297.2 6.1 %all-to-all-done.5 = bf16[4,64,640]{2,1,0:T(8,128)(2,1)S(1)} async-done(((bf16[4,64,640]{2,1,0:T(8,128)(2,1)}), bf16[4,64,640]{2,1,0:T(8,128)(2,1)S(1)}, u32[]{:S(2)}, u32[]{:S(2)}) %all-to-all-start.5) | async-done | bytes 327712 | tf_op jit(solution)/shard_map/all_to_all | solution.py:151
  304.7 25.0 %all_to_all.41 = bf16[16,64,256]{2,1,0:T(8,128)(2,1)S(1)} all-to-all(bf16[16,64,256]{2,1,0:T(8,128)(2,1)S(1)} %broadcast_in_dim.284), channel_id=1, replica_groups=mesh['section'=16,'za'=4,'zb'=4,'y'=2] {'za','zb'}, dimensions={0} | all-to-all | bytes 1048576 | tf_op jit(solution)/shard_map/all_to_all | solution.py:167
  330.7 16.9 %collective-permute-start.10 = (bf16[64,512]{1,0:T(8,128)(2,1)S(1)}, bf16[64,512]{1,0:T(8,128)(2,1)S(1)}, u32[]{:S(2)}, u32[]{:S(2)}) collective-permute-start(bf16[64,512]{1,0:T(8,128)(2,1)S(1)} %fusion.46), channel_id=1, source_target_pairs={{0,32},{32,64},{64,96},{96,128},{128,160},{160,192},{192,224},{224... | collective-permute-start | bytes 196616 | tf_op jit(solution)/shard_map/ppermute | solution.py:27
  348.9 15.8 %all_gather.22 = bf16[64,2048]{1,0:T(8,128)(2,1)S(1)} all-gather(bf16[64,512]{1,0:T(8,128)(2,1)S(1)} %collective-permute-done.10), channel_id=1, replica_groups=mesh['section'=16,'za'=4,'zb'=4,'y'=2] {'za'}, dimensions={1}, use_global_device_ids=true | all-gather | bytes 327680 | tf_op jit(solution)/shard_map/all_gather | solution.py:143
  372.5 6.1 %all-to-all-done.7 = bf16[4,64,640]{2,1,0:T(8,128)(2,1)S(1)} async-done(((bf16[4,64,640]{2,1,0:T(8,128)(2,1)}), bf16[4,64,640]{2,1,0:T(8,128)(2,1)S(1)}, u32[]{:S(2)}, u32[]{:S(2)}) %all-to-all-start.7) | async-done | bytes 327712 | tf_op jit(solution)/shard_map/all_to_all | solution.py:151
  380.0 25.9 %all_gather.23 = bf16[64,4096]{1,0:T(8,128)(2,1)S(1)} all-gather(bf16[64,256]{1,0:T(8,128)(2,1)S(1)} %pad_maximum_fusion.45), channel_id=1, replica_groups=mesh['section'=16,'za'=4,'zb'=4,'y'=2] {'za','zb'}, dimensions={1}, use_global_device_ids=true | all-gather | bytes 557056 | tf_op jit(solution)/shard_map/all_gather | solution.py:170
  408.9 17.0 %collective-permute-start.11 = (bf16[64,256]{1,0:T(8,128)(2,1)S(1)}, bf16[64,256]{1,0:T(8,128)(2,1)S(1)}, u32[]{:S(2)}, u32[]{:S(2)}) collective-permute-start(bf16[64,256]{1,0:T(8,128)(2,1)S(1)} %get-tuple-element.53), channel_id=1, source_target_pairs={{0,32},{32,64},{64,96},{96,128},{128,160},{160,192},{192,224},{224... | collective-permute-start | bytes 98312 | tf_op jit(solution)/shard_map/ppermute | solution.py:27
  (232 shorter events, 99.1 us)
Async XLA Ops:
  1.5 33.5 %collective-permute-start = (bf16[48,256]{1,0:T(8,128)(2,1)S(1)}, bf16[48,256]{1,0:T(8,128)(2,1)S(1)}, u32[]{:S(2)}, u32[]{:S(2)}) collective-permute-start(bf16[48,256]{1,0:T(8,128)(2,1)S(1)} %pad_maximum_fusion.40), channel_id=1, source_target_pairs={{0,1},{1,0},{2,3},{3,2},{4,5},{5,4},{6,7},{7,6},{8,9},{9,8},{10,11... | collective-permute-start | bytes 73736 | tf_op jit(solution)/shard_map/ppermute | solution.py:27
  8.4 38.6 %collective-permute-start.2 = (bf16[2048,128]{1,0:T(8,128)(2,1)}, bf16[2048,128]{1,0:T(8,128)(2,1)S(1)}, u32[]{:S(2)}, u32[]{:S(2)}) collective-permute-start(bf16[2048,128]{1,0:T(8,128)(2,1)} %bitcast.12), channel_id=1, source_target_pairs={{0,4},{2,6},{4,0},{6,2},{1,5},{3,7},{5,1},{7,3},{8,12},{10,14},{12... | collective-permute-start | bytes 1572872 | tf_op jit(solution)/shard_map/ppermute | solution.py:27
  13.3 33.7 %collective-permute-start.3 = (bf16[2048,128]{1,0:T(8,128)(2,1)}, bf16[2048,128]{1,0:T(8,128)(2,1)S(1)}, u32[]{:S(2)}, u32[]{:S(2)}) collective-permute-start(bf16[2048,128]{1,0:T(8,128)(2,1)} %bitcast.13), channel_id=1, source_target_pairs={{0,2},{2,4},{4,6},{6,0},{1,3},{3,5},{5,7},{7,1},{8,10},{10,12},{12... | collective-permute-start | bytes 1572872 | tf_op jit(solution)/shard_map/ppermute | solution.py:27
  16.9 34.9 %collective-permute-start.1 = (bf16[2048,128]{1,0:T(8,128)(2,1)}, bf16[2048,128]{1,0:T(8,128)(2,1)S(1)}, u32[]{:S(2)}, u32[]{:S(2)}) collective-permute-start(bf16[2048,128]{1,0:T(8,128)(2,1)} %bitcast.11), channel_id=1, source_target_pairs={{0,6},{2,0},{4,2},{6,4},{1,7},{3,1},{5,3},{7,5},{8,14},{10,8},{12,... | collective-permute-start | bytes 1572872 | tf_op jit(solution)/shard_map/ppermute | solution.py:27
  20.4 31.4 %collective-permute-start.4 = (bf16[2048,128]{1,0:T(8,128)(2,1)S(1)}, bf16[2048,128]{1,0:T(8,128)(2,1)S(1)}, u32[]{:S(2)}, u32[]{:S(2)}) collective-permute-start(bf16[2048,128]{1,0:T(8,128)(2,1)S(1)} %bitcast.151), channel_id=1, source_target_pairs={{0,1},{1,0},{2,3},{3,2},{4,5},{5,4},{6,7},{7,6},{8,9},{9,8},{10,11... | collective-permute-start | bytes 1572872 | tf_op jit(solution)/shard_map/ppermute | solution.py:27
  24.8 16.4 %all-to-all-start = ((bf16[32,4,256]{2,1,0:T(4,128)(2,1)}), bf16[32,4,256]{2,1,0:T(4,128)(2,1)S(1)}, u32[]{:S(2)}, u32[]{:S(2)}) async-start(bf16[32,4,256]{2,1,0:T(4,128)(2,1)} %reshape.225), calls=%async_computation | async-start | bytes 131072 | tf_op jit(solution)/shard_map/all_to_all | solution.py:100
  52.7 29.9 %all-to-all-start.1 = ((bf16[4,256,256]{1,2,0:T(8,128)(2,1)}), bf16[4,256,256]{1,2,0:T(8,128)(2,1)S(1)}, u32[]{:S(2)}, u32[]{:S(2)}) async-start(bf16[4,256,256]{1,2,0:T(8,128)(2,1)} %bitcast.17), calls=%async_computation.1 | async-start | bytes 1048576 | tf_op jit(solution)/shard_map/all_to_all | solution.py:110
  67.1 43.2 %collective-permute-start.5 = (bf16[3,2048,128]{2,1,0:T(8,128)(2,1)}, bf16[3,2048,128]{2,1,0:T(8,128)(2,1)}, u32[]{:S(2)}, u32[]{:S(2)}) collective-permute-start(bf16[3,2048,128]{2,1,0:T(8,128)(2,1)} %pad_maximum_fusion.1), channel_id=1, source_target_pairs={{0,1},{1,0},{2,3},{3,2},{4,5},{5,4},{6,7},{7,6},{8,9},{9,8},{10,11... | collective-permute-start | bytes 4718600 | tf_op jit(solution)/shard_map/ppermute | solution.py:27
  108.0 14.1 %collective-permute-start.6 = (bf16[4,256,256]{1,2,0:T(8,128)(2,1)S(1)}, bf16[4,256,256]{1,2,0:T(8,128)(2,1)S(1)}, u32[]{:S(2)}, u32[]{:S(2)}) collective-permute-start(bf16[4,256,256]{1,2,0:T(8,128)(2,1)S(1)} %all-to-all-done.1), channel_id=1, source_target_pairs={{0,1},{1,0},{2,3},{3,2},{4,5},{5,4},{6,7},{7,6},{8,9},{9,8},{10,11... | collective-permute-start | bytes 1572872 | tf_op jit(solution)/shard_map/ppermute | solution.py:27
  127.1 13.6 %all-to-all-start.2 = ((bf16[4,64,640]{2,1,0:T(8,128)(2,1)}), bf16[4,64,640]{2,1,0:T(8,128)(2,1)S(1)}, u32[]{:S(2)}, u32[]{:S(2)}) async-start(bf16[4,64,640]{2,1,0:T(8,128)(2,1)} %fusion.40), calls=%async_computation.2 | async-start | bytes 655360 | tf_op jit(solution)/shard_map/all_to_all | solution.py:151
  135.6 44.8 %collective-permute-start.7 = (bf16[4096,256]{1,0:T(8,128)(2,1)}, bf16[4096,256]{1,0:T(8,128)(2,1)}, u32[]{:S(2)}, u32[]{:S(2)}) collective-permute-start(bf16[4096,256]{1,0:T(8,128)(2,1)} %bitcast.146), channel_id=1, source_target_pairs={{0,1},{1,0},{2,3},{3,2},{4,5},{5,4},{6,7},{7,6},{8,9},{9,8},{10,11... | collective-permute-start | bytes 6291464 | tf_op jit(solution)/shard_map/ppermute | solution.py:27
  140.6 39.7 %copy-start.12 = (bf16[1,4096,256]{2,1,0:T(8,128)(2,1)S(1)}, bf16[1,4096,256]{2,1,0:T(8,128)(2,1)}, u32[]{:S(2)}) copy-start(bf16[1,4096,256]{2,1,0:T(8,128)(2,1)} %param.17) | copy-start | bytes 6291460
  184.3 11.4 %collective-permute-start.8 = (bf16[64,512]{1,0:T(8,128)(2,1)S(1)}, bf16[64,512]{1,0:T(8,128)(2,1)S(1)}, u32[]{:S(2)}, u32[]{:S(2)}) collective-permute-start(bf16[64,512]{1,0:T(8,128)(2,1)S(1)} %fusion.44), channel_id=1, source_target_pairs={{0,32},{32,64},{64,96},{96,128},{128,160},{160,192},{192,224},{224... | collective-permute-start | bytes 196616 | tf_op jit(solution)/shard_map/ppermute | solution.py:27
  216.6 11.7 %all-to-all-start.3 = ((bf16[4,64,640]{2,1,0:T(8,128)(2,1)}), bf16[4,64,640]{2,1,0:T(8,128)(2,1)S(1)}, u32[]{:S(2)}, u32[]{:S(2)}) async-start(bf16[4,64,640]{2,1,0:T(8,128)(2,1)} %fusion.33), calls=%async_computation.3 | async-start | bytes 655360 | tf_op jit(solution)/shard_map/all_to_all | solution.py:151
  258.4 32.1 %copy-start.10 = (bf16[2048,256]{1,0:T(8,128)(2,1)S(1)}, bf16[2048,256]{1,0:T(8,128)(2,1)}, u32[]{:S(2)}) copy-start(bf16[2048,256]{1,0:T(8,128)(2,1)} %copy-done.8) | copy-start | bytes 3145732
  258.4 32.4 %copy-start.6 = (bf16[2048,256]{1,0:T(8,128)(2,1)S(1)}, bf16[2048,256]{1,0:T(8,128)(2,1)}, u32[]{:S(2)}) copy-start(bf16[2048,256]{1,0:T(8,128)(2,1)} %copy-done.4) | copy-start | bytes 3145732
  258.5 15.0 %collective-permute-start.9 = (bf16[64,512]{1,0:T(8,128)(2,1)S(1)}, bf16[64,512]{1,0:T(8,128)(2,1)S(1)}, u32[]{:S(2)}, u32[]{:S(2)}) collective-permute-start(bf16[64,512]{1,0:T(8,128)(2,1)S(1)} %fusion.45), channel_id=1, source_target_pairs={{0,32},{32,64},{64,96},{96,128},{128,160},{160,192},{192,224},{224... | collective-permute-start | bytes 196616 | tf_op jit(solution)/shard_map/ppermute | solution.py:27
  293.0 10.3 %all-to-all-start.5 = ((bf16[4,64,640]{2,1,0:T(8,128)(2,1)}), bf16[4,64,640]{2,1,0:T(8,128)(2,1)S(1)}, u32[]{:S(2)}, u32[]{:S(2)}) async-start(bf16[4,64,640]{2,1,0:T(8,128)(2,1)} %fusion.26), calls=%async_computation.5 | async-start | bytes 655360 | tf_op jit(solution)/shard_map/all_to_all | solution.py:151
  330.6 34.5 %copy-start.11 = (bf16[2048,256]{1,0:T(8,128)(2,1)S(1)}, bf16[2048,256]{1,0:T(8,128)(2,1)}, u32[]{:S(2)}) copy-start(bf16[2048,256]{1,0:T(8,128)(2,1)} %copy-done.8) | copy-start | bytes 3145732
  330.6 34.8 %copy-start.7 = (bf16[2048,256]{1,0:T(8,128)(2,1)S(1)}, bf16[2048,256]{1,0:T(8,128)(2,1)}, u32[]{:S(2)}) copy-start(bf16[2048,256]{1,0:T(8,128)(2,1)} %copy-done.4) | copy-start | bytes 3145732
  330.7 18.3 %collective-permute-start.10 = (bf16[64,512]{1,0:T(8,128)(2,1)S(1)}, bf16[64,512]{1,0:T(8,128)(2,1)S(1)}, u32[]{:S(2)}, u32[]{:S(2)}) collective-permute-start(bf16[64,512]{1,0:T(8,128)(2,1)S(1)} %fusion.46), channel_id=1, source_target_pairs={{0,32},{32,64},{64,96},{96,128},{128,160},{160,192},{192,224},{224... | collective-permute-start | bytes 196616 | tf_op jit(solution)/shard_map/ppermute | solution.py:27
  367.7 10.9 %all-to-all-start.7 = ((bf16[4,64,640]{2,1,0:T(8,128)(2,1)}), bf16[4,64,640]{2,1,0:T(8,128)(2,1)S(1)}, u32[]{:S(2)}, u32[]{:S(2)}) async-start(bf16[4,64,640]{2,1,0:T(8,128)(2,1)} %fusion.19), calls=%async_computation.7 | async-start | bytes 655360 | tf_op jit(solution)/shard_map/all_to_all | solution.py:151
  408.9 19.0 %collective-permute-start.11 = (bf16[64,256]{1,0:T(8,128)(2,1)S(1)}, bf16[64,256]{1,0:T(8,128)(2,1)S(1)}, u32[]{:S(2)}, u32[]{:S(2)}) collective-permute-start(bf16[64,256]{1,0:T(8,128)(2,1)S(1)} %get-tuple-element.53), channel_id=1, source_target_pairs={{0,32},{32,64},{64,96},{96,128},{128,160},{160,192},{192,224},{224... | collective-permute-start | bytes 98312 | tf_op jit(solution)/shard_map/ppermute | solution.py:27
  425.9 5.5 %collective-permute-start.12 = (bf16[64,256]{1,0:T(8,128)(2,1)S(1)}, bf16[64,256]{1,0:T(8,128)(2,1)S(1)}, u32[]{:S(2)}, u32[]{:S(2)}) collective-permute-start(bf16[64,256]{1,0:T(8,128)(2,1)S(1)} %get-tuple-element.54), channel_id=1, source_target_pairs={{0,33},{1,32},{32,65},{33,64},{64,97},{65,96},{96,129},{97,128},{1... | collective-permute-start | bytes 98312 | tf_op jit(solution)/shard_map/ppermute | solution.py:181
  (26 other events, 245.3 us)

commit v4 on v3

--- a/solution.py
+++ b/solution.py
@@ -105,12 +105,16 @@
     first_other = shift(parts[0], "y", 1)
     both, group_own, first_other, w_kv = lax.optimization_barrier((both, group_own, first_other, w_keyval[0]))
     state = both[:MB_ROWS]
-    group_other = shift(jnp.stack(group_own[1:]), "y", 1)
+    group_other = shift(jnp.stack(group_own[1:3]), "y", 1)
     w_kv = w_kv.reshape(COLS, GROUP, 2 * HD).transpose(1, 0, 2)
     kv_own = lax.all_to_all(w_kv, "za", 0, 0, tiled=True)
     both, kv_own = lax.optimization_barrier((both, kv_own))
-    w_kv_rows = in_order(kv_own, shift(kv_own, "y", 1), y, 1).reshape(features, 2 * HD)
-    group_other = [first_other] + [group_other[j] for j in range(GROUP - 1)]
+    kv_flat = kv_own.reshape(GROUP * COLS, 2 * HD)
+    kv_flat = jnp.concatenate([kv_flat[:, :HD], kv_flat[:, HD:]], 0)
+    last = shift(jnp.stack([group_own[3], kv_flat]), "y", 1)
+    kv_other = jnp.concatenate([last[1, : GROUP * COLS], last[1, GROUP * COLS :]], 1).reshape(kv_own.shape)
+    w_kv_rows = in_order(kv_own, kv_other, y, 1).reshape(features, 2 * HD)
+    group_other = [first_other, group_other[0], group_other[1], last[0]]
     w_group = [jnp.concatenate([mine, others], 1) for mine, others in zip(group_own, group_other)]
     w_group = lax.optimization_barrier(w_group)
 

time: 434 us -> 440 us (1.014)
  blocking collectives: 182 us -> 166 us
  starting transfers between devices: 128 us -> 144 us
  waiting for transfers between devices: 71.9 us -> 77.1 us
    all_to_all x4, starting transfers between devices: 21.9 us -> 35.4 us  [local(): arrived = lax.all_to_all(message, 'zb', 0, 0, tiled=True)]
    all_gather x2, blocking collectives: 55.1 us -> 46.7 us  [local(): attended = lax.all_gather(attended, ('za', 'zb'), axis=1, tiled=True)]
    ppermute x12, waiting for transfers between devices: 29.7 us -> 36.2 us  [shift(): lax.ppermute(block, axis, [(i, (i + distance) % count) for i in range(cou...]
    all_to_all x1, waiting for transfers between devices: 11.1 us -> 4.81 us  [local(): kv_own = lax.all_to_all(w_kv, 'za', 0, 0, tiled=True)]
    all_gather x1, blocking collectives: 25.5 us -> 20.2 us  [local(): wide = lax.all_gather(both, 'za', axis=1, tiled=True)]
    all_to_all x4, waiting for transfers between devices: 21.4 us -> 26.6 us  [local(): arrived = lax.all_to_all(message, 'zb', 0, 0, tiled=True)]
  transfers between devices with their start and end apart: 19 -> 19, of which waited for: 14 -> 14; matrix products, arithmetic and copies ran while one was open for 4% -> 3% of each run, Pallas kernels for 0% -> 0%
where the time goes in v4:
time: 440 us; the launch traced here: 439 us
  blocking collectives  166 us (38%)
  starting transfers between devices  144 us (33%)
  waiting for transfers between devices  77.1 us (18%)
  other arithmetic  19.6 us (4%)
  matrix products  16.7 us (4%)
  local copies, waits for them, and re-layouts  14 us (3%)
    ppermute x12, starting transfers between devices, shift(): lax.ppermute(block, axis, [(i, (i + distance) % count) for i in range(cou...  84.6 us
    all_to_all x2, blocking collectives, local(): lax.all_to_all(to_all(attended, GROUP * GROUP), ('za', 'zb'), 0, 0, tiled...  50.5 us
    all_gather x3, blocking collectives, local(): wide = lax.all_gather(state, 'za', axis=1, tiled=True).astype(F32)  48.5 us
    all_gather x2, blocking collectives, local(): attended = lax.all_gather(attended, ('za', 'zb'), axis=1, tiled=True)  46.7 us
    ppermute x12, waiting for transfers between devices, shift(): lax.ppermute(block, axis, [(i, (i + distance) % count) for i in range(cou...  36.2 us
    all_to_all x4, starting transfers between devices, local(): arrived = lax.all_to_all(message, 'zb', 0, 0, tiled=True)  35.4 us
    all_to_all x4, waiting for transfers between devices, local(): arrived = lax.all_to_all(message, 'zb', 0, 0, tiled=True)  26.6 us
    all_gather x1, blocking collectives, local(): wide = lax.all_gather(both, 'za', axis=1, tiled=True)  20.2 us
  transfers between devices with their start and end apart: 19, of which 14 were waited for; matrix products, arithmetic and copies ran while one was open for 3% of the time, Pallas kernels for 0%

profile of v4, /device:TPU:1, one launch (start us, length us, event | category | flops | bytes accessed | tf_op | source)
XLA Modules:
  0.0 438.7 jit_solution(21602150288507577)
XLA Ops:
  24.8 9.2 %all-to-all-start = ((bf16[32,4,256]{2,1,0:T(4,128)(2,1)}), bf16[32,4,256]{2,1,0:T(4,128)(2,1)S(1)}, u32[]{:S(2)}, u32[]{:S(2)}) async-start(bf16[32,4,256]{2,1,0:T(4,128)(2,1)} %reshape.233), calls=%async_computation | async-start | bytes 131072 | tf_op jit(solution)/shard_map/all_to_all | solution.py:100
  35.0 6.1 %all-to-all-done = bf16[32,4,256]{2,1,0:T(4,128)(2,1)S(1)} async-done(((bf16[32,4,256]{2,1,0:T(4,128)(2,1)}), bf16[32,4,256]{2,1,0:T(4,128)(2,1)S(1)}, u32[]{:S(2)}, u32[]{:S(2)}) %all-to-all-start) | async-done | bytes 65568 | tf_op jit(solution)/shard_map/all_to_all | solution.py:100
  41.8 5.1 %collective-permute-done.2 = bf16[2048,128]{1,0:T(8,128)(2,1)S(1)} collective-permute-done((bf16[2048,128]{1,0:T(8,128)(2,1)}, bf16[2048,128]{1,0:T(8,128)(2,1)S(1)}, u32[]{:S(2)}, u32[]{:S(2)}) %collective-permute-start.2) | collective-permute-done | bytes 524320 | tf_op jit(solution)/shard_map/ppermute | solution.py:27
  54.9 13.3 %all-to-all-start.1 = ((bf16[4,256,256]{1,2,0:T(8,128)(2,1)}), bf16[4,256,256]{1,2,0:T(8,128)(2,1)S(1)}, u32[]{:S(2)}, u32[]{:S(2)}) async-start(bf16[4,256,256]{1,2,0:T(8,128)(2,1)} %bitcast.17), calls=%async_computation.1 | async-start | bytes 1048576 | tf_op jit(solution)/shard_map/all_to_all | solution.py:110
  69.5 7.8 %collective-permute-done.5 = bf16[2,2048,128]{2,1,0:T(8,128)(2,1)} collective-permute-done((bf16[2,2048,128]{2,1,0:T(8,128)(2,1)}, bf16[2,2048,128]{2,1,0:T(8,128)(2,1)}, u32[]{:S(2)}, u32[]{:S(2)}) %collective-permute-start.5) | collective-permute-done | bytes 1048608 | tf_op jit(solution)/shard_map/ppermute | solution.py:27
  88.6 20.2 %all_gather.18 = bf16[80,2048]{1,0:T(8,128)(2,1)S(1)} all-gather(bf16[80,512]{1,0:T(8,128)(2,1)S(1)} %copy-done.17), channel_id=1, replica_groups=mesh['section'=16,'za'=4,'zb'=4,'y'=2] {'za'}, dimensions={1}, use_global_device_ids=true | all-gather | bytes 409600 | tf_op jit(solution)/shard_map/all_gather | solution.py:141
  118.9 19.9 %all-to-all-start.2 = ((bf16[4,64,640]{2,1,0:T(8,128)(2,1)}), bf16[4,64,640]{2,1,0:T(8,128)(2,1)S(1)}, u32[]{:S(2)}, u32[]{:S(2)}) async-start(bf16[4,64,640]{2,1,0:T(8,128)(2,1)} %fusion.40), calls=%async_computation.2 | async-start | bytes 655360 | tf_op jit(solution)/shard_map/all_to_all | solution.py:155
  149.2 23.8 %all_gather.19 = bf16[64,4096]{1,0:T(8,128)(2,1)S(1)} all-gather(bf16[64,256]{1,0:T(8,128)(2,1)S(1)} %pad_maximum_fusion.44), channel_id=1, replica_groups=mesh['section'=16,'za'=4,'zb'=4,'y'=2] {'za','zb'}, dimensions={1}, use_global_device_ids=true | all-gather | bytes 557056 | tf_op jit(solution)/shard_map/all_gather | solution.py:174
  173.0 14.5 %collective-permute-done.7 = bf16[4096,256]{1,0:T(8,128)(2,1)} collective-permute-done((bf16[4096,256]{1,0:T(8,128)(2,1)}, bf16[4096,256]{1,0:T(8,128)(2,1)}, u32[]{:S(2)}, u32[]{:S(2)}) %collective-permute-start.7) | collective-permute-done | bytes 2097184 | tf_op jit(solution)/shard_map/ppermute | solution.py:27
  191.4 7.6 %collective-permute-start.8 = (bf16[64,512]{1,0:T(8,128)(2,1)S(1)}, bf16[64,512]{1,0:T(8,128)(2,1)S(1)}, u32[]{:S(2)}, u32[]{:S(2)}) collective-permute-start(bf16[64,512]{1,0:T(8,128)(2,1)S(1)} %fusion.44), channel_id=1, source_target_pairs={{0,32},{32,64},{64,96},{96,128},{128,160},{160,192},{192,224},{224... | collective-permute-start | bytes 196616 | tf_op jit(solution)/shard_map/ppermute | solution.py:27
  200.9 15.7 %all_gather.20 = bf16[64,2048]{1,0:T(8,128)(2,1)S(1)} all-gather(bf16[64,512]{1,0:T(8,128)(2,1)S(1)} %collective-permute-done.8), channel_id=1, replica_groups=mesh['section'=16,'za'=4,'zb'=4,'y'=2] {'za'}, dimensions={1}, use_global_device_ids=true | all-gather | bytes 327680 | tf_op jit(solution)/shard_map/all_gather | solution.py:147
  219.6 6.2 %all-to-all-start.3 = ((bf16[4,64,640]{2,1,0:T(8,128)(2,1)}), bf16[4,64,640]{2,1,0:T(8,128)(2,1)S(1)}, u32[]{:S(2)}, u32[]{:S(2)}) async-start(bf16[4,64,640]{2,1,0:T(8,128)(2,1)} %fusion.33), calls=%async_computation.3 | async-start | bytes 655360 | tf_op jit(solution)/shard_map/all_to_all | solution.py:155
  225.8 6.1 %all-to-all-done.3 = bf16[4,64,640]{2,1,0:T(8,128)(2,1)S(1)} async-done(((bf16[4,64,640]{2,1,0:T(8,128)(2,1)}), bf16[4,64,640]{2,1,0:T(8,128)(2,1)S(1)}, u32[]{:S(2)}, u32[]{:S(2)}) %all-to-all-start.3) | async-done | bytes 327712 | tf_op jit(solution)/shard_map/all_to_all | solution.py:155
  233.4 24.9 %all_to_all.40 = bf16[16,64,256]{2,1,0:T(8,128)(2,1)S(1)} all-to-all(bf16[16,64,256]{2,1,0:T(8,128)(2,1)S(1)} %broadcast_in_dim.279), channel_id=1, replica_groups=mesh['section'=16,'za'=4,'zb'=4,'y'=2] {'za','zb'}, dimensions={0} | all-to-all | bytes 1048576 | tf_op jit(solution)/shard_map/all_to_all | solution.py:171
  259.3 13.3 %collective-permute-start.9 = (bf16[64,512]{1,0:T(8,128)(2,1)S(1)}, bf16[64,512]{1,0:T(8,128)(2,1)S(1)}, u32[]{:S(2)}, u32[]{:S(2)}) collective-permute-start(bf16[64,512]{1,0:T(8,128)(2,1)S(1)} %fusion.45), channel_id=1, source_target_pairs={{0,32},{32,64},{64,96},{96,128},{128,160},{160,192},{192,224},{224... | collective-permute-start | bytes 196616 | tf_op jit(solution)/shard_map/ppermute | solution.py:27
  274.5 16.3 %all_gather.21 = bf16[64,2048]{1,0:T(8,128)(2,1)S(1)} all-gather(bf16[64,512]{1,0:T(8,128)(2,1)S(1)} %collective-permute-done.9), channel_id=1, replica_groups=mesh['section'=16,'za'=4,'zb'=4,'y'=2] {'za'}, dimensions={1}, use_global_device_ids=true | all-gather | bytes 327680 | tf_op jit(solution)/shard_map/all_gather | solution.py:147
  297.9 6.1 %all-to-all-done.5 = bf16[4,64,640]{2,1,0:T(8,128)(2,1)S(1)} async-done(((bf16[4,64,640]{2,1,0:T(8,128)(2,1)}), bf16[4,64,640]{2,1,0:T(8,128)(2,1)S(1)}, u32[]{:S(2)}, u32[]{:S(2)}) %all-to-all-start.5) | async-done | bytes 327712 | tf_op jit(solution)/shard_map/all_to_all | solution.py:155
  305.4 25.6 %all_to_all.41 = bf16[16,64,256]{2,1,0:T(8,128)(2,1)S(1)} all-to-all(bf16[16,64,256]{2,1,0:T(8,128)(2,1)S(1)} %broadcast_in_dim.284), channel_id=1, replica_groups=mesh['section'=16,'za'=4,'zb'=4,'y'=2] {'za','zb'}, dimensions={0} | all-to-all | bytes 1048576 | tf_op jit(solution)/shard_map/all_to_all | solution.py:171
  332.0 23.6 %collective-permute-start.10 = (bf16[64,512]{1,0:T(8,128)(2,1)S(1)}, bf16[64,512]{1,0:T(8,128)(2,1)S(1)}, u32[]{:S(2)}, u32[]{:S(2)}) collective-permute-start(bf16[64,512]{1,0:T(8,128)(2,1)S(1)} %fusion.46), channel_id=1, source_target_pairs={{0,32},{32,64},{64,96},{96,128},{128,160},{160,192},{192,224},{224... | collective-permute-start | bytes 196616 | tf_op jit(solution)/shard_map/ppermute | solution.py:27
  356.9 16.4 %all_gather.22 = bf16[64,2048]{1,0:T(8,128)(2,1)S(1)} all-gather(bf16[64,512]{1,0:T(8,128)(2,1)S(1)} %collective-permute-done.10), channel_id=1, replica_groups=mesh['section'=16,'za'=4,'zb'=4,'y'=2] {'za'}, dimensions={1}, use_global_device_ids=true | all-gather | bytes 327680 | tf_op jit(solution)/shard_map/all_gather | solution.py:147
  376.3 5.2 %all-to-all-start.7 = ((bf16[4,64,640]{2,1,0:T(8,128)(2,1)}), bf16[4,64,640]{2,1,0:T(8,128)(2,1)S(1)}, u32[]{:S(2)}, u32[]{:S(2)}) async-start(bf16[4,64,640]{2,1,0:T(8,128)(2,1)} %fusion.19), calls=%async_computation.7 | async-start | bytes 655360 | tf_op jit(solution)/shard_map/all_to_all | solution.py:155
  381.5 10.4 %all-to-all-done.7 = bf16[4,64,640]{2,1,0:T(8,128)(2,1)S(1)} async-done(((bf16[4,64,640]{2,1,0:T(8,128)(2,1)}), bf16[4,64,640]{2,1,0:T(8,128)(2,1)S(1)}, u32[]{:S(2)}, u32[]{:S(2)}) %all-to-all-start.7) | async-done | bytes 327712 | tf_op jit(solution)/shard_map/all_to_all | solution.py:155
  393.2 22.9 %all_gather.23 = bf16[64,4096]{1,0:T(8,128)(2,1)S(1)} all-gather(bf16[64,256]{1,0:T(8,128)(2,1)S(1)} %pad_maximum_fusion.47), channel_id=1, replica_groups=mesh['section'=16,'za'=4,'zb'=4,'y'=2] {'za','zb'}, dimensions={1}, use_global_device_ids=true | all-gather | bytes 557056 | tf_op jit(solution)/shard_map/all_gather | solution.py:174
  419.2 13.6 %collective-permute-start.11 = (bf16[64,256]{1,0:T(8,128)(2,1)S(1)}, bf16[64,256]{1,0:T(8,128)(2,1)S(1)}, u32[]{:S(2)}, u32[]{:S(2)}) collective-permute-start(bf16[64,256]{1,0:T(8,128)(2,1)S(1)} %get-tuple-element.56), channel_id=1, source_target_pairs={{0,32},{32,64},{64,96},{96,128},{128,160},{160,192},{192,224},{224... | collective-permute-start | bytes 98312 | tf_op jit(solution)/shard_map/ppermute | solution.py:27
  (232 shorter events, 103.5 us)
Async XLA Ops:
  1.5 33.5 %collective-permute-start = (bf16[48,256]{1,0:T(8,128)(2,1)S(1)}, bf16[48,256]{1,0:T(8,128)(2,1)S(1)}, u32[]{:S(2)}, u32[]{:S(2)}) collective-permute-start(bf16[48,256]{1,0:T(8,128)(2,1)S(1)} %pad_maximum_fusion.42), channel_id=1, source_target_pairs={{0,1},{1,0},{2,3},{3,2},{4,5},{5,4},{6,7},{7,6},{8,9},{9,8},{10,11... | collective-permute-start | bytes 73736 | tf_op jit(solution)/shard_map/ppermute | solution.py:27
  8.4 38.6 %collective-permute-start.2 = (bf16[2048,128]{1,0:T(8,128)(2,1)}, bf16[2048,128]{1,0:T(8,128)(2,1)S(1)}, u32[]{:S(2)}, u32[]{:S(2)}) collective-permute-start(bf16[2048,128]{1,0:T(8,128)(2,1)} %bitcast.12), channel_id=1, source_target_pairs={{0,4},{2,6},{4,0},{6,2},{1,5},{3,7},{5,1},{7,3},{8,12},{10,14},{12... | collective-permute-start | bytes 1572872 | tf_op jit(solution)/shard_map/ppermute | solution.py:27
  13.3 33.7 %collective-permute-start.3 = (bf16[2048,128]{1,0:T(8,128)(2,1)}, bf16[2048,128]{1,0:T(8,128)(2,1)S(1)}, u32[]{:S(2)}, u32[]{:S(2)}) collective-permute-start(bf16[2048,128]{1,0:T(8,128)(2,1)} %bitcast.13), channel_id=1, source_target_pairs={{0,2},{2,4},{4,6},{6,0},{1,3},{3,5},{5,7},{7,1},{8,10},{10,12},{12... | collective-permute-start | bytes 1572872 | tf_op jit(solution)/shard_map/ppermute | solution.py:27
  16.9 34.9 %collective-permute-start.1 = (bf16[2048,128]{1,0:T(8,128)(2,1)}, bf16[2048,128]{1,0:T(8,128)(2,1)S(1)}, u32[]{:S(2)}, u32[]{:S(2)}) collective-permute-start(bf16[2048,128]{1,0:T(8,128)(2,1)} %bitcast.11), channel_id=1, source_target_pairs={{0,6},{2,0},{4,2},{6,4},{1,7},{3,1},{5,3},{7,5},{8,14},{10,8},{12,... | collective-permute-start | bytes 1572872 | tf_op jit(solution)/shard_map/ppermute | solution.py:27
  20.4 31.4 %collective-permute-start.4 = (bf16[2048,128]{1,0:T(8,128)(2,1)S(1)}, bf16[2048,128]{1,0:T(8,128)(2,1)S(1)}, u32[]{:S(2)}, u32[]{:S(2)}) collective-permute-start(bf16[2048,128]{1,0:T(8,128)(2,1)S(1)} %bitcast.158), channel_id=1, source_target_pairs={{0,1},{1,0},{2,3},{3,2},{4,5},{5,4},{6,7},{7,6},{8,9},{9,8},{10,11... | collective-permute-start | bytes 1572872 | tf_op jit(solution)/shard_map/ppermute | solution.py:27
  24.8 16.4 %all-to-all-start = ((bf16[32,4,256]{2,1,0:T(4,128)(2,1)}), bf16[32,4,256]{2,1,0:T(4,128)(2,1)S(1)}, u32[]{:S(2)}, u32[]{:S(2)}) async-start(bf16[32,4,256]{2,1,0:T(4,128)(2,1)} %reshape.233), calls=%async_computation | async-start | bytes 131072 | tf_op jit(solution)/shard_map/all_to_all | solution.py:100
  47.0 38.2 %copy-start.12 = (bf16[2048,128]{1,0:T(8,128)(2,1)}, bf16[2048,128]{1,0:T(8,128)(2,1)S(1)}, u32[]{:S(2)}) copy-start(bf16[2048,128]{1,0:T(8,128)(2,1)S(1)} %collective-permute-done.3) | copy-start | bytes 1572868
  53.0 24.3 %collective-permute-start.5 = (bf16[2,2048,128]{2,1,0:T(8,128)(2,1)}, bf16[2,2048,128]{2,1,0:T(8,128)(2,1)}, u32[]{:S(2)}, u32[]{:S(2)}) collective-permute-start(bf16[2,2048,128]{2,1,0:T(8,128)(2,1)} %pad_maximum_fusion.2), channel_id=1, source_target_pairs={{0,1},{1,0},{2,3},{3,2},{4,5},{5,4},{6,7},{7,6},{8,9},{9,8},{10,11... | collective-permute-start | bytes 3145736 | tf_op jit(solution)/shard_map/ppermute | solution.py:27
  54.9 30.0 %all-to-all-start.1 = ((bf16[4,256,256]{1,2,0:T(8,128)(2,1)}), bf16[4,256,256]{1,2,0:T(8,128)(2,1)S(1)}, u32[]{:S(2)}, u32[]{:S(2)}) async-start(bf16[4,256,256]{1,2,0:T(8,128)(2,1)} %bitcast.17), calls=%async_computation.1 | async-start | bytes 1048576 | tf_op jit(solution)/shard_map/all_to_all | solution.py:110
  85.3 23.7 %collective-permute-start.6 = (bf16[2,2048,128]{2,1,0:T(8,128)(2,1)S(1)}, bf16[2,2048,128]{2,1,0:T(8,128)(2,1)S(1)}, u32[]{:S(2)}, u32[]{:S(2)}) collective-permute-start(bf16[2,2048,128]{2,1,0:T(8,128)(2,1)S(1)} %pad_maximum_fusion.5), channel_id=1, source_target_pairs={{0,1},{1,0},{2,3},{3,2},{4,5},{5,4},{6,7},{7,6},{8,9},{9,8},{10,11... | collective-permute-start | bytes 3145736 | tf_op jit(solution)/shard_map/ppermute | solution.py:27
  118.9 28.2 %all-to-all-start.2 = ((bf16[4,64,640]{2,1,0:T(8,128)(2,1)}), bf16[4,64,640]{2,1,0:T(8,128)(2,1)S(1)}, u32[]{:S(2)}, u32[]{:S(2)}) async-start(bf16[4,64,640]{2,1,0:T(8,128)(2,1)} %fusion.40), calls=%async_computation.2 | async-start | bytes 655360 | tf_op jit(solution)/shard_map/all_to_all | solution.py:155
  140.0 47.5 %collective-permute-start.7 = (bf16[4096,256]{1,0:T(8,128)(2,1)}, bf16[4096,256]{1,0:T(8,128)(2,1)}, u32[]{:S(2)}, u32[]{:S(2)}) collective-permute-start(bf16[4096,256]{1,0:T(8,128)(2,1)} %bitcast.154), channel_id=1, source_target_pairs={{0,1},{1,0},{2,3},{3,2},{4,5},{5,4},{6,7},{7,6},{8,9},{9,8},{10,11... | collective-permute-start | bytes 6291464 | tf_op jit(solution)/shard_map/ppermute | solution.py:27
  147.1 40.3 %copy-start.11 = (bf16[1,4096,256]{2,1,0:T(8,128)(2,1)S(1)}, bf16[1,4096,256]{2,1,0:T(8,128)(2,1)}, u32[]{:S(2)}) copy-start(bf16[1,4096,256]{2,1,0:T(8,128)(2,1)} %param.17) | copy-start | bytes 6291460
  191.4 8.9 %collective-permute-start.8 = (bf16[64,512]{1,0:T(8,128)(2,1)S(1)}, bf16[64,512]{1,0:T(8,128)(2,1)S(1)}, u32[]{:S(2)}, u32[]{:S(2)}) collective-permute-start(bf16[64,512]{1,0:T(8,128)(2,1)S(1)} %fusion.44), channel_id=1, source_target_pairs={{0,32},{32,64},{64,96},{96,128},{128,160},{160,192},{192,224},{224... | collective-permute-start | bytes 196616 | tf_op jit(solution)/shard_map/ppermute | solution.py:27
  219.6 12.4 %all-to-all-start.3 = ((bf16[4,64,640]{2,1,0:T(8,128)(2,1)}), bf16[4,64,640]{2,1,0:T(8,128)(2,1)S(1)}, u32[]{:S(2)}, u32[]{:S(2)}) async-start(bf16[4,64,640]{2,1,0:T(8,128)(2,1)} %fusion.33), calls=%async_computation.3 | async-start | bytes 655360 | tf_op jit(solution)/shard_map/all_to_all | solution.py:155
  259.2 32.4 %copy-start.6 = (bf16[2048,256]{1,0:T(8,128)(2,1)S(1)}, bf16[2048,256]{1,0:T(8,128)(2,1)}, u32[]{:S(2)}) copy-start(bf16[2048,256]{1,0:T(8,128)(2,1)} %get-tuple-element.33) | copy-start | bytes 3145732
  259.3 14.6 %collective-permute-start.9 = (bf16[64,512]{1,0:T(8,128)(2,1)S(1)}, bf16[64,512]{1,0:T(8,128)(2,1)S(1)}, u32[]{:S(2)}, u32[]{:S(2)}) collective-permute-start(bf16[64,512]{1,0:T(8,128)(2,1)S(1)} %fusion.45), channel_id=1, source_target_pairs={{0,32},{32,64},{64,96},{96,128},{128,160},{160,192},{192,224},{224... | collective-permute-start | bytes 196616 | tf_op jit(solution)/shard_map/ppermute | solution.py:27
  293.8 10.2 %all-to-all-start.5 = ((bf16[4,64,640]{2,1,0:T(8,128)(2,1)}), bf16[4,64,640]{2,1,0:T(8,128)(2,1)S(1)}, u32[]{:S(2)}, u32[]{:S(2)}) async-start(bf16[4,64,640]{2,1,0:T(8,128)(2,1)} %fusion.26), calls=%async_computation.5 | async-start | bytes 655360 | tf_op jit(solution)/shard_map/all_to_all | solution.py:155
  331.9 41.8 %copy-start.10 = (bf16[2048,256]{1,0:T(8,128)(2,1)S(1)}, bf16[2048,256]{1,0:T(8,128)(2,1)}, u32[]{:S(2)}) copy-start(bf16[2048,256]{1,0:T(8,128)(2,1)} %get-tuple-element.32) | copy-start | bytes 3145732
  331.9 42.1 %copy-start.7 = (bf16[2048,256]{1,0:T(8,128)(2,1)S(1)}, bf16[2048,256]{1,0:T(8,128)(2,1)}, u32[]{:S(2)}) copy-start(bf16[2048,256]{1,0:T(8,128)(2,1)} %get-tuple-element.33) | copy-start | bytes 3145732
  332.0 25.0 %collective-permute-start.10 = (bf16[64,512]{1,0:T(8,128)(2,1)S(1)}, bf16[64,512]{1,0:T(8,128)(2,1)S(1)}, u32[]{:S(2)}, u32[]{:S(2)}) collective-permute-start(bf16[64,512]{1,0:T(8,128)(2,1)S(1)} %fusion.46), channel_id=1, source_target_pairs={{0,32},{32,64},{64,96},{96,128},{128,160},{160,192},{192,224},{224... | collective-permute-start | bytes 196616 | tf_op jit(solution)/shard_map/ppermute | solution.py:27
  376.3 15.6 %all-to-all-start.7 = ((bf16[4,64,640]{2,1,0:T(8,128)(2,1)}), bf16[4,64,640]{2,1,0:T(8,128)(2,1)S(1)}, u32[]{:S(2)}, u32[]{:S(2)}) async-start(bf16[4,64,640]{2,1,0:T(8,128)(2,1)} %fusion.19), calls=%async_computation.7 | async-start | bytes 655360 | tf_op jit(solution)/shard_map/all_to_all | solution.py:155
  419.2 15.5 %collective-permute-start.11 = (bf16[64,256]{1,0:T(8,128)(2,1)S(1)}, bf16[64,256]{1,0:T(8,128)(2,1)S(1)}, u32[]{:S(2)}, u32[]{:S(2)}) collective-permute-start(bf16[64,256]{1,0:T(8,128)(2,1)S(1)} %get-tuple-element.56), channel_id=1, source_target_pairs={{0,32},{32,64},{64,96},{96,128},{128,160},{160,192},{192,224},{224... | collective-permute-start | bytes 98312 | tf_op jit(solution)/shard_map/ppermute | solution.py:27
  432.8 5.2 %collective-permute-start.12 = (bf16[64,256]{1,0:T(8,128)(2,1)S(1)}, bf16[64,256]{1,0:T(8,128)(2,1)S(1)}, u32[]{:S(2)}, u32[]{:S(2)}) collective-permute-start(bf16[64,256]{1,0:T(8,128)(2,1)S(1)} %get-tuple-element.57), channel_id=1, source_target_pairs={{0,33},{1,32},{32,65},{33,64},{64,97},{65,96},{96,129},{97,128},{1... | collective-permute-start | bytes 98312 | tf_op jit(solution)/shard_map/ppermute | solution.py:185
  (22 other events, 260.5 us)

commit v5 on v4

--- a/solution.py
+++ b/solution.py
@@ -140,7 +140,8 @@
         if lap_step == 0:
             wide = lax.all_gather(both, "za", axis=1, tiled=True)
             wide, w_o = lax.optimization_barrier((wide, w_out[0]))
-            w_o_pair = lax.optimization_barrier(jnp.concatenate([w_out[0], shift(w_o, "y", 1)], 1))
+            middle = w_o.shape[0] // 2
+            w_o_upper = shift(w_o[:middle], "y", 1)
             gain_wide = wide[MB_ROWS : MB_ROWS + 1].astype(F32)
             wide = wide[:MB_ROWS].astype(F32)
         else:
@@ -153,6 +154,10 @@
         message = jnp.stack([jnp.concatenate([part, shared], 1) for part in queries])
         message = jnp.roll(message, b, axis=0)
         arrived = lax.all_to_all(message, "zb", 0, 0, tiled=True)
+        if lap_step == 0:
+            arrived, w_o_upper = lax.optimization_barrier((arrived, w_o_upper))
+            w_o_other = jnp.concatenate([w_o_upper, shift(w_o[middle:], "y", 1)], 0)
+            w_o_pair = lax.optimization_barrier(jnp.concatenate([w_out[0], w_o_other], 1))
         total = jnp.sum(arrived.astype(F32), axis=0)
         inverse = lax.rsqrt(jnp.sum(total[:, 4 * HD :], axis=1, keepdims=True) / D + 1e-05)
         total = total[:, : 4 * HD] * inverse

time: 440 us -> 447 us (1.016)
  blocking collectives: 166 us -> 184 us
  starting transfers between devices: 144 us -> 137 us
    all_gather x2, blocking collectives: 46.7 us -> 64.9 us  [local(): attended = lax.all_gather(attended, ('za', 'zb'), axis=1, tiled=True)]
    all_to_all x4, starting transfers between devices: 35.4 us -> 25.8 us  [local(): arrived = lax.all_to_all(message, 'zb', 0, 0, tiled=True)]
    ppermute x12 -> x13, starting transfers between devices: 84.6 us -> 86.6 us  [shift(): lax.ppermute(block, axis, [(i, (i + distance) % count) for i in range(cou...]
    ppermute x12 -> x13, waiting for transfers between devices: 36.2 us -> 35 us  [shift(): lax.ppermute(block, axis, [(i, (i + distance) % count) for i in range(cou...]
  transfers between devices with their start and end apart: 19 -> 20, of which waited for: 14 -> 13; matrix products, arithmetic and copies ran while one was open for 3% -> 5% of each run, Pallas kernels for 0% -> 0%
where the time goes in v5:
time: 447 us; the launch traced here: 446 us
  blocking collectives  184 us (41%)
  starting transfers between devices  137 us (31%)
  waiting for transfers between devices  74.6 us (17%)
  other arithmetic  20 us (4%)
  matrix products  16.6 us (4%)
  local copies, waits for them, and re-layouts  12.4 us (3%)
    ppermute x13, starting transfers between devices, shift(): lax.ppermute(block, axis, [(i, (i + distance) % count) for i in range(cou...  86.6 us
    all_gather x2, blocking collectives, local(): attended = lax.all_gather(attended, ('za', 'zb'), axis=1, tiled=True)  64.9 us
    all_gather x3, blocking collectives, local(): wide = lax.all_gather(state, 'za', axis=1, tiled=True).astype(F32)  50 us
    all_to_all x2, blocking collectives, local(): lax.all_to_all(to_all(attended, GROUP * GROUP), ('za', 'zb'), 0, 0, tiled...  49.7 us
    ppermute x13, waiting for transfers between devices, shift(): lax.ppermute(block, axis, [(i, (i + distance) % count) for i in range(cou...  35 us
    all_to_all x4, starting transfers between devices, local(): arrived = lax.all_to_all(message, 'zb', 0, 0, tiled=True)  25.8 us
    all_to_all x4, waiting for transfers between devices, local(): arrived = lax.all_to_all(message, 'zb', 0, 0, tiled=True)  23.4 us
    all_gather x1, blocking collectives, local(): wide = lax.all_gather(both, 'za', axis=1, tiled=True)  19.4 us
  transfers between devices with their start and end apart: 20, of which 13 were waited for; matrix products, arithmetic and copies ran while one was open for 5% of the time, Pallas kernels for 0%

profile of v5, /device:TPU:1, one launch (start us, length us, event | category | flops | bytes accessed | tf_op | source)
XLA Modules:
  0.0 445.8 jit_solution(6239193687346423029)
XLA Ops:
  2.9 7.1 %collective-permute-start.1 = (bf16[2048,128]{1,0:T(8,128)(2,1)}, bf16[2048,128]{1,0:T(8,128)(2,1)S(1)}, u32[]{:S(2)}, u32[]{:S(2)}) collective-permute-start(bf16[2048,128]{1,0:T(8,128)(2,1)} %bitcast.11), channel_id=1, source_target_pairs={{0,6},{2,0},{4,2},{6,4},{1,7},{3,1},{5,3},{7,5},{8,14},{10,8},{12,... | collective-permute-start | bytes 1572872 | tf_op jit(solution)/shard_map/ppermute | solution.py:27
  21.8 9.0 %all-to-all-start = ((bf16[32,4,256]{2,1,0:T(4,128)(2,1)}), bf16[32,4,256]{2,1,0:T(4,128)(2,1)S(1)}, u32[]{:S(2)}, u32[]{:S(2)}) async-start(bf16[32,4,256]{2,1,0:T(4,128)(2,1)} %reshape.233), calls=%async_computation | async-start | bytes 131072 | tf_op jit(solution)/shard_map/all_to_all | solution.py:100
  31.8 6.1 %all-to-all-done = bf16[32,4,256]{2,1,0:T(4,128)(2,1)S(1)} async-done(((bf16[32,4,256]{2,1,0:T(4,128)(2,1)}), bf16[32,4,256]{2,1,0:T(4,128)(2,1)S(1)}, u32[]{:S(2)}, u32[]{:S(2)}) %all-to-all-start) | async-done | bytes 65568 | tf_op jit(solution)/shard_map/all_to_all | solution.py:100
  38.7 15.4 %collective-permute-done.2 = bf16[2048,128]{1,0:T(8,128)(2,1)S(1)} collective-permute-done((bf16[2048,128]{1,0:T(8,128)(2,1)}, bf16[2048,128]{1,0:T(8,128)(2,1)S(1)}, u32[]{:S(2)}, u32[]{:S(2)}) %collective-permute-start.2) | collective-permute-done | bytes 524320 | tf_op jit(solution)/shard_map/ppermute | solution.py:27
  58.4 13.5 %all-to-all-start.1 = ((bf16[4,256,256]{1,2,0:T(8,128)(2,1)}), bf16[4,256,256]{1,2,0:T(8,128)(2,1)S(1)}, u32[]{:S(2)}, u32[]{:S(2)}) async-start(bf16[4,256,256]{1,2,0:T(8,128)(2,1)} %bitcast.17), calls=%async_computation.1 | async-start | bytes 1048576 | tf_op jit(solution)/shard_map/all_to_all | solution.py:110
  72.2 8.6 %collective-permute-done.5 = bf16[2,2048,128]{2,1,0:T(8,128)(2,1)} collective-permute-done((bf16[2,2048,128]{2,1,0:T(8,128)(2,1)}, bf16[2,2048,128]{2,1,0:T(8,128)(2,1)}, u32[]{:S(2)}, u32[]{:S(2)}) %collective-permute-start.5) | collective-permute-done | bytes 1048608 | tf_op jit(solution)/shard_map/ppermute | solution.py:27
  83.2 6.4 %all-to-all-done.1 = bf16[4,256,256]{1,2,0:T(8,128)(2,1)S(1)} async-done(((bf16[4,256,256]{1,2,0:T(8,128)(2,1)}), bf16[4,256,256]{1,2,0:T(8,128)(2,1)S(1)}, u32[]{:S(2)}, u32[]{:S(2)}) %all-to-all-start.1) | async-done | bytes 524320 | tf_op jit(solution)/shard_map/all_to_all | solution.py:110
  93.4 19.4 %all_gather.18 = bf16[80,2048]{1,0:T(8,128)(2,1)S(1)} all-gather(bf16[80,512]{1,0:T(8,128)(2,1)} %maximum_maximum_fusion.1), channel_id=1, replica_groups=mesh['section'=16,'za'=4,'zb'=4,'y'=2] {'za'}, dimensions={1}, use_global_device_ids=true | all-gather | bytes 409600 | tf_op jit(solution)/shard_map/all_gather | solution.py:141
  131.0 11.8 %all-to-all-start.2 = ((bf16[4,64,640]{2,1,0:T(8,128)(2,1)}), bf16[4,64,640]{2,1,0:T(8,128)(2,1)S(1)}, u32[]{:S(2)}, u32[]{:S(2)}) async-start(bf16[4,64,640]{2,1,0:T(8,128)(2,1)} %fusion.40), calls=%async_computation.2 | async-start | bytes 655360 | tf_op jit(solution)/shard_map/all_to_all | solution.py:156
  149.0 7.1 %collective-permute-done.8 = bf16[2048,256]{1,0:T(8,128)(2,1)} collective-permute-done((bf16[2048,256]{1,0:T(8,128)(2,1)}, bf16[2048,256]{1,0:T(8,128)(2,1)}, u32[]{:S(2)}, u32[]{:S(2)}) %collective-permute-start.8) | collective-permute-done | bytes 1048608 | tf_op jit(solution)/shard_map/ppermute | solution.py:27
  160.0 40.7 %all_gather.19 = bf16[64,4096]{1,0:T(8,128)(2,1)S(1)} all-gather(bf16[64,256]{1,0:T(8,128)(2,1)S(1)} %pad_maximum_fusion.43), channel_id=1, replica_groups=mesh['section'=16,'za'=4,'zb'=4,'y'=2] {'za','zb'}, dimensions={1}, use_global_device_ids=true | all-gather | bytes 557056 | tf_op jit(solution)/shard_map/all_gather | solution.py:179
  201.6 12.6 %collective-permute-start.9 = (bf16[64,512]{1,0:T(8,128)(2,1)S(1)}, bf16[64,512]{1,0:T(8,128)(2,1)S(1)}, u32[]{:S(2)}, u32[]{:S(2)}) collective-permute-start(bf16[64,512]{1,0:T(8,128)(2,1)S(1)} %fusion.44), channel_id=1, source_target_pairs={{0,32},{32,64},{64,96},{96,128},{128,160},{160,192},{192,224},{224... | collective-permute-start | bytes 196616 | tf_op jit(solution)/shard_map/ppermute | solution.py:27
  215.6 18.1 %all_gather.20 = bf16[64,2048]{1,0:T(8,128)(2,1)S(1)} all-gather(bf16[64,512]{1,0:T(8,128)(2,1)S(1)} %collective-permute-done.9), channel_id=1, replica_groups=mesh['section'=16,'za'=4,'zb'=4,'y'=2] {'za'}, dimensions={1}, use_global_device_ids=true | all-gather | bytes 327680 | tf_op jit(solution)/shard_map/all_gather | solution.py:148
  247.7 24.9 %all_to_all.40 = bf16[16,64,256]{2,1,0:T(8,128)(2,1)S(1)} all-to-all(bf16[16,64,256]{2,1,0:T(8,128)(2,1)S(1)} %broadcast_in_dim.279), channel_id=1, replica_groups=mesh['section'=16,'za'=4,'zb'=4,'y'=2] {'za','zb'}, dimensions={0} | all-to-all | bytes 1048576 | tf_op jit(solution)/shard_map/all_to_all | solution.py:176
  273.6 12.8 %collective-permute-start.10 = (bf16[64,512]{1,0:T(8,128)(2,1)S(1)}, bf16[64,512]{1,0:T(8,128)(2,1)S(1)}, u32[]{:S(2)}, u32[]{:S(2)}) collective-permute-start(bf16[64,512]{1,0:T(8,128)(2,1)S(1)} %fusion.45), channel_id=1, source_target_pairs={{0,32},{32,64},{64,96},{96,128},{128,160},{160,192},{192,224},{224... | collective-permute-start | bytes 196616 | tf_op jit(solution)/shard_map/ppermute | solution.py:27
  287.7 16.2 %all_gather.21 = bf16[64,2048]{1,0:T(8,128)(2,1)S(1)} all-gather(bf16[64,512]{1,0:T(8,128)(2,1)S(1)} %collective-permute-done.10), channel_id=1, replica_groups=mesh['section'=16,'za'=4,'zb'=4,'y'=2] {'za'}, dimensions={1}, use_global_device_ids=true | all-gather | bytes 327680 | tf_op jit(solution)/shard_map/all_gather | solution.py:148
  311.2 6.1 %all-to-all-done.5 = bf16[4,64,640]{2,1,0:T(8,128)(2,1)S(1)} async-done(((bf16[4,64,640]{2,1,0:T(8,128)(2,1)}), bf16[4,64,640]{2,1,0:T(8,128)(2,1)S(1)}, u32[]{:S(2)}, u32[]{:S(2)}) %all-to-all-start.5) | async-done | bytes 327712 | tf_op jit(solution)/shard_map/all_to_all | solution.py:156
  318.8 24.7 %all_to_all.41 = bf16[16,64,256]{2,1,0:T(8,128)(2,1)S(1)} all-to-all(bf16[16,64,256]{2,1,0:T(8,128)(2,1)S(1)} %broadcast_in_dim.284), channel_id=1, replica_groups=mesh['section'=16,'za'=4,'zb'=4,'y'=2] {'za','zb'}, dimensions={0} | all-to-all | bytes 1048576 | tf_op jit(solution)/shard_map/all_to_all | solution.py:176
  344.4 16.2 %collective-permute-start.11 = (bf16[64,512]{1,0:T(8,128)(2,1)S(1)}, bf16[64,512]{1,0:T(8,128)(2,1)S(1)}, u32[]{:S(2)}, u32[]{:S(2)}) collective-permute-start(bf16[64,512]{1,0:T(8,128)(2,1)S(1)} %fusion.46), channel_id=1, source_target_pairs={{0,32},{32,64},{64,96},{96,128},{128,160},{160,192},{192,224},{224... | collective-permute-start | bytes 196616 | tf_op jit(solution)/shard_map/ppermute | solution.py:27
  362.0 15.7 %all_gather.22 = bf16[64,2048]{1,0:T(8,128)(2,1)S(1)} all-gather(bf16[64,512]{1,0:T(8,128)(2,1)S(1)} %collective-permute-done.11), channel_id=1, replica_groups=mesh['section'=16,'za'=4,'zb'=4,'y'=2] {'za'}, dimensions={1}, use_global_device_ids=true | all-gather | bytes 327680 | tf_op jit(solution)/shard_map/all_gather | solution.py:148
  380.7 6.2 %all-to-all-start.7 = ((bf16[4,64,640]{2,1,0:T(8,128)(2,1)}), bf16[4,64,640]{2,1,0:T(8,128)(2,1)S(1)}, u32[]{:S(2)}, u32[]{:S(2)}) async-start(bf16[4,64,640]{2,1,0:T(8,128)(2,1)} %fusion.19), calls=%async_computation.7 | async-start | bytes 655360 | tf_op jit(solution)/shard_map/all_to_all | solution.py:156
  386.9 6.1 %all-to-all-done.7 = bf16[4,64,640]{2,1,0:T(8,128)(2,1)S(1)} async-done(((bf16[4,64,640]{2,1,0:T(8,128)(2,1)}), bf16[4,64,640]{2,1,0:T(8,128)(2,1)S(1)}, u32[]{:S(2)}, u32[]{:S(2)}) %all-to-all-start.7) | async-done | bytes 327712 | tf_op jit(solution)/shard_map/all_to_all | solution.py:156
  394.4 24.2 %all_gather.23 = bf16[64,4096]{1,0:T(8,128)(2,1)S(1)} all-gather(bf16[64,256]{1,0:T(8,128)(2,1)S(1)} %pad_maximum_fusion.46), channel_id=1, replica_groups=mesh['section'=16,'za'=4,'zb'=4,'y'=2] {'za','zb'}, dimensions={1}, use_global_device_ids=true | all-gather | bytes 557056 | tf_op jit(solution)/shard_map/all_gather | solution.py:179
  421.7 17.9 %collective-permute-start.12 = (bf16[64,256]{1,0:T(8,128)(2,1)S(1)}, bf16[64,256]{1,0:T(8,128)(2,1)S(1)}, u32[]{:S(2)}, u32[]{:S(2)}) collective-permute-start(bf16[64,256]{1,0:T(8,128)(2,1)S(1)} %get-tuple-element.62), channel_id=1, source_target_pairs={{0,32},{32,64},{64,96},{96,128},{128,160},{160,192},{192,224},{224... | collective-permute-start | bytes 98312 | tf_op jit(solution)/shard_map/ppermute | solution.py:27
  (247 shorter events, 97.4 us)
Async XLA Ops:
  2.9 35.8 %collective-permute-start.1 = (bf16[2048,128]{1,0:T(8,128)(2,1)}, bf16[2048,128]{1,0:T(8,128)(2,1)S(1)}, u32[]{:S(2)}, u32[]{:S(2)}) collective-permute-start(bf16[2048,128]{1,0:T(8,128)(2,1)} %bitcast.11), channel_id=1, source_target_pairs={{0,6},{2,0},{4,2},{6,4},{1,7},{3,1},{5,3},{7,5},{8,14},{10,8},{12,... | collective-permute-start | bytes 1572872 | tf_op jit(solution)/shard_map/ppermute | solution.py:27
  10.0 44.1 %collective-permute-start.2 = (bf16[2048,128]{1,0:T(8,128)(2,1)}, bf16[2048,128]{1,0:T(8,128)(2,1)S(1)}, u32[]{:S(2)}, u32[]{:S(2)}) collective-permute-start(bf16[2048,128]{1,0:T(8,128)(2,1)} %bitcast.12), channel_id=1, source_target_pairs={{0,4},{2,6},{4,0},{6,2},{1,5},{3,7},{5,1},{7,3},{8,12},{10,14},{12... | collective-permute-start | bytes 1572872 | tf_op jit(solution)/shard_map/ppermute | solution.py:27
  11.9 42.2 %collective-permute-start.3 = (bf16[2048,128]{1,0:T(8,128)(2,1)}, bf16[2048,128]{1,0:T(8,128)(2,1)S(1)}, u32[]{:S(2)}, u32[]{:S(2)}) collective-permute-start(bf16[2048,128]{1,0:T(8,128)(2,1)} %bitcast.13), channel_id=1, source_target_pairs={{0,2},{2,4},{4,6},{6,0},{1,3},{3,5},{5,7},{7,1},{8,10},{10,12},{12... | collective-permute-start | bytes 1572872 | tf_op jit(solution)/shard_map/ppermute | solution.py:27
  14.1 40.0 %collective-permute-start.4 = (bf16[2048,128]{1,0:T(8,128)(2,1)S(1)}, bf16[2048,128]{1,0:T(8,128)(2,1)S(1)}, u32[]{:S(2)}, u32[]{:S(2)}) collective-permute-start(bf16[2048,128]{1,0:T(8,128)(2,1)S(1)} %bitcast.159), channel_id=1, source_target_pairs={{0,1},{1,0},{2,3},{3,2},{4,5},{5,4},{6,7},{7,6},{8,9},{9,8},{10,11... | collective-permute-start | bytes 1572872 | tf_op jit(solution)/shard_map/ppermute | solution.py:27
  17.4 14.4 %collective-permute-start = (bf16[48,256]{1,0:T(8,128)(2,1)S(1)}, bf16[48,256]{1,0:T(8,128)(2,1)S(1)}, u32[]{:S(2)}, u32[]{:S(2)}) collective-permute-start(bf16[48,256]{1,0:T(8,128)(2,1)S(1)} %pad_maximum_fusion.41), channel_id=1, source_target_pairs={{0,1},{1,0},{2,3},{3,2},{4,5},{5,4},{6,7},{7,6},{8,9},{9,8},{10,11... | collective-permute-start | bytes 73736 | tf_op jit(solution)/shard_map/ppermute | solution.py:27
  21.8 16.2 %all-to-all-start = ((bf16[32,4,256]{2,1,0:T(4,128)(2,1)}), bf16[32,4,256]{2,1,0:T(4,128)(2,1)S(1)}, u32[]{:S(2)}, u32[]{:S(2)}) async-start(bf16[32,4,256]{2,1,0:T(4,128)(2,1)} %reshape.233), calls=%async_computation | async-start | bytes 131072 | tf_op jit(solution)/shard_map/all_to_all | solution.py:100
  55.2 25.5 %collective-permute-start.5 = (bf16[2,2048,128]{2,1,0:T(8,128)(2,1)}, bf16[2,2048,128]{2,1,0:T(8,128)(2,1)}, u32[]{:S(2)}, u32[]{:S(2)}) collective-permute-start(bf16[2,2048,128]{2,1,0:T(8,128)(2,1)} %pad_maximum_fusion.1), channel_id=1, source_target_pairs={{0,1},{1,0},{2,3},{3,2},{4,5},{5,4},{6,7},{7,6},{8,9},{9,8},{10,11... | collective-permute-start | bytes 3145736 | tf_op jit(solution)/shard_map/ppermute | solution.py:27
  58.4 31.2 %all-to-all-start.1 = ((bf16[4,256,256]{1,2,0:T(8,128)(2,1)}), bf16[4,256,256]{1,2,0:T(8,128)(2,1)S(1)}, u32[]{:S(2)}, u32[]{:S(2)}) async-start(bf16[4,256,256]{1,2,0:T(8,128)(2,1)} %bitcast.17), calls=%async_computation.1 | async-start | bytes 1048576 | tf_op jit(solution)/shard_map/all_to_all | solution.py:110
  72.0 47.7 %copy-start.25 = (pred[128]{0:T(512)(128)(4,1)}, pred[128]{0:T(512)(128)(4,1)S(1)}, u32[]{:S(2)}) copy-start(pred[128]{0:T(512)(128)(4,1)S(1)} %iota_compare_fusion.8) | copy-start | bytes 388
  72.0 47.7 %copy-start.27 = (pred[128]{0:T(512)(128)(4,1)}, pred[128]{0:T(512)(128)(4,1)S(1)}, u32[]{:S(2)}) copy-start(pred[128]{0:T(512)(128)(4,1)S(1)} %get-tuple-element.162) | copy-start | bytes 388
  91.3 28.5 %collective-permute-start.6 = (bf16[2,2048,128]{2,1,0:T(8,128)(2,1)S(1)}, bf16[2,2048,128]{2,1,0:T(8,128)(2,1)S(1)}, u32[]{:S(2)}, u32[]{:S(2)}) collective-permute-start(bf16[2,2048,128]{2,1,0:T(8,128)(2,1)S(1)} %pad_maximum_fusion.4), channel_id=1, source_target_pairs={{0,1},{1,0},{2,3},{3,2},{4,5},{5,4},{6,7},{7,6},{8,9},{9,8},{10,11... | collective-permute-start | bytes 3145736 | tf_op jit(solution)/shard_map/ppermute | solution.py:27
  114.2 29.7 %collective-permute-start.7 = (bf16[2048,256]{1,0:T(8,128)(2,1)}, bf16[2048,256]{1,0:T(8,128)(2,1)}, u32[]{:S(2)}, u32[]{:S(2)}) collective-permute-start(bf16[2048,256]{1,0:T(8,128)(2,1)} %get-tuple-element.49), channel_id=1, source_target_pairs={{0,1},{1,0},{2,3},{3,2},{4,5},{5,4},{6,7},{7,6},{8,9},{9,8},{10,11... | collective-permute-start | bytes 3145736 | tf_op jit(solution)/shard_map/ppermute | solution.py:27
  117.1 39.0 %collective-permute-start.8 = (bf16[2048,256]{1,0:T(8,128)(2,1)}, bf16[2048,256]{1,0:T(8,128)(2,1)}, u32[]{:S(2)}, u32[]{:S(2)}) collective-permute-start(bf16[2048,256]{1,0:T(8,128)(2,1)} %get-tuple-element.48), channel_id=1, source_target_pairs={{0,1},{1,0},{2,3},{3,2},{4,5},{5,4},{6,7},{7,6},{8,9},{9,8},{10,11... | collective-permute-start | bytes 3145736 | tf_op jit(solution)/shard_map/ppermute | solution.py:27
  131.0 18.0 %all-to-all-start.2 = ((bf16[4,64,640]{2,1,0:T(8,128)(2,1)}), bf16[4,64,640]{2,1,0:T(8,128)(2,1)S(1)}, u32[]{:S(2)}, u32[]{:S(2)}) async-start(bf16[4,64,640]{2,1,0:T(8,128)(2,1)} %fusion.40), calls=%async_computation.2 | async-start | bytes 655360 | tf_op jit(solution)/shard_map/all_to_all | solution.py:156
  158.6 75.3 %copy-start.1 = (bf16[4096,512]{1,0:T(8,128)(2,1)}, bf16[4096,512]{1,0:T(8,128)(2,1)S(1)}, u32[]{:S(2)}) copy-start(bf16[4096,512]{1,0:T(8,128)(2,1)S(1)} %maximum_maximum_fusion) | copy-start | bytes 12582916
  159.1 74.9 %copy-start.9 = (bf16[2048,256]{1,0:T(8,128)(2,1)S(1)}, bf16[2048,256]{1,0:T(8,128)(2,1)}, u32[]{:S(2)}) copy-start(bf16[2048,256]{1,0:T(8,128)(2,1)} %get-tuple-element.35) | copy-start | bytes 3145732
  201.6 14.0 %collective-permute-start.9 = (bf16[64,512]{1,0:T(8,128)(2,1)S(1)}, bf16[64,512]{1,0:T(8,128)(2,1)S(1)}, u32[]{:S(2)}, u32[]{:S(2)}) collective-permute-start(bf16[64,512]{1,0:T(8,128)(2,1)S(1)} %fusion.44), channel_id=1, source_target_pairs={{0,32},{32,64},{64,96},{96,128},{128,160},{160,192},{192,224},{224... | collective-permute-start | bytes 196616 | tf_op jit(solution)/shard_map/ppermute | solution.py:27
  236.6 9.6 %all-to-all-start.3 = ((bf16[4,64,640]{2,1,0:T(8,128)(2,1)}), bf16[4,64,640]{2,1,0:T(8,128)(2,1)S(1)}, u32[]{:S(2)}, u32[]{:S(2)}) async-start(bf16[4,64,640]{2,1,0:T(8,128)(2,1)} %fusion.33), calls=%async_computation.3 | async-start | bytes 655360 | tf_op jit(solution)/shard_map/all_to_all | solution.py:156
  273.6 14.1 %collective-permute-start.10 = (bf16[64,512]{1,0:T(8,128)(2,1)S(1)}, bf16[64,512]{1,0:T(8,128)(2,1)S(1)}, u32[]{:S(2)}, u32[]{:S(2)}) collective-permute-start(bf16[64,512]{1,0:T(8,128)(2,1)S(1)} %fusion.45), channel_id=1, source_target_pairs={{0,32},{32,64},{64,96},{96,128},{128,160},{160,192},{192,224},{224... | collective-permute-start | bytes 196616 | tf_op jit(solution)/shard_map/ppermute | solution.py:27
  306.8 10.5 %all-to-all-start.5 = ((bf16[4,64,640]{2,1,0:T(8,128)(2,1)}), bf16[4,64,640]{2,1,0:T(8,128)(2,1)S(1)}, u32[]{:S(2)}, u32[]{:S(2)}) async-start(bf16[4,64,640]{2,1,0:T(8,128)(2,1)} %fusion.26), calls=%async_computation.5 | async-start | bytes 655360 | tf_op jit(solution)/shard_map/all_to_all | solution.py:156
  344.4 17.6 %collective-permute-start.11 = (bf16[64,512]{1,0:T(8,128)(2,1)S(1)}, bf16[64,512]{1,0:T(8,128)(2,1)S(1)}, u32[]{:S(2)}, u32[]{:S(2)}) collective-permute-start(bf16[64,512]{1,0:T(8,128)(2,1)S(1)} %fusion.46), channel_id=1, source_target_pairs={{0,32},{32,64},{64,96},{96,128},{128,160},{160,192},{192,224},{224... | collective-permute-start | bytes 196616 | tf_op jit(solution)/shard_map/ppermute | solution.py:27
  380.7 12.3 %all-to-all-start.7 = ((bf16[4,64,640]{2,1,0:T(8,128)(2,1)}), bf16[4,64,640]{2,1,0:T(8,128)(2,1)S(1)}, u32[]{:S(2)}, u32[]{:S(2)}) async-start(bf16[4,64,640]{2,1,0:T(8,128)(2,1)} %fusion.19), calls=%async_computation.7 | async-start | bytes 655360 | tf_op jit(solution)/shard_map/all_to_all | solution.py:156
  421.7 19.8 %collective-permute-start.12 = (bf16[64,256]{1,0:T(8,128)(2,1)S(1)}, bf16[64,256]{1,0:T(8,128)(2,1)S(1)}, u32[]{:S(2)}, u32[]{:S(2)}) collective-permute-start(bf16[64,256]{1,0:T(8,128)(2,1)S(1)} %get-tuple-element.62), channel_id=1, source_target_pairs={{0,32},{32,64},{64,96},{96,128},{128,160},{160,192},{192,224},{224... | collective-permute-start | bytes 98312 | tf_op jit(solution)/shard_map/ppermute | solution.py:27
  439.6 5.5 %collective-permute-start.13 = (bf16[64,256]{1,0:T(8,128)(2,1)S(1)}, bf16[64,256]{1,0:T(8,128)(2,1)S(1)}, u32[]{:S(2)}, u32[]{:S(2)}) collective-permute-start(bf16[64,256]{1,0:T(8,128)(2,1)S(1)} %get-tuple-element.63), channel_id=1, source_target_pairs={{0,33},{1,32},{32,65},{33,64},{64,97},{65,96},{96,129},{97,128},{1... | collective-permute-start | bytes 98312 | tf_op jit(solution)/shard_map/ppermute | solution.py:190
  (29 other events, 776.6 us)
